TPU v7x, 32 devices: a whole 2x2x4 slice. The times are simulated.
32 devices in a mesh: pipe: 2 (over core), fsdp: 4 (over z), tensor: 4 (over y, x).
Axes of the slice: x: 2, y: 2, z: 4, core: 2. Of those that a mesh axis runs over, the one named last changes fastest.
Arguments:
- tokens: bfloat16 [2, 4096, 1536], P(None, ('fsdp', 'tensor')), may hold values from -6 to 6
- out_grad: bfloat16 [2, 4096, 1536], P(None, ('fsdp', 'tensor')), may hold values from -6 to 6
- seq_lengths: int32 [2, 4, 3], P(None, 'fsdp'), may hold values from 1 to 1022, as said below
- norm_gain: bfloat16 [2, 1536], P('pipe', 'fsdp'), may hold values from 0.5 to 1.5
- w_zx: bfloat16 [2, 1536, 2, 3072], P('pipe', 'fsdp', None, 'tensor'), may hold values from -0.15625 to 0.15625
- w_bc: bfloat16 [2, 1536, 256], P('pipe', 'fsdp'), may hold values from -0.15625 to 0.15625
- w_dt: bfloat16 [2, 1536, 48], P('pipe', 'fsdp', 'tensor'), may hold values from -0.15625 to 0.15625
- conv_x: bfloat16 [2, 5, 48, 64], P('pipe', None, 'tensor', 'fsdp'), may hold values from -0.5 to 0.5
- conv_bc: bfloat16 [2, 5, 256], P('pipe', None, 'fsdp'), may hold values from -0.5 to 0.5
- out_gain: bfloat16 [2, 48, 64], P('pipe', 'tensor', 'fsdp'), may hold values from 0.5 to 1.5
- head_params: float32 [2, 3, 48], P('pipe', None, 'tensor'), may hold values from -4 to 1.5, as said below
- out_weight: bfloat16 [2, 3072, 1536], P('pipe', 'tensor', 'fsdp'), may hold values from -0.109375 to 0.109375
Outputs:
- section_outputs: bfloat16 [2, 2, 4096, 1536], P('pipe', None, ('fsdp', 'tensor'))
- input_grads: bfloat16 [2, 2, 4096, 1536], P('pipe', None, ('fsdp', 'tensor'))
- grad_norm_gain: float32 [2, 1536], P('pipe', ('fsdp', 'tensor'))
- grad_w_zx: float32 [2, 1536, 2, 3072], P('pipe', 'fsdp', None, 'tensor')
- grad_w_bc: float32 [2, 1536, 256], P('pipe', ('fsdp', 'tensor'))
- grad_w_dt: float32 [2, 1536, 48], P('pipe', 'fsdp', 'tensor')
- grad_conv_x: float32 [2, 5, 48, 64], P('pipe', None, 'tensor', 'fsdp')
- grad_conv_bc: float32 [2, 5, 256], P('pipe', None, ('fsdp', 'tensor'))
- grad_out_gain: float32 [2, 48, 64], P('pipe', 'tensor', 'fsdp')
- grad_head_params: float32 [2, 3, 48], P('pipe', None, 'tensor')
- grad_out_weight: float32 [2, 3072, 1536], P('pipe', 'tensor', 'fsdp')
Inputs may be any that keep to these rules, and one draw needn't show every extreme that they name: `seq_lengths`: each row of 3 lengths sums to 1024; the first and the last are under 1024 / 8, so the middle sequence starts in the first 128 rows of its group and ends in the last; in data group 0 of every micro-batch the first and the last are 1. `head_params`: row 0 between -4 and -1, row 1 between -4 and 1.5, row 2 between 0.5 and 1.5.
All inputs are finite; a program needn't handle non-finite values.
Results may differ from a plain program's by a relative error of at most 0.028.
Values may be sent and summed in bfloat16 or wider, within the bound.
No kernel may reach another device: no remote copies, remote signals or barrier semaphores. Data moves between devices by JAX's collectives and lax.ppermute only.
A program may use at most 256 MiB of HBM per device.

v0:
```python
import jax
import jax.numpy as jnp
from jax import lax
from jax.sharding import PartitionSpec as P

D = 1536
STATE = 128
STRETCH = 256
INNER = 3072


NORM_EPSILON = 1e-05


def shifted_2(block, axis, distance):
    devices = range(lax.axis_size(axis))
    route = [(i - distance, i) for i in devices if i - distance in devices]
    return lax.ppermute(block, axis, route)


def segment_rows(lengths, row_count):
    seq_ends = jnp.cumsum(lengths)
    starts = seq_ends - lengths
    positions = jnp.arange(row_count, dtype=jnp.int32)
    segment = jnp.sum((positions[:, None] >= seq_ends[None, :]).astype(jnp.int32), axis=1)
    member = (segment[:, None] == jnp.arange(lengths.shape[0], dtype=jnp.int32)[None, :]).astype(
        jnp.int32
    )
    inside = positions - jnp.sum(member * starts[None, :], axis=1)
    return (segment, inside)


def rms_norm(row_block, gain_vec):
    return (
        row_block
        * lax.rsqrt(jnp.mean(row_block * row_block, axis=1, keepdims=True) + NORM_EPSILON)
        * gain_vec
    )


def mixer_local(
    gate_in,
    conv_in,
    shared_in,
    step_in,
    conv_taps,
    shared_taps,
    head_vals,
    segment,
    inside,
    block_rows,
):
    row_count, inner_width = conv_in.shape
    head_count = step_in.shape[1]
    head_size = inner_width // head_count
    state_size = shared_in.shape[1] // 2
    tap_count = conv_taps.shape[0] - 1
    joined = jnp.concatenate([conv_in, shared_in], axis=1)
    filters = jnp.concatenate([conv_taps.reshape(tap_count + 1, inner_width), shared_taps], axis=1)
    conv_out = jnp.zeros_like(joined) + filters[tap_count]
    for lag_rows in range(tap_count):
        shifted = jnp.pad(joined, ((lag_rows, 0), (0, 0)))[:row_count]
        within = (inside >= lag_rows).astype(joined.dtype)[:, None]
        conv_out = conv_out + filters[tap_count - 1 - lag_rows] * shifted * within
    activated = jax.nn.silu(conv_out)
    values = activated[:, :inner_width].reshape(row_count, head_count, head_size)
    inputs_b = activated[:, inner_width : inner_width + state_size]
    outputs_c = activated[:, inner_width + state_size :]
    step_size = jax.nn.softplus(step_in + head_vals[0])
    log_decay = -step_size * jnp.exp(head_vals[1])
    scaled = values * step_size[:, :, None]
    block_count = row_count // block_rows
    positions = jnp.arange(block_rows, dtype=jnp.int32)
    lower_mask = positions[:, None] >= positions[None, :]
    lower_ones = lower_mask.astype(joined.dtype)

    def block_step(carried, block_items):
        held_state, previous = carried
        b_block, c_block, x_block, decay_block, seg_block = block_items
        cumulative = jnp.dot(lower_ones, decay_block, precision=lax.Precision.HIGHEST)
        across = cumulative.T
        same_seq = ((seg_block[:, None] == seg_block[None, :]) & lower_mask)[None, :, :]
        gap_logs = across[:, :, None] - across[:, None, :]
        weights = jnp.where(same_seq, jnp.exp(jnp.where(same_seq, gap_logs, 0.0)), 0.0)
        intersection = jnp.dot(c_block, b_block.T, precision=lax.Precision.HIGHEST)
        local_out = jnp.einsum(
            "hij,jhp->ihp",
            weights * intersection[None, :, :],
            x_block,
            precision=lax.Precision.HIGHEST,
        )
        carried_on = (seg_block == previous).astype(x_block.dtype)
        start_scale = jnp.exp(cumulative) * carried_on[:, None]
        from_state = (
            jnp.einsum("in,hpn->ihp", c_block, held_state, precision=lax.Precision.HIGHEST)
            * start_scale[:, :, None]
        )
        final_seg = seg_block[block_rows - 1]
        ending = (
            jnp.exp(cumulative[block_rows - 1][None, :] - cumulative)
            * (seg_block == final_seg).astype(x_block.dtype)[:, None]
        )
        fresh_state = jnp.einsum(
            "jh,jhp,jn->hpn", ending, x_block, b_block, precision=lax.Precision.HIGHEST
        )
        kept_scale = jnp.exp(cumulative[block_rows - 1]) * (final_seg == previous).astype(
            x_block.dtype
        )
        held_state = fresh_state + kept_scale[:, None, None] * held_state
        return ((held_state, final_seg), local_out + from_state)

    start_carry = (
        jnp.zeros((head_count, head_size, state_size), joined.dtype),
        jnp.array(-1, jnp.int32),
    )
    block_items = (
        inputs_b.reshape(block_count, block_rows, state_size),
        outputs_c.reshape(block_count, block_rows, state_size),
        scaled.reshape(block_count, block_rows, head_count, head_size),
        log_decay.reshape(block_count, block_rows, head_count),
        segment.reshape(block_count, block_rows),
    )
    final_carry, outputs = lax.scan(jax.checkpoint(block_step), start_carry, block_items)
    total = outputs.reshape(row_count, head_count, head_size) + head_vals[2][None, :, None] * values
    return total.reshape(row_count, inner_width) * jax.nn.silu(gate_in)


def contract_rows(left_rows, right_rows):
    return lax.dot_general(
        left_rows, right_rows, (((0,), (0,)), ((), ())), preferred_element_type=jnp.float32
    )


def reduce_grads(tick_grads):
    split_part, shared_part, head_part = tick_grads
    split_sum = (
        lax.psum_scatter(
            split_part[0].astype(jnp.bfloat16), "fsdp", scatter_dimension=0, tiled=True
        ).astype(jnp.float32),
        lax.psum_scatter(
            split_part[1].astype(jnp.bfloat16), "fsdp", scatter_dimension=0, tiled=True
        ).astype(jnp.float32),
        lax.psum_scatter(
            split_part[2].astype(jnp.bfloat16), "fsdp", scatter_dimension=2, tiled=True
        ).astype(jnp.float32),
        lax.psum_scatter(
            split_part[3].astype(jnp.bfloat16), "fsdp", scatter_dimension=1, tiled=True
        ).astype(jnp.float32),
        lax.psum_scatter(
            split_part[4].astype(jnp.bfloat16), "fsdp", scatter_dimension=1, tiled=True
        ).astype(jnp.float32),
    )
    shared_sum = (
        lax.psum_scatter(shared_part[0], ("fsdp", "tensor"), scatter_dimension=0, tiled=True),
        lax.psum_scatter(shared_part[1], ("fsdp", "tensor"), scatter_dimension=0, tiled=True),
        lax.psum_scatter(shared_part[2], ("fsdp", "tensor"), scatter_dimension=1, tiled=True),
    )
    head_sum = lax.psum(head_part, "fsdp")
    return (tuple(split_sum), tuple(shared_sum), head_sum)


def assemble(partial_grads, grad_cols, grad_out):
    grad_taps, grad_scale, grad_gain, grad_shared_taps, grad_heads = partial_grads
    inner_width = grad_out.shape[0]
    shared_end = 2 * inner_width + 2 * STATE
    split_grads = (
        grad_cols[:, : 2 * inner_width].reshape(grad_cols.shape[0], 2, inner_width),
        grad_cols[:, shared_end:],
        grad_taps,
        grad_scale,
        grad_out,
    )
    shared_grads = (grad_gain, grad_cols[:, 2 * inner_width : shared_end], grad_shared_taps)
    return (split_grads, shared_grads, grad_heads)


def shards(
    tokens,
    out_grad,
    seq_lengths,
    norm_gain,
    w_zx,
    w_bc,
    w_dt,
    conv_x,
    conv_bc,
    out_gain,
    head_params,
    out_weight,
):
    section_index = lax.axis_index("pipe")
    micro_count = tokens.shape[0]
    local_rows = tokens.shape[1]
    row_count = local_rows * lax.axis_size("tensor")
    head_values = head_params[0]
    gain_vec = lax.all_gather(norm_gain[0], "fsdp", axis=0, tiled=True)
    zx_full = lax.all_gather(w_zx[0], "fsdp", axis=0, tiled=True)
    shared_full = lax.all_gather(w_bc[0], "fsdp", axis=0, tiled=True)
    step_full = lax.all_gather(w_dt[0], "fsdp", axis=0, tiled=True)
    taps_full = lax.all_gather(conv_x[0], "fsdp", axis=2, tiled=True)
    shared_taps = lax.all_gather(conv_bc[0], "fsdp", axis=1, tiled=True)
    scale_full = lax.all_gather(out_gain[0], "fsdp", axis=1, tiled=True)
    out_full = lax.all_gather(out_weight[0], "fsdp", axis=1, tiled=True)
    inner_width = zx_full.shape[2]
    joined_cols = jnp.concatenate(
        [zx_full.reshape(D, 2 * inner_width), shared_full, step_full], axis=1
    )
    fetched = (
        gain_vec.astype(jnp.float32),
        joined_cols,
        taps_full.astype(jnp.float32),
        shared_taps.astype(jnp.float32),
        scale_full.astype(jnp.float32).reshape(inner_width),
        out_full,
    )

    def backward_tick(grad_rows, kept, weights):
        x_rows, segment, inside, gathered, projected, mixed_v, scale_rows, hidden_low = kept
        gain_vec, joined_cols, taps_full, shared_taps, out_scale, out_full = weights
        inner_width = out_full.shape[0]
        head_count = taps_full.shape[1]
        head_size = taps_full.shape[2]
        grad_low = grad_rows.astype(jnp.bfloat16)
        piece_rows = lax.all_gather(grad_low, "tensor", axis=0, tiled=True)
        grad_out = contract_rows(hidden_low, piece_rows)
        back_rows = lax.dot_general(
            piece_rows, out_full, (((1,), (1,)), ((), ())), preferred_element_type=jnp.float32
        )
        grad_hidden = back_rows
        first_part, grad_hidden = (grad_out, grad_hidden)
        weighted = grad_hidden * out_scale
        grad_scale = jnp.sum(grad_hidden * mixed_v * scale_rows[:, None], axis=0)
        inner_sum = lax.psum(jnp.sum(weighted * mixed_v, axis=1), "tensor")
        cubed = scale_rows * scale_rows * scale_rows
        grad_mixed = scale_rows[:, None] * weighted - mixed_v * (cubed * inner_sum / INNER)[:, None]
        shared_end = 2 * inner_width + 2 * STATE

        def mixer_part(gate_in, conv_in, shared_in, step_in, conv_taps, shared_tap_vals, head_vals):
            return mixer_local(
                gate_in,
                conv_in,
                shared_in,
                step_in,
                conv_taps,
                shared_tap_vals,
                head_vals,
                segment,
                inside,
                STRETCH,
            )

        mixed_again, pull_back = jax.vjp(
            mixer_part,
            projected[:, :inner_width],
            projected[:, inner_width : 2 * inner_width],
            projected[:, 2 * inner_width : shared_end],
            projected[:, shared_end:],
            taps_full,
            shared_taps,
            head_values,
        )
        grad_gate, grad_conv, grad_shared, grad_step, grad_taps, grad_shared_taps, grad_heads = (
            pull_back(grad_mixed)
        )
        grad_proj = jnp.concatenate([grad_gate, grad_conv, grad_shared, grad_step], axis=1).astype(
            jnp.bfloat16
        )
        grad_normed = lax.psum_scatter(
            lax.dot_general(
                grad_proj, joined_cols, (((1,), (1,)), ((), ())), preferred_element_type=jnp.float32
            ).astype(jnp.bfloat16),
            "tensor",
            scatter_dimension=0,
            tiled=True,
        ).astype(jnp.float32)
        normed_again, norm_pull = jax.vjp(rms_norm, x_rows, gain_vec)
        grad_x_norm, grad_gain = norm_pull(grad_normed)
        partial_grads = (
            grad_taps,
            grad_scale.reshape(head_count, head_size),
            grad_gain,
            grad_shared_taps,
            grad_heads,
        )
        grad_cols = contract_rows(gathered, grad_proj)
        return (grad_rows + grad_x_norm, partial_grads, (grad_cols, first_part))

    received = jnp.zeros((local_rows, D), jnp.float32)
    outputs_tick = []
    kept_tick = []
    for tick_index in range(micro_count + 1):
        micro_index = jnp.clip(tick_index - section_index, 0, micro_count - 1)
        segment, inside = segment_rows(seq_lengths[micro_index, 0], row_count)
        own_rows = tokens[min(tick_index, micro_count - 1)].astype(jnp.float32)
        x_rows = jnp.where(section_index == 0, own_rows, received)
        (
            forward_gain_vec,
            forward_joined_cols,
            forward_taps_full,
            forward_shared_taps,
            forward_out_scale,
            forward_out_full,
        ) = fetched
        forward_inner_width = forward_out_full.shape[0]
        normed_low = rms_norm(x_rows, forward_gain_vec).astype(jnp.bfloat16)
        forward_gathered = lax.all_gather(normed_low, "tensor", axis=0, tiled=True)
        forward_projected = jnp.dot(
            forward_gathered, forward_joined_cols, preferred_element_type=jnp.float32
        )
        forward_shared_end = 2 * forward_inner_width + 2 * STATE
        forward_mixed_v = mixer_local(
            forward_projected[:, :forward_inner_width],
            forward_projected[:, forward_inner_width : 2 * forward_inner_width],
            forward_projected[:, 2 * forward_inner_width : forward_shared_end],
            forward_projected[:, forward_shared_end:],
            forward_taps_full,
            forward_shared_taps,
            head_values,
            segment,
            inside,
            STRETCH,
        )
        squares = lax.psum(jnp.sum(forward_mixed_v * forward_mixed_v, axis=1), "tensor")
        forward_scale_rows = lax.rsqrt(squares / INNER + NORM_EPSILON)
        forward_hidden_low = (
            forward_mixed_v * forward_scale_rows[:, None] * forward_out_scale
        ).astype(jnp.bfloat16)
        out_rows = lax.psum_scatter(
            jnp.dot(
                forward_hidden_low, forward_out_full, preferred_element_type=jnp.float32
            ).astype(jnp.bfloat16),
            "tensor",
            scatter_dimension=0,
            tiled=True,
        ).astype(jnp.float32)
        y_rows = x_rows + out_rows
        kept = (
            x_rows,
            segment,
            inside,
            forward_gathered,
            forward_projected,
            forward_mixed_v,
            forward_scale_rows,
            forward_hidden_low,
        )
        outputs_tick.append(y_rows)
        kept_tick.append(kept)
        if tick_index < micro_count:
            received = shifted_2(y_rows.astype(jnp.bfloat16), "pipe", 1).astype(jnp.float32)
    incoming = jnp.zeros((local_rows, D), jnp.float32)
    grads_tick = []
    totals = None
    for tick_index in range(micro_count + 1):
        kept = jax.tree.map(
            lambda first_arr, second_arr: jnp.where(section_index == 0, first_arr, second_arr),
            kept_tick[max(tick_index - 1, 0)],
            kept_tick[min(tick_index + 1, micro_count)],
        )
        cotangent = out_grad[min(tick_index, micro_count - 1)].astype(jnp.float32)
        grad_rows = jnp.where(section_index == 1, cotangent, incoming)
        valid_flag = jnp.where(
            section_index == 0, tick_index >= 1, tick_index < micro_count
        ).astype(jnp.float32)
        grad_x, partial_grads, held = backward_tick(grad_rows, kept, fetched)
        partial_grads = jax.tree.map(lambda grad_value: grad_value * valid_flag, partial_grads)
        grads_tick.append(grad_x)
        grad_cols, grad_out = held
        tick_grads = assemble(partial_grads, grad_cols * valid_flag, grad_out * valid_flag)
        totals = tick_grads if totals is None else jax.tree.map(jnp.add, totals, tick_grads)
        if tick_index < micro_count:
            incoming = shifted_2(grad_x.astype(jnp.bfloat16), "pipe", -1).astype(jnp.float32)
    reduced = reduce_grads(totals)
    split_sum, shared_sum, head_sum = reduced
    section_out = jnp.stack(
        [
            jnp.where(section_index == 0, outputs_tick[micro_index], outputs_tick[micro_index + 1])
            for micro_index in range(micro_count)
        ]
    ).astype(jnp.bfloat16)[None]
    input_out = jnp.stack(
        [
            jnp.where(section_index == 1, grads_tick[micro_index], grads_tick[micro_index + 1])
            for micro_index in range(micro_count)
        ]
    ).astype(jnp.bfloat16)[None]
    return (
        section_out,
        input_out,
        shared_sum[0][None],
        split_sum[0][None],
        shared_sum[1][None],
        split_sum[1][None],
        split_sum[2][None],
        shared_sum[2][None],
        split_sum[3][None],
        head_sum[None],
        split_sum[4][None],
    )


def solution(mesh):
    return jax.shard_map(
        shards,
        mesh=mesh,
        in_specs=(
            P(None, ("fsdp", "tensor"), None),
            P(None, ("fsdp", "tensor"), None),
            P(None, "fsdp", None),
            P("pipe", "fsdp"),
            P("pipe", "fsdp", None, "tensor"),
            P("pipe", "fsdp", None),
            P("pipe", "fsdp", "tensor"),
            P("pipe", None, "tensor", "fsdp"),
            P("pipe", None, "fsdp"),
            P("pipe", "tensor", "fsdp"),
            P("pipe", None, "tensor"),
            P("pipe", "tensor", "fsdp"),
        ),
        out_specs=(
            P("pipe", None, ("fsdp", "tensor"), None),
            P("pipe", None, ("fsdp", "tensor"), None),
            P("pipe", ("fsdp", "tensor")),
            P("pipe", "fsdp", None, "tensor"),
            P("pipe", ("fsdp", "tensor"), None),
            P("pipe", "fsdp", "tensor"),
            P("pipe", None, "tensor", "fsdp"),
            P("pipe", None, ("fsdp", "tensor")),
            P("pipe", "tensor", "fsdp"),
            P("pipe", None, "tensor"),
            P("pipe", "tensor", "fsdp"),
        ),
        check_vma=False,
    )
```

profile of v0, /device:TPU:0, one launch (start us, length us, event | category | flops | bytes accessed | tf_op | source)
XLA Modules:
  0.0 3040.4 jit_solution(14922106743842971335)
XLA Ops:
  27.3 29.9 all-gather.2
  124.9 39.6 %all-gather.17.cloned.1.call-done = bf16[1024,1536]{1,0:T(8,128)(2,1)} async-done(((bf16[256,1536]{1,0:T(8,128)(2,1)}), bf16[1024,1536]{1,0:T(8,128)(2,1)}) %all-gather.17.cloned.1.call-update) | async-done | bytes 3145744 | tf_op jit(solution)/shard_map/all_gather | solution.py:306
  198.0 120.2 %while.177 = (s32[]{:T(128)}, f32[12,64,128]{2,1,0:T(8,128)S(1)}, s32[]{:T(128)}, f32[4,256,12,64]{1,0,3,2:T(4,128)}, f32[4,256,12]{1,0,2:T(4,128)S(1)}, /*index...) while((s32[]{:T(128)}, f32[12,64,128]{2,1,0:T(8,128)S(1)}, ...), condition=%wide.region_5.6_spmd.clone, body=%wide.region_4.5_spmd.clone.sunk | while | flops 1322526720 | bytes 9600442 | solution.py:123
  206.8 17.9 dynamic_update_slice.233
  236.9 17.9 dynamic_update_slice.233
  266.9 17.9 dynamic_update_slice.233
  297.0 17.9 dynamic_update_slice.233
  341.4 44.1 %reduce-scatter.25.cloned.1.call-done = bf16[256,1536]{1,0:T(8,128)(2,1)} async-done(((bf16[1024,1536]{1,0:T(8,128)(2,1)}), bf16[256,1536]{1,0:T(8,128)(2,1)}) %reduce-scatter.25.cloned.1.call-update) | async-done | bytes 786448 | tf_op jit(solution)/shard_map/reduce_scatter | solution.py:328
  394.9 41.3 %all-gather.19.cloned.1.call-done = bf16[1024,1536]{1,0:T(8,128)(2,1)} async-done(((bf16[256,1536]{1,0:T(8,128)(2,1)}), bf16[1024,1536]{1,0:T(8,128)(2,1)}) %all-gather.19.cloned.1.call-update) | async-done | bytes 3145744 | tf_op jit(solution)/shard_map/all_gather | solution.py:306
  473.7 147.2 %while.178 = (s32[]{:T(128)}, f32[12,64,128]{2,1,0:T(8,128)S(1)}, s32[]{:T(128)}, f32[4,256,12,64]{1,0,3,2:T(4,128)}, f32[4,256,12]{1,0,2:T(4,128)}, /*index=5*/...) while((s32[]{:T(128)}, f32[12,64,128]{2,1,0:T(8,128)S(1)}, ...), condition=%wide.region_14.15_spmd.clone, body=%wide.region_13.14_spmd.clone.sunk | while | flops 1322526720 | bytes 9649914 | solution.py:123
  653.7 44.1 %reduce-scatter.27.cloned.1.call-done = bf16[256,1536]{1,0:T(8,128)(2,1)} async-done(((bf16[1024,1536]{1,0:T(8,128)(2,1)}), bf16[256,1536]{1,0:T(8,128)(2,1)}) %reduce-scatter.27.cloned.1.call-update) | async-done | bytes 786448 | tf_op jit(solution)/shard_map/reduce_scatter | solution.py:328
  709.7 41.5 %all-gather.21.cloned.1.call-done = bf16[1024,1536]{1,0:T(8,128)(2,1)} async-done(((bf16[256,1536]{1,0:T(8,128)(2,1)}), bf16[1024,1536]{1,0:T(8,128)(2,1)}) %all-gather.21.cloned.1.call-update) | async-done | bytes 3145744 | tf_op jit(solution)/shard_map/all_gather | solution.py:306
  751.2 19.0 broadcast_select_fusion.3
  804.9 119.6 %while.179 = (s32[]{:T(128)}, f32[12,64,128]{2,1,0:T(8,128)S(1)}, s32[]{:T(128)}, f32[4,256,12,64]{1,0,3,2:T(4,128)}, f32[4,256,12]{1,0,2:T(4,128)S(1)}, /*index...) while((s32[]{:T(128)}, f32[12,64,128]{2,1,0:T(8,128)S(1)}, ...), condition=%wide.region_23.24_spmd.clone, body=%wide.region_22.23_spmd.clone.sunk | while | flops 1322526720 | bytes 9600442 | solution.py:123
  813.8 17.9 dynamic_update_slice.235
  843.7 17.9 dynamic_update_slice.235
  873.5 17.9 dynamic_update_slice.235
  903.4 17.9 dynamic_update_slice.235
  959.9 135.3 %while.180 = (s32[]{:T(128)}, f32[12,64,128]{2,1,0:T(8,128)S(1)}, s32[]{:T(128)}, f32[4,256,12,64]{1,0,3,2:T(4,128)}, f32[4,12,64,128]{3,2,1,0:T(8,128)S(1)}, /*...) while((s32[]{:T(128)}, f32[12,64,128]{2,1,0:T(8,128)S(1)}, ...), condition=%wide.region_28.30_spmd.clone, body=%wide.region_27.29_spmd.clone.sunk | while | flops 1322625024 | bytes 10358787 | solution.py:123
  972.4 17.9 dynamic_update_slice.237
  1006.3 17.9 dynamic_update_slice.237
  1040.1 17.9 dynamic_update_slice.237
  1073.9 17.9 dynamic_update_slice.237
  1113.5 208.0 %while.181 = (s32[]{:T(128)}, f32[12,64,128]{2,1,0:T(8,128)S(1)}, f32[4,256,128]{2,1,0:T(8,128)}, f32[4,256,128]{2,1,0:T(8,128)}, f32[4,256,12,64]{1,0,3,2:T(4,1...) while((s32[]{:T(128)}, f32[12,64,128]{2,1,0:T(8,128)S(1)}, ...), condition=%wide.region_38.40_spmd.clone, body=%wide.region_31.39_spmd.clone.sunk | while | flops 3053136896 | bytes 27561300 | solution.py:123
  1140.9 17.9 dynamic_update_slice.241
  1192.8 17.9 dynamic_update_slice.241
  1244.7 17.9 dynamic_update_slice.241
  1395.3 44.0 %reduce-scatter.31.cloned.1.call-done = bf16[256,1536]{1,0:T(8,128)(2,1)} async-done(((bf16[1024,1536]{1,0:T(8,128)(2,1)}), bf16[256,1536]{1,0:T(8,128)(2,1)}) %reduce-scatter.31.cloned.1.call-update) | async-done | bytes 786448 | tf_op jit(solution)/shard_map/reduce_scatter | solution.py:268
  1471.1 136.2 %while.182 = (s32[]{:T(128)}, f32[12,64,128]{2,1,0:T(8,128)S(1)}, s32[]{:T(128)}, f32[4,256,12,64]{1,0,3,2:T(4,128)}, f32[4,12,64,128]{3,2,1,0:T(8,128)S(1)}, /*...) while((s32[]{:T(128)}, f32[12,64,128]{2,1,0:T(8,128)S(1)}, ...), condition=%wide.region_44.46_spmd.clone, body=%wide.region_43.45_spmd.clone.sunk | while | flops 1322625024 | bytes 10358787 | solution.py:123
  1483.9 17.9 dynamic_update_slice.244
  1518.0 17.9 dynamic_update_slice.244
  1552.0 17.9 dynamic_update_slice.244
  1586.0 17.9 dynamic_update_slice.244
  1647.7 207.2 %while.183 = (s32[]{:T(128)}, f32[12,64,128]{2,1,0:T(8,128)S(1)}, f32[4,256,128]{2,1,0:T(8,128)}, f32[4,256,128]{2,1,0:T(8,128)}, f32[4,256,12,64]{1,0,3,2:T(4,1...) while((s32[]{:T(128)}, f32[12,64,128]{2,1,0:T(8,128)S(1)}, ...), condition=%wide.region_54.56_spmd.clone, body=%wide.region_47.55_spmd.clone.sunk | while | flops 3053136896 | bytes 27561300 | solution.py:123
  1674.8 17.9 dynamic_update_slice.248
  1726.4 17.9 dynamic_update_slice.248
  1778.1 17.9 dynamic_update_slice.248
  1829.7 17.9 dynamic_update_slice.248
  1900.5 43.2 %reduce-scatter.33.cloned.1.call-done = bf16[256,1536]{1,0:T(8,128)(2,1)} async-done(((bf16[1024,1536]{1,0:T(8,128)(2,1)}), bf16[256,1536]{1,0:T(8,128)(2,1)}) %reduce-scatter.33.cloned.1.call-update) | async-done | bytes 786448 | tf_op jit(solution)/shard_map/reduce_scatter | solution.py:268
  1990.2 136.2 %while.184 = (s32[]{:T(128)}, f32[12,64,128]{2,1,0:T(8,128)S(1)}, s32[]{:T(128)}, f32[4,256,12,64]{1,0,3,2:T(4,128)}, f32[4,12,64,128]{3,2,1,0:T(8,128)S(1)}, /*...) while((s32[]{:T(128)}, f32[12,64,128]{2,1,0:T(8,128)S(1)}, ...), condition=%wide.region_60.62_spmd.clone, body=%wide.region_59.61_spmd.clone.sunk | while | flops 1322625024 | bytes 10358787 | solution.py:123
  2003.4 17.9 dynamic_update_slice.251
  2178.5 207.7 %while.185 = (s32[]{:T(128)}, f32[12,64,128]{2,1,0:T(8,128)S(1)}, f32[4,256,128]{2,1,0:T(8,128)}, f32[4,256,128]{2,1,0:T(8,128)}, f32[4,256,12,64]{1,0,3,2:T(4,1...) while((s32[]{:T(128)}, f32[12,64,128]{2,1,0:T(8,128)S(1)}, ...), condition=%wide.region_70.72_spmd.clone, body=%wide.region_63.71_spmd.clone.sunk | while | flops 3053136896 | bytes 27561300 | solution.py:123
  2538.0 126.4 %reduce-scatter.37.cloned.1.call-done = f32[96,256]{1,0:T(8,128)} async-done(((f32[1536,256]{1,0:T(8,128)}), f32[96,256]{1,0:T(8,128)}) %reduce-scatter.37.cloned.1.call-update) | async-done | bytes 98320
  2666.1 48.0 %reduce-scatter.47.cloned.1.call-done = bf16[384,768]{1,0:T(8,128)(2,1)} async-done(((bf16[1536,768]{1,0:T(8,128)(2,1)}), bf16[384,768]{1,0:T(8,128)(2,1)}) %reduce-scatter.47.cloned.1.call-update) | async-done | bytes 589840
  2716.4 171.6 %all-reduce.71.cloned.1.call-done = bf16[1536,2,768]{2,1,0:T(2,128)(2,1)} async-done(((bf16[1536,2,768]{2,1,0:T(2,128)(2,1)}), bf16[1536,2,768]{2,1,0:T(2,128)(2,1)}) %all-reduce.71.cloned.1.call-update) | async-done | bytes 4718608
  2892.6 41.2 %reduce-scatter.35.cloned.1.call-done = bf16[256,1536]{1,0:T(8,128)(2,1)} async-done(((bf16[1024,1536]{1,0:T(8,128)(2,1)}), bf16[256,1536]{1,0:T(8,128)(2,1)}) %reduce-scatter.35.cloned.1.call-update) | async-done | bytes 786448 | tf_op jit(solution)/shard_map/reduce_scatter | solution.py:268
  2933.8 47.0 %reduce-scatter.29.cloned.1.call-done = bf16[256,1536]{1,0:T(8,128)(2,1)} async-done(((bf16[1024,1536]{1,0:T(8,128)(2,1)}), bf16[256,1536]{1,0:T(8,128)(2,1)}) %reduce-scatter.29.cloned.1.call-update) | async-done | bytes 786448 | tf_op jit(solution)/shard_map/reduce_scatter | solution.py:328
  2985.5 41.3 %all-reduce.66 = f32[1536]{0:T(1024)S(1)} all-reduce(f32[1536]{0:T(1024)S(1)} %multiply_add_fusion.3), channel_id=16, replica_groups=mesh['pipe'=2,'fsdp'=4,'tensor'=4] {'fsdp','tensor'}, use_global_device_ids=true, to_apply=%region_78.80.clone | all-reduce | flops 1536 | bytes 12288
  (1797 shorter events, 1718.4 us)
Async XLA Ops:
  7.2 112.2 %all-gather.29.cloned.1.call-start = ((), (), s32[]{:S(2)}) async-start(), calls=%async_computation.24 | async-start | bytes 5898240 | tf_op jit(solution)/shard_map/all_gather | solution.py:197
  7.9 79.9 %copy-start.263 = (bf16[1,5,64]{2,1,0:T(8,128)(2,1)S(1)}, bf16[1,5,64]{2,1,0:T(8,128)(2,1)}, u32[]{:S(2)}) copy-start(bf16[1,5,64]{2,1,0:T(8,128)(2,1)} %param.39) | copy-start | bytes 1924
  8.0 94.6 %copy-start.262 = (f32[1,3,12]{2,0,1:T(1,128)S(1)}, f32[1,3,12]{2,0,1:T(1,128)}, u32[]{:S(2)}) copy-start(f32[1,3,12]{2,0,1:T(1,128)} %param.41) | copy-start | bytes 436
  8.0 94.8 %copy-start.260 = (bf16[1,12,16]{2,1,0:T(8,128)(2,1)S(1)}, bf16[1,12,16]{2,1,0:T(8,128)(2,1)}, u32[]{:S(2)}) copy-start(bf16[1,12,16]{2,1,0:T(8,128)(2,1)} %param.40) | copy-start | bytes 1156
  8.0 156.5 %all-gather.17.cloned.1.call-start = ((), (), s32[]{:S(2)}) async-start(), calls=%async_computation.12 | async-start | bytes 3932160 | tf_op jit(solution)/shard_map/all_gather | solution.py:306
  21.7 369.1 %copy-start.103 = (f32[1536]{0:T(1024)}, f32[1536]{0:T(1024)S(1)}, u32[]{:S(2)}) copy-start(f32[1536]{0:T(1024)S(1)} %convert_reduce_fusion.4) | copy-start | bytes 18436
  25.5 309.4 %all-gather.31.cloned.1.call-start = ((), (), s32[]{:S(2)}) async-start(), calls=%async_computation.25 | async-start | bytes 2949120 | tf_op jit(solution)/shard_map/all_gather | solution.py:203
  26.3 359.2 %reduce-scatter.25.cloned.1.call-start = ((), (), s32[]{:S(2)}) async-start(), calls=%async_computation.13 | async-start | bytes 3932160 | tf_op jit(solution)/shard_map/reduce_scatter | solution.py:328
  26.6 98.2 %copy-start.190 = (s32[1024]{0:T(1024)}, s32[1024]{0:T(1024)S(1)}, u32[]{:S(2)}) copy-start(s32[1024]{0:T(1024)S(1)} %convert_reduce_fusion) | copy-start | bytes 12292
  27.1 97.8 %copy-start.192 = (s32[1024]{0:T(1024)}, s32[1024]{0:T(1024)S(1)}, u32[]{:S(2)}) copy-start(s32[1024]{0:T(1024)S(1)} %convert_reduce_fusion.1) | copy-start | bytes 12292
  57.2 107.3 %copy-start.70 = (bf16[1,1536,256]{2,1,0:T(8,128)(2,1)}, bf16[1,1536,256]{2,1,0:T(8,128)(2,1)S(1)}, u32[]{:S(2)}) copy-start(bf16[1,1536,256]{2,1,0:T(8,128)(2,1)S(1)} %all-gather.2) | copy-start | bytes 2359300
  72.9 91.6 %copy-start.90 = (bf16[1536,12]{1,0:T(8,128)(2,1)}, bf16[1536,12]{1,0:T(8,128)(2,1)S(1)}, u32[]{:S(2)}) copy-start(bf16[1536,12]{1,0:T(8,128)(2,1)S(1)} %copy.448) | copy-start | bytes 110596
  102.6 87.6 %copy-start.220 = (f32[12]{0:T(128)}, f32[12]{0:T(128)S(1)}, u32[]{:S(2)}) copy-start(f32[12]{0:T(128)S(1)} %get-tuple-element.3163) | copy-start | bytes 148
  102.6 87.6 %copy-start.226 = (f32[12]{0:T(128)}, f32[12]{0:T(128)S(1)}, u32[]{:S(2)}) copy-start(f32[12]{0:T(128)S(1)} %get-tuple-element.3164) | copy-start | bytes 148
  102.7 218.3 %copy-start.112 = (f32[768]{0:T(1024)}, f32[768]{0:T(1024)S(1)}, u32[]{:S(2)}) copy-start(f32[768]{0:T(1024)S(1)} %mul.2672) | copy-start | bytes 9220
  116.3 217.1 %copy-start.108 = (f32[768]{0:T(1024)}, f32[768]{0:T(1024)S(1)}, u32[]{:S(2)}) copy-start(f32[768]{0:T(1024)S(1)} %reshape.1546) | copy-start | bytes 9220
  116.4 332.8 %copy-start.124 = (f32[1,1024]{1,0:T(1,128)}, f32[1,1024]{1,0:T(1,128)S(1)}, u32[]{:S(2)}) copy-start(f32[1,1024]{1,0:T(1,128)S(1)} %get-tuple-element.3119) | copy-start | bytes 12292
  116.4 332.8 %copy-start.129 = (f32[1,1024]{1,0:T(1,128)}, f32[1,1024]{1,0:T(1,128)S(1)}, u32[]{:S(2)}) copy-start(f32[1,1024]{1,0:T(1,128)S(1)} %get-tuple-element.3120) | copy-start | bytes 12292
  341.4 94.9 %all-gather.19.cloned.1.call-start = ((), (), s32[]{:S(2)}) async-start(), calls=%async_computation.14 | async-start | bytes 3932160 | tf_op jit(solution)/shard_map/all_gather | solution.py:306
  386.9 3.6 collective-permute-start
  390.5 307.2 %copy-start.37 = (bf16[256,1536]{1,0:T(8,128)(2,1)}, bf16[256,1536]{1,0:T(8,128)(2,1)S(1)}, u32[]{:S(2)}) copy-start(bf16[256,1536]{1,0:T(8,128)(2,1)S(1)} %collective-permute-done) | copy-start | bytes 2359300
  392.1 245.3 %all-gather.23.cloned.1.call-start = ((), (), s32[]{:S(2)}) async-start(), calls=%async_computation.18 | async-start | bytes 3932160 | tf_op jit(solution)/shard_map/all_gather | solution.py:224
  394.3 303.4 %reduce-scatter.27.cloned.1.call-start = ((), (), s32[]{:S(2)}) async-start(), calls=%async_computation.15 | async-start | bytes 3932160 | tf_op jit(solution)/shard_map/reduce_scatter | solution.py:328
  653.6 97.6 %all-gather.21.cloned.1.call-start = ((), (), s32[]{:S(2)}) async-start(), calls=%async_computation.16 | async-start | bytes 3932160 | tf_op jit(solution)/shard_map/all_gather | solution.py:306
  701.0 3.8 collective-permute-start.1
  707.1 732.3 %reduce-scatter.31.cloned.1.call-start = ((), (), s32[]{:S(2)}) async-start(), calls=%async_computation.19 | async-start | bytes 3932160 | tf_op jit(solution)/shard_map/reduce_scatter | solution.py:268
  707.2 75.7 %copy-start.179 = (f32[1024]{0:T(1024)}, f32[1024]{0:T(1024)S(1)}, u32[]{:S(2)}) copy-start(f32[1024]{0:T(1024)S(1)} %get-tuple-element.3154) | copy-start | bytes 12292
  707.2 75.7 %copy-start.181 = (f32[1024]{0:T(1024)}, f32[1024]{0:T(1024)S(1)}, u32[]{:S(2)}) copy-start(f32[1024]{0:T(1024)S(1)} %get-tuple-element.3155) | copy-start | bytes 12292
  1395.2 218.3 %all-gather.25.cloned.1.call-start = ((), (), s32[]{:S(2)}) async-start(), calls=%async_computation.20 | async-start | bytes 3932160 | tf_op jit(solution)/shard_map/all_gather | solution.py:224
  1444.1 22.3 collective-permute-start.2
  1468.7 475.0 %reduce-scatter.33.cloned.1.call-start = ((), (), s32[]{:S(2)}) async-start(), calls=%async_computation.21 | async-start | bytes 3932160 | tf_op jit(solution)/shard_map/reduce_scatter | solution.py:268
  1899.0 244.0 %all-gather.27.cloned.1.call-start = ((), (), s32[]{:S(2)}) async-start(), calls=%async_computation.22 | async-start | bytes 3932160 | tf_op jit(solution)/shard_map/all_gather | solution.py:224
  1951.8 33.6 %collective-permute-start.3 = (bf16[256,1536]{1,0:T(8,128)(2,1)}, bf16[256,1536]{1,0:T(8,128)(2,1)}, u32[]{:S(2)}, u32[]{:S(2)}) collective-permute-start(bf16[256,1536]{1,0:T(8,128)(2,1)} %get-tuple-element.2978), channel_id=1, source_target_pairs={{16,0},{17,1},{18,2},{19,3},{20,4},{21,5},{22,6},{23,7},{24,8},{25... | collective-permute-start | bytes 2359304 | tf_op jit(solution)/shard_map/ppermute | solution.py:18
  1987.7 537.7 %reduce-scatter.45.cloned.1.call-start = ((), (), s32[]{:S(2)}) async-start(), calls=%async_computation.30 | async-start | bytes 20480
  2392.5 134.4 %reduce-scatter.43.cloned.1.call-start = ((), (), s32[]{:S(2)}) async-start(), calls=%async_computation.29 | async-start | bytes 139264
  2420.9 107.3 %reduce-scatter.41.cloned.1.call-start = ((), (), s32[]{:S(2)}) async-start(), calls=%async_computation.28 | async-start | bytes 20480
  2421.9 114.4 %reduce-scatter.39.cloned.1.call-start = ((), (), s32[]{:S(2)}) async-start(), calls=%async_computation.27 | async-start | bytes 491520
  2445.3 219.1 %reduce-scatter.37.cloned.1.call-start = ((), (), s32[]{:S(2)}) async-start(), calls=%async_computation.26 | async-start | bytes 1671168
  2449.7 264.4 %reduce-scatter.47.cloned.1.call-start = ((), (), s32[]{:S(2)}) async-start(), calls=%async_computation.31 | async-start | bytes 2949120
  2463.2 424.8 %all-reduce.71.cloned.1.call-start = ((), (), s32[]{:S(2)}) async-start(), calls=%async_computation.32 | async-start | bytes 9437184
  2488.3 445.5 %reduce-scatter.35.cloned.1.call-start = ((), (), s32[]{:S(2)}) async-start(), calls=%async_computation.23 | async-start | bytes 3932160 | tf_op jit(solution)/shard_map/reduce_scatter | solution.py:268
  2501.4 479.3 %reduce-scatter.29.cloned.1.call-start = ((), (), s32[]{:S(2)}) async-start(), calls=%async_computation.17 | async-start | bytes 3932160 | tf_op jit(solution)/shard_map/reduce_scatter | solution.py:328
  2714.1 266.7 %copy-start.2 = (bf16[2,256,1536]{2,1,0:T(8,128)(2,1)S(1)}, bf16[2,256,1536]{2,1,0:T(8,128)(2,1)}, u32[]{:S(2)}) copy-start(bf16[2,256,1536]{2,1,0:T(8,128)(2,1)} %param.31) | copy-start | bytes 4718596
  2714.1 266.7 %copy-start.39 = (bf16[256,1536]{1,0:T(8,128)(2,1)S(1)}, bf16[256,1536]{1,0:T(8,128)(2,1)}, u32[]{:S(2)}) copy-start(bf16[256,1536]{1,0:T(8,128)(2,1)} %copy-done.37) | copy-start | bytes 2359300
  2714.1 266.7 %copy-start.42 = (bf16[256,1536]{1,0:T(8,128)(2,1)S(1)}, bf16[256,1536]{1,0:T(8,128)(2,1)}, u32[]{:S(2)}) copy-start(bf16[256,1536]{1,0:T(8,128)(2,1)} %copy-done.40) | copy-start | bytes 2359300
  2714.1 266.7 %copy-start.107 = (f32[1536]{0:T(1024)S(1)}, f32[1536]{0:T(1024)}, u32[]{:S(2)}) copy-start(f32[1536]{0:T(1024)} %copy-done.103) | copy-start | bytes 18436
  2892.6 92.9 %copy-start.214 = (f32[1536]{0:T(1024)S(1)}, f32[1536]{0:T(1024)}, u32[]{:S(2)}) copy-start(f32[1536]{0:T(1024)} %get-tuple-element.2751) | copy-start | bytes 18436
  2892.6 92.9 %copy-start.215 = (f32[1536]{0:T(1024)S(1)}, f32[1536]{0:T(1024)}, u32[]{:S(2)}) copy-start(f32[1536]{0:T(1024)} %get-tuple-element.2749) | copy-start | bytes 18436
  (310 other events, 2618.1 us)
Sparse Core Ops, SparseCore 0:
  9.6 109.7 all-gather.28
  121.9 42.5 all-gather.16
  166.1 50.2 all-gather.30
  341.5 43.9 reduce-scatter.24
  392.2 43.9 all-gather.18
  438.5 43.9 all-gather.22
  653.7 43.9 reduce-scatter.26
  707.2 43.9 all-gather.20
  1395.3 43.9 reduce-scatter.30
  1468.8 45.5 all-gather.24
  1899.1 44.5 reduce-scatter.32
  1987.8 44.0 all-gather.26
  2392.6 18.7 reduce-scatter.44
  2421.0 75.7 reduce-scatter.42
  2499.5 15.2 reduce-scatter.40
  2517.5 18.8 reduce-scatter.38
  2541.6 122.7 reduce-scatter.36
  2667.1 46.9 reduce-scatter.46
  2716.5 171.4 all-reduce.70
  2890.8 42.9 reduce-scatter.34
  2936.8 43.9 reduce-scatter.28
where the time goes:
time: 3080 us; the launch traced here: 3040 us
  local copies, waits for them, and re-layouts  1080 us (35%)
  waiting for transfers between devices  746 us (24%)
  matrix products  630 us (20%)
  other arithmetic  305 us (10%)
  blocking collectives  201 us (7%)
  loops' own time  51.3 us (2%)
    dynamic_update_slice x108, local copies, waits for them, and re-layouts, mixer_local(): lax.scan(jax.checkpoint(block_step), start_carry, block_items)  692 us
    unnamed x28, waiting for transfers between devices  354 us
    dot_general x48, matrix products, block_step(): jnp.einsum('hij,jhp->ihp', weights * intersection[None, :, :], x_block, p...  224 us
    reduce_scatter x3, waiting for transfers between devices, shards(): lax.psum_scatter(jnp.dot(forward_hidden_low, forward_out_full, preferred_...  135 us
    reduce_scatter x3, waiting for transfers between devices, backward_tick(): lax.psum_scatter(lax.dot_general(grad_proj, joined_cols, (((1,), (1,)), (...  128 us
    all_gather x3, waiting for transfers between devices, shards(): forward_gathered = lax.all_gather(normed_low, 'tensor', axis=0, tiled=True)  122 us
    unnamed x602, local copies, waits for them, and re-layouts  96.6 us
    dot_general x48, matrix products, block_step(): jnp.einsum('jh,jhp,jn->hpn', ending, x_block, b_block, precision=lax.Prec...  86.6 us
  transfers between devices with their start and end apart: 25, of which 16 were waited for; matrix products, arithmetic and copies ran while one was open for 27% of the time, Pallas kernels for 0%

commit v1 on v0

v1 whole, which is shorter than its diff:
```python
import jax
import jax.numpy as jnp
from jax import lax
from jax.experimental import pallas as pl
from jax.experimental.pallas import tpu as pltpu
from jax.sharding import PartitionSpec as P

STATE = 128
CHUNK = 256
HALF = 128
LANES = 128
NORM_EPSILON = 1e-05
LOG2E = 1.4426950408889634
F32 = jnp.float32
BF16 = jnp.bfloat16
VMEM_LIMIT = 56 * 1024 * 1024


def dot(a, b):
    return lax.dot_general(a, b, (((1,), (0,)), ((), ())), preferred_element_type=F32)


def dot_nt(a, b):
    return lax.dot_general(a, b, (((1,), (1,)), ((), ())), preferred_element_type=F32)


def dot_tn(a, b):
    return lax.dot_general(a, b, (((0,), (0,)), ((), ())), preferred_element_type=F32)


def pieces(value, count):
    found = []
    for _ in range(count):
        part = value.astype(BF16)
        found.append(part)
        value = value - part.astype(F32)
    return found


def dot_exact(ones, value):
    first, second, third = pieces(value, 3)
    return dot(ones, first) + (dot(ones, second) + dot(ones, third))


def spread(value, expander):
    first, second = pieces(value, 2)
    return dot(first, expander) + dot(second, expander)


def sigmoid(value):
    return 0.5 * jnp.tanh(0.5 * value) + 0.5


def softplus(value):
    return jnp.maximum(value, 0.0) + jnp.log1p(jnp.exp(-jnp.abs(value)))


def iota(shape, axis):
    return lax.broadcasted_iota(jnp.int32, shape, axis)


def segment_of(rows, first_end, second_end):
    return (rows >= first_end).astype(jnp.int32) + (rows >= second_end).astype(jnp.int32)


def head_expander(width):
    size = (LANES, width)
    return (iota(size, 0) == iota(size, 1) // 64).astype(BF16)


def head_folder(width):
    size = (width, LANES)
    return (iota(size, 1) == iota(size, 0) // 64).astype(BF16)


def lower_ones():
    size = (CHUNK, CHUNK)
    return (iota(size, 0) >= iota(size, 1)).astype(BF16)


def upper_ones():
    size = (CHUNK, CHUNK)
    return (iota(size, 0) <= iota(size, 1)).astype(BF16)


def decays(raw, head_ref, base, first_end, second_end, chunk):
    pre = raw + head_ref[0:1, :]
    step = softplus(pre)
    log_decay = -step * head_ref[1:2, :]
    total = dot_exact(lower_ones(), log_decay) * LOG2E
    rows = base + iota((CHUNK, LANES), 0)
    segment = segment_of(rows, first_end, second_end)
    previous = jnp.where(chunk == 0, -1, segment_of(base - 1, first_end, second_end))
    final = segment_of(base + CHUNK - 1, first_end, second_end)
    last = total[CHUNK - 1 : CHUNK, :]
    start = jnp.where(segment == previous, jnp.exp2(total), 0.0)
    ending = jnp.where(segment == final, jnp.exp2(last - total), 0.0)
    kept = jnp.where(final == previous, jnp.exp2(last), 0.0)
    return pre, step, log_decay, total, start, ending, kept


def same_block(row_base, col_base, first_end, second_end):
    size = (HALF, HALF)
    rows = row_base + iota(size, 0)
    cols = col_base + iota(size, 1)
    return (
        (segment_of(rows, first_end, second_end) == segment_of(cols, first_end, second_end)),
        rows,
        cols,
    )


def forward_kernel(
    scalars,
    x_ref,
    own_ref,
    other_ref,
    step_ref,
    out_own_ref,
    out_other_ref,
    taps_ref,
    gain_ref,
    skip_ref,
    head_ref,
    *rest,
):
    with_grad = len(rest) == 17
    rest = list(rest)
    grad_ref = rest.pop(0) if with_grad else None
    (
        part_ref,
        sums_ref,
        z_ref,
        conv_ref,
        input_ref,
        y_ref,
        raw_ref,
        state_ref,
        joined,
        state,
        hidden,
        end_x,
        from_state,
        step_wide,
        start_wide,
        end_wide,
    ) = rest
    chunk = pl.program_id(0)
    side, first_end, second_end = scalars[0], scalars[1], scalars[2]
    base = chunk * CHUNK
    width = hidden.shape[1]
    half = width // 2

    @pl.when(chunk == 0)
    def _():
        state[...] = jnp.zeros_like(state)
        joined[0:8, :] = jnp.zeros((8, joined.shape[1]), F32)

    x = x_ref[0]
    own = dot(x, own_ref[...])
    other = dot(x, other_ref[...])
    raw = dot(x, step_ref[...])
    raw_ref[0] = raw
    z_ref[0, :, :half] = own[:, :half].astype(BF16)
    z_ref[0, :, half:] = other[:, :half].astype(BF16)
    joined[8:, :half] = own[:, half:width]
    joined[8:, half:width] = other[:, half:width]
    joined[8:, width : width + STATE] = jnp.where(side == 0, own[:, width:], other[:, width:])
    joined[8:, width + STATE :] = jnp.where(side == 0, other[:, width:], own[:, width:])

    _, step, _, total, start, ending, kept = decays(
        raw, head_ref, base, first_end, second_end, chunk
    )
    expander = head_expander(width)
    step_wide[...] = spread(step, expander)
    start_wide[...] = spread(start, expander)
    end_wide[...] = spread(ending, expander)
    kept_wide = spread(jnp.broadcast_to(kept, (8, LANES)), expander)[0:1]
    total_rows = total.T

    rows = base + iota((CHUNK, LANES), 0)
    inside = rows - jnp.where(
        rows >= second_end, second_end, jnp.where(rows >= first_end, first_end, 0)
    )
    masks = [(inside >= lag).astype(F32) for lag in range(1, 4)]

    def activate(lanes):
        current = joined[8:, lanes]
        found = taps_ref[4:5, lanes] + taps_ref[3:4, lanes] * current
        for lag in range(1, 4):
            shifted = joined[8 - lag : 8 - lag + CHUNK, lanes] * masks[lag - 1]
            found = found + taps_ref[3 - lag : 4 - lag, lanes] * shifted
        conv_ref[0, :, lanes] = found.astype(BF16)
        input_ref[0, :, lanes] = current.astype(BF16)
        return found * sigmoid(found)

    b_f32 = activate(slice(width, width + STATE))
    b_low = b_f32.astype(BF16)
    c_low = activate(slice(width + STATE, width + 2 * STATE)).astype(BF16)
    state_ref[0] = state[...].astype(BF16)
    from_state[...] = dot(c_low, state[...].astype(BF16))
    inter = dot_nt(c_low, b_low)

    def masked(row_at, col_at):
        same, row_ids, col_ids = same_block(base + row_at, base + col_at, first_end, second_end)
        if row_at == col_at:
            same = same & (row_ids >= col_ids)
        return jnp.where(same, inter[row_at : row_at + HALF, col_at : col_at + HALF], 0.0)

    inter_00, inter_10, inter_11 = masked(0, 0), masked(HALF, 0), masked(HALF, HALF)
    low_lanes = iota((CHUNK, LANES), 1) < 64
    squares = jnp.zeros((CHUNK, LANES), F32)
    for tile in range(width // LANES):
        lanes = slice(tile * LANES, (tile + 1) * LANES)
        values = activate(lanes)
        scaled = values * step_wide[:, lanes]
        end_x[:, lanes] = (scaled * end_wide[:, lanes]).astype(BF16)
        scaled_parts = [
            jnp.where(low_lanes, scaled, 0.0).astype(BF16),
            jnp.where(low_lanes, 0.0, scaled).astype(BF16),
        ]
        top, bottom = [], []
        for side_at in range(2):
            head = 2 * tile + side_at
            column = total[:, head : head + 1]
            row = total_rows[head : head + 1, :]
            top_col, low_col = column[:HALF], column[HALF:]
            top_row, low_row = row[:, :HALF], row[:, HALF:]
            top.append((inter_00 * jnp.exp2(jnp.minimum(top_col - top_row, 0.0))).astype(BF16))
            bottom.append((inter_10 * jnp.exp2(low_col - top_row)).astype(BF16))
            bottom.append((inter_11 * jnp.exp2(jnp.minimum(low_col - low_row, 0.0))).astype(BF16))
        local_top = dot(
            jnp.concatenate(top, axis=1),
            jnp.concatenate([scaled_parts[0][:HALF], scaled_parts[1][:HALF]], axis=0),
        )
        local_bottom = dot(
            jnp.concatenate(bottom, axis=1), jnp.concatenate(scaled_parts, axis=0)
        )
        local = jnp.concatenate([local_top, local_bottom], axis=0)
        y = local + from_state[:, lanes] * start_wide[:, lanes] + skip_ref[0:1, lanes] * values
        y_ref[0, :, lanes] = y.astype(BF16)
        z = z_ref[0, :, lanes].astype(F32)
        mixed = y * (z * sigmoid(z))
        squares = squares + mixed * mixed
        hidden[:, lanes] = (mixed * gain_ref[0:1, lanes]).astype(BF16)
    state[...] = kept_wide * state[...] + dot(b_f32.T.astype(BF16), end_x[...])
    joined[0:8, :] = joined[CHUNK : CHUNK + 8, :]
    part = dot(hidden[:, :half], out_own_ref[...]) + dot(hidden[:, half:], out_other_ref[...])
    part_ref[0] = part.astype(BF16)
    ones = jnp.ones((8, LANES), BF16)
    first, second = pieces(squares, 2)
    square_rows = dot_nt(ones, first) + dot_nt(ones, second)
    if with_grad:
        crossed = jnp.zeros((CHUNK, LANES), F32)
        for tile in range(part.shape[1] // LANES):
            lanes = slice(tile * LANES, (tile + 1) * LANES)
            crossed = crossed + part[:, lanes] * grad_ref[0, :, lanes].astype(F32)
        first, second = pieces(crossed, 2)
        cross_rows = dot_nt(ones, first) + dot_nt(ones, second)
        square_rows = jnp.where(iota((8, CHUNK), 0) == 0, square_rows, cross_rows)
    sums_ref[...] = square_rows


def backward_kernel(
    scalars,
    grad_ref,
    rows_ref,
    own_ref,
    other_ref,
    step_ref,
    out_own_ref,
    out_other_ref,
    taps_ref,
    gain_ref,
    skip_ref,
    head_ref,
    z_ref,
    conv_ref,
    input_ref,
    y_ref,
    raw_ref,
    state_ref,
    back_ref,
    own_grad_ref,
    other_grad_ref,
    step_grad_ref,
    hidden_ref,
    taps_grad_ref,
    wide_grad_ref,
    head_grad_ref,
    grad_state,
    grad_conv,
    grad_y,
    grad_y_low,
    step_wide,
    start_wide,
    end_wide,
    from_state,
    to_state,
    end_x,
    start_dy,
    sum_end,
    sum_start,
    sum_step,
    grad_inter,
):
    turn = pl.program_id(0)
    chunk = pl.num_programs(0) - 1 - turn
    side, first_end, second_end = scalars[0], scalars[1], scalars[2]
    base = chunk * CHUNK
    width = hidden_ref.shape[2]
    half = width // 2

    @pl.when(turn == 0)
    def _():
        grad_state[...] = jnp.zeros_like(grad_state)
        grad_conv[CHUNK:, :] = jnp.zeros((8, grad_conv.shape[1]), F32)
        taps_grad_ref[...] = jnp.zeros_like(taps_grad_ref)
        wide_grad_ref[...] = jnp.zeros_like(wide_grad_ref)
        head_grad_ref[...] = jnp.zeros_like(head_grad_ref)

    grad = grad_ref[0]
    grad_hidden = [dot_nt(grad, out_own_ref[...]), dot_nt(grad, out_other_ref[...])]
    columns = jnp.concatenate([rows_ref[...], jnp.zeros((LANES - 8, CHUNK), F32)], axis=0).T
    scale = jnp.broadcast_to(columns[:, 0:1], (CHUNK, LANES))
    inner = jnp.broadcast_to(columns[:, 1:2], (CHUNK, LANES))
    for tile in range(width // LANES):
        lanes = slice(tile * LANES, (tile + 1) * LANES)
        at = tile * LANES % half
        back = grad_hidden[tile * LANES // half][:, at : at + LANES]
        gain = gain_ref[0:1, lanes]
        z = z_ref[0, :, lanes].astype(F32)
        gate = sigmoid(z)
        gated = z * gate
        y = y_ref[0, :, lanes].astype(F32)
        mixed = y * gated
        scaled_mixed = mixed * scale
        hidden_ref[0, :, lanes] = (scaled_mixed * gain).astype(BF16)
        wide_grad_ref[0:1, lanes] += jnp.sum(back * scaled_mixed, axis=0, keepdims=True)
        grad_mixed = scale * (back * gain) - mixed * inner
        dy = grad_mixed * gated
        grad_y[:, lanes] = dy
        grad_y_low[:, lanes] = dy.astype(BF16)
        dz = (grad_mixed * y * (gate + gated * (1.0 - gate))).astype(BF16)
        if tile * LANES < half:
            own_grad_ref[0, :, at : at + LANES] = dz
        else:
            other_grad_ref[0, :, at : at + LANES] = dz

    pre, step, log_decay, total, start, ending, kept = decays(
        raw_ref[0], head_ref, base, first_end, second_end, chunk
    )
    expander = head_expander(width)
    step_wide[...] = spread(step, expander)
    start_wide[...] = spread(start, expander)
    end_wide[...] = spread(ending, expander)
    kept_wide = spread(jnp.broadcast_to(kept, (8, LANES)), expander)[0:1]
    total_rows = total.T

    def activated(lanes):
        conv = conv_ref[0, :, lanes].astype(F32)
        gate = sigmoid(conv)
        value = conv * gate
        return value, gate + value * (1.0 - gate)

    b_lanes, c_lanes = slice(width, width + STATE), slice(width + STATE, width + 2 * STATE)
    b_f32, b_slope = activated(b_lanes)
    c_f32, c_slope = activated(c_lanes)
    b_low, c_low = b_f32.astype(BF16), c_f32.astype(BF16)
    state_low = state_ref[0]
    grad_state_low = grad_state[...].astype(BF16)
    from_state[...] = dot(c_low, state_low)
    to_state[...] = dot(b_low, grad_state_low)
    inter = dot_nt(b_low, c_low)

    def same_pairs(row_at, col_at):
        same, row_ids, col_ids = same_block(base + row_at, base + col_at, first_end, second_end)
        if row_at == col_at:
            same = same & (row_ids <= col_ids)
        return same

    same_00, same_01, same_11 = same_pairs(0, 0), same_pairs(0, HALF), same_pairs(HALF, HALF)
    inter_00 = jnp.where(same_00, inter[:HALF, :HALF], 0.0)
    inter_01 = jnp.where(same_01, inter[:HALF, HALF:], 0.0)
    inter_11 = jnp.where(same_11, inter[HALF:, HALF:], 0.0)
    low_lanes = iota((CHUNK, LANES), 1) < 64
    lane_ids = iota((CHUNK, LANES), 1)
    row_ids = iota((LANES, CHUNK), 0)
    col_sums = jnp.zeros((CHUNK, LANES), F32)
    row_sum_list = []
    grad_inter[...] = jnp.zeros_like(grad_inter)
    for tile in range(width // LANES):
        lanes = slice(tile * LANES, (tile + 1) * LANES)
        values, slope = activated(lanes)
        scaled = values * step_wide[:, lanes]
        scaled_low = scaled.astype(BF16)
        dy = grad_y[:, lanes]
        dy_low = grad_y_low[:, lanes]
        top, bottom = [], []
        for side_at in range(2):
            head = 2 * tile + side_at
            picked = low_lanes if side_at == 0 else ~low_lanes
            lhs = jnp.where(picked, scaled, 0.0).astype(BF16)
            pair_grad = dot_nt(lhs, dy_low)
            column = total[:, head : head + 1]
            row = total_rows[head : head + 1, :]
            top_col, low_col = column[:HALF], column[HALF:]
            top_row, low_row = row[:, :HALF], row[:, HALF:]
            decay_00 = jnp.exp2(jnp.minimum(top_row - top_col, 0.0))
            decay_01 = jnp.exp2(low_row - top_col)
            decay_11 = jnp.exp2(jnp.minimum(low_row - low_col, 0.0))
            part_00 = pair_grad[:HALF, :HALF] * decay_00
            part_01 = pair_grad[:HALF, HALF:] * decay_01
            part_11 = pair_grad[HALF:, HALF:] * decay_11
            grad_inter[:HALF, :HALF] += part_00
            grad_inter[:HALF, HALF:] += part_01
            grad_inter[HALF:, HALF:] += part_11
            full_00, full_01, full_11 = part_00 * inter_00, part_01 * inter_01, part_11 * inter_11
            top.append((inter_00 * decay_00).astype(BF16))
            top.append((inter_01 * decay_01).astype(BF16))
            bottom.append((inter_11 * decay_11).astype(BF16))
            col_sum = jnp.concatenate(
                [
                    jnp.sum(full_00 + full_01, axis=1, keepdims=True),
                    jnp.sum(full_11, axis=1, keepdims=True),
                ],
                axis=0,
            )
            col_sums = jnp.where(lane_ids == head, col_sum, col_sums)
            row_sum_list.append(
                jnp.concatenate(
                    [
                        jnp.sum(full_00, axis=0, keepdims=True),
                        jnp.sum(full_01 + full_11, axis=0, keepdims=True),
                    ],
                    axis=1,
                )
            )
        dy_parts = [
            jnp.where(low_lanes, dy, 0.0).astype(BF16),
            jnp.where(low_lanes, 0.0, dy).astype(BF16),
        ]
        local_top = dot(jnp.concatenate(top, axis=1), jnp.concatenate(dy_parts, axis=0))
        local_bottom = dot(
            jnp.concatenate(bottom, axis=1),
            jnp.concatenate([dy_parts[0][HALF:], dy_parts[1][HALF:]], axis=0),
        )
        local = jnp.concatenate([local_top, local_bottom], axis=0)
        tail = end_wide[:, lanes]
        back_state = to_state[:, lanes]
        grad_scaled = local + tail * back_state
        ended = scaled * tail
        end_x[:, lanes] = ended.astype(BF16)
        sum_end[:, lanes] = (ended * back_state).astype(BF16)
        started = dy * start_wide[:, lanes]
        start_dy[:, lanes] = started.astype(BF16)
        sum_start[:, lanes] = (started * from_state[:, lanes]).astype(BF16)
        sum_step[:, lanes] = (grad_scaled * values).astype(BF16)
        grad_values = step_wide[:, lanes] * grad_scaled + skip_ref[0:1, lanes] * dy
        wide_grad_ref[1:2, lanes] += jnp.sum(dy * values, axis=0, keepdims=True)
        grad_conv[:CHUNK, lanes] = grad_values * slope

    grad_inter_00 = jnp.where(same_00, grad_inter[:HALF, :HALF], 0.0)
    grad_inter_01 = jnp.where(same_01, grad_inter[:HALF, HALF:], 0.0)
    grad_inter_11 = jnp.where(same_11, grad_inter[HALF:, HALF:], 0.0)
    pair_t = jnp.concatenate(
        [
            jnp.concatenate([grad_inter_00, grad_inter_01], axis=1),
            jnp.concatenate([jnp.zeros((HALF, HALF), F32), grad_inter_11], axis=1),
        ],
        axis=0,
    )
    grad_b = dot(pair_t.astype(BF16), c_low) + dot_nt(end_x[...], grad_state_low)
    grad_c = dot(pair_t.T.astype(BF16), b_low) + dot_nt(start_dy[...], state_low)
    grad_conv[:CHUNK, b_lanes] = grad_b * b_slope
    grad_conv[:CHUNK, c_lanes] = grad_c * c_slope

    folder = head_folder(width)
    end_sums = dot(sum_end[...], folder)
    start_sums = dot(sum_start[...], folder)
    step_sums = dot(sum_step[...], folder)
    state_pairs = jnp.sum(grad_state[...] * state_low.astype(F32), axis=0, keepdims=True)
    first, second = pieces(jnp.broadcast_to(state_pairs, (8, width)), 2)
    state_sums = (dot(first, folder) + dot(second, folder))[0:1] * kept
    row_sums = jnp.concatenate(
        row_sum_list + [jnp.zeros((LANES - len(row_sum_list), CHUNK), F32)], axis=0
    ).T
    grad_total = row_sums - col_sums + start_sums - end_sums
    last = state_sums + jnp.sum(end_sums, axis=0, keepdims=True)
    grad_total = grad_total + jnp.where(iota((CHUNK, LANES), 0) == CHUNK - 1, last, 0.0)
    grad_decay = dot_exact(upper_ones(), grad_total)
    grad_step = step_sums - grad_decay * head_ref[1:2, :]
    grad_raw = grad_step * sigmoid(pre)
    head_grad_ref[0:1, :] += jnp.sum(grad_raw, axis=0, keepdims=True)
    head_grad_ref[1:2, :] += jnp.sum(grad_decay * log_decay, axis=0, keepdims=True)
    step_grad_ref[0] = grad_raw.astype(BF16)
    grad_state[...] = kept_wide * grad_state[...] + dot(c_f32.T.astype(BF16), start_dy[...])

    rows = base + iota((CHUNK, LANES), 0)
    segment = segment_of(rows, first_end, second_end)
    masks = [
        (segment_of(rows + lag, first_end, second_end) == segment).astype(F32)
        for lag in range(1, 4)
    ]
    for tile in range((width + 2 * STATE) // LANES):
        lanes = slice(tile * LANES, (tile + 1) * LANES)
        inputs = input_ref[0, :, lanes].astype(F32)
        current = grad_conv[:CHUNK, lanes]
        found = taps_ref[3:4, lanes] * current
        taps_grad_ref[4:5, lanes] += jnp.sum(current, axis=0, keepdims=True)
        taps_grad_ref[3:4, lanes] += jnp.sum(current * inputs, axis=0, keepdims=True)
        for lag in range(1, 4):
            shifted = grad_conv[lag : lag + CHUNK, lanes] * masks[lag - 1]
            found = found + taps_ref[3 - lag : 4 - lag, lanes] * shifted
            taps_grad_ref[3 - lag : 4 - lag, lanes] += jnp.sum(
                shifted * inputs, axis=0, keepdims=True
            )
        found = found.astype(BF16)
        if tile * LANES < half:
            own_grad_ref[0, :, half + tile * LANES : half + (tile + 1) * LANES] = found
        elif tile * LANES < width:
            other_grad_ref[0, :, tile * LANES : (tile + 1) * LANES] = found
        elif tile * LANES == width:
            shared_b = found
        else:
            own_grad_ref[0, :, width:] = jnp.where(side == 0, shared_b, found)
            other_grad_ref[0, :, width:] = jnp.where(side == 0, found, shared_b)
    grad_conv[CHUNK:, :] = grad_conv[0:8, :]
    back_ref[0] = (
        dot_nt(own_grad_ref[0], own_ref[...])
        + dot_nt(other_grad_ref[0], other_ref[...])
        + dot_nt(step_grad_ref[0], step_ref[...])
    ).astype(BF16)


def whole(shape):
    return pl.BlockSpec(shape, lambda i, s: (0,) * len(shape))


def run_forward(scalars, slots, weights, grad_slots):
    own, other, step, out_own, out_other, taps, gain, skip, head = weights
    count, rows, depth = slots.shape
    width = gain.shape[1]
    joined = width + 2 * STATE

    def slot(cols, height=rows):
        return pl.BlockSpec((1, height, cols), lambda i, s: (i ^ s[3], 0, 0))

    inputs = [slots, own, other, step, out_own, out_other, taps, gain, skip, head]
    in_specs = [slot(depth)] + [whole(a.shape) for a in inputs[1:]]
    if grad_slots is not None:
        inputs.append(grad_slots)
        in_specs.append(slot(depth))
    return pl.pallas_call(
        forward_kernel,
        grid_spec=pltpu.PrefetchScalarGridSpec(
            num_scalar_prefetch=1,
            grid=(count,),
            in_specs=in_specs,
            out_specs=[
                slot(depth),
                pl.BlockSpec((8, CHUNK), lambda i, s: (0, i)),
                slot(width),
                slot(joined),
                slot(joined),
                slot(width),
                slot(LANES),
                slot(width, STATE),
            ],
            scratch_shapes=[
                pltpu.VMEM((CHUNK + 8, joined), F32),
                pltpu.VMEM((STATE, width), F32),
                pltpu.VMEM((CHUNK, width), BF16),
                pltpu.VMEM((CHUNK, width), BF16),
            ]
            + [pltpu.VMEM((CHUNK, width), F32)] * 4,
        ),
        out_shape=[
            jax.ShapeDtypeStruct((count, rows, depth), BF16),
            jax.ShapeDtypeStruct((8, count * rows), F32),
            jax.ShapeDtypeStruct((count, rows, width), BF16),
            jax.ShapeDtypeStruct((count, rows, joined), BF16),
            jax.ShapeDtypeStruct((count, rows, joined), BF16),
            jax.ShapeDtypeStruct((count, rows, width), BF16),
            jax.ShapeDtypeStruct((count, rows, LANES), F32),
            jax.ShapeDtypeStruct((count, STATE, width), BF16),
        ],
        compiler_params=pltpu.CompilerParams(vmem_limit_bytes=VMEM_LIMIT),
        name="forward_mixer",
    )(scalars, *inputs)


def run_backward(scalars, grad_slots, row_values, weights, kept):
    own, other, step, out_own, out_other, taps, gain, skip, head = weights
    count, rows, depth = grad_slots.shape
    width = gain.shape[1]
    joined = width + 2 * STATE
    final = count - 1

    def slot(cols, height=rows):
        return pl.BlockSpec((1, height, cols), lambda i, s: ((final - i) ^ s[3], 0, 0))

    z, conv, inputs, y, raw, states = kept
    constants = [own, other, step, out_own, out_other, taps, gain, skip, head]
    return pl.pallas_call(
        backward_kernel,
        grid_spec=pltpu.PrefetchScalarGridSpec(
            num_scalar_prefetch=1,
            grid=(count,),
            in_specs=[slot(depth), pl.BlockSpec((8, CHUNK), lambda i, s: (0, final - i))]
            + [whole(a.shape) for a in constants]
            + [slot(width), slot(joined), slot(joined), slot(width), slot(LANES)]
            + [slot(width, STATE)],
            out_specs=[
                slot(depth),
                slot(own.shape[1]),
                slot(own.shape[1]),
                slot(LANES),
                slot(width),
                whole((8, joined)),
                whole((8, width)),
                whole((8, LANES)),
            ],
            scratch_shapes=[
                pltpu.VMEM((STATE, width), F32),
                pltpu.VMEM((CHUNK + 8, joined), F32),
                pltpu.VMEM((CHUNK, width), F32),
                pltpu.VMEM((CHUNK, width), BF16),
            ]
            + [pltpu.VMEM((CHUNK, width), F32)] * 5
            + [pltpu.VMEM((CHUNK, width), BF16)] * 5
            + [pltpu.VMEM((CHUNK, CHUNK), F32)],
        ),
        out_shape=[
            jax.ShapeDtypeStruct((count, rows, depth), BF16),
            jax.ShapeDtypeStruct((count, rows, own.shape[1]), BF16),
            jax.ShapeDtypeStruct((count, rows, own.shape[1]), BF16),
            jax.ShapeDtypeStruct((count, rows, LANES), BF16),
            jax.ShapeDtypeStruct((count, rows, width), BF16),
            jax.ShapeDtypeStruct((8, joined), F32),
            jax.ShapeDtypeStruct((8, width), F32),
            jax.ShapeDtypeStruct((8, LANES), F32),
        ],
        compiler_params=pltpu.CompilerParams(vmem_limit_bytes=VMEM_LIMIT),
        name="backward_mixer",
    )(scalars, grad_slots, row_values, *constants, z, conv, inputs, y, raw, states)


def crossing(bit):
    return [(i, i ^ bit) for i in range(4)]


def exchange(block, bit):
    return lax.ppermute(block, "tensor", crossing(bit))


def swap_cores(block):
    return lax.ppermute(block, "pipe", [(0, 1), (1, 0)])


def gather_rows(block):
    cols = block.shape[1] // 2
    left, right = block[:, :cols], block[:, cols:]
    left_1 = exchange(left, 1)
    right_2 = exchange(right, 2)
    left_23 = exchange(jnp.stack([left, left_1]), 2)
    right_13 = exchange(jnp.stack([right, right_2]), 1)
    return jnp.stack(
        [
            block,
            jnp.concatenate([left_1, right_13[0]], axis=1),
            jnp.concatenate([left_23[0], right_2], axis=1),
            jnp.concatenate([left_23[1], right_13[1]], axis=1),
        ]
    )


def scatter_rows(slots):
    cols = slots.shape[2] // 2
    left, right = slots[:, :, :cols], slots[:, :, cols:]
    got_left = exchange(left[2:], 2)
    got_right = exchange(jnp.stack([right[1], right[3]]), 1)
    left_0 = left[0].astype(F32) + got_left[0].astype(F32)
    left_1 = left[1].astype(F32) + got_left[1].astype(F32)
    right_0 = right[0].astype(F32) + got_right[0].astype(F32)
    right_2 = right[2].astype(F32) + got_right[1].astype(F32)
    last_left = exchange(left_1.astype(BF16), 1)
    last_right = exchange(right_2.astype(BF16), 2)
    return jnp.concatenate(
        [left_0 + last_left.astype(F32), right_0 + last_right.astype(F32)], axis=1
    )


def sum_tensor(value):
    value = value + exchange(value, 1)
    return value + exchange(value, 2)


def rms_scale(x):
    return lax.rsqrt(jnp.mean(x * x, axis=1, keepdims=True) + NORM_EPSILON)


def shards(
    tokens,
    out_grad,
    seq_lengths,
    norm_gain,
    w_zx,
    w_bc,
    w_dt,
    conv_x,
    conv_bc,
    out_gain,
    head_params,
    out_weight,
):
    core = lax.axis_index("pipe")
    place = lax.axis_index("tensor")
    is_first = core == 0
    fsdp_count = lax.axis_size("fsdp")
    local_depth = norm_gain.shape[1]
    depth = local_depth * fsdp_count
    width = w_zx.shape[3]
    half = width // 2
    head_count = w_dt.shape[2]
    head_size = width // head_count
    local_head = conv_x.shape[3]
    inner_total = width * lax.axis_size("tensor")
    local_rows = tokens.shape[1]
    joined = width + 2 * STATE
    tap_rows = conv_x.shape[1]

    def by_core(first, second):
        return jnp.where(is_first, first, second)

    def local_order(value):
        size = value.shape[-1] // 2
        return by_core(
            value, jnp.concatenate([value[..., size:], value[..., :size]], axis=-1)
        )

    x_0 = lax.dynamic_index_in_dim(tokens, core, 0, keepdims=False).astype(F32)
    cotangent = lax.dynamic_index_in_dim(out_grad, core, 0, keepdims=False)
    lengths = lax.dynamic_index_in_dim(seq_lengths, core, 0, keepdims=False)[0]
    scalars = jnp.stack([core, lengths[0], lengths[0] + lengths[1], place]).astype(jnp.int32)

    def halves(which):
        at = which * half
        return jnp.concatenate(
            [
                lax.dynamic_slice_in_dim(w_zx[0, :, 0], at, half, 1),
                lax.dynamic_slice_in_dim(w_zx[0, :, 1], at, half, 1),
                lax.dynamic_slice_in_dim(w_bc[0], which * STATE, STATE, 1),
            ],
            axis=1,
        )

    mine, theirs = halves(core), swap_cores(halves(1 - core))
    mine_out = lax.dynamic_slice_in_dim(out_weight[0], core * half, half, 0)
    theirs_out = swap_cores(lax.dynamic_slice_in_dim(out_weight[0], (1 - core) * half, half, 0))

    small = [norm_gain[0], w_dt[0], conv_x[0], conv_bc[0], out_gain[0]]
    packed = jnp.concatenate([a.reshape(-1) for a in small])
    small_size = packed.shape[0]
    packed = jnp.pad(packed, (0, -small_size % 2048)).reshape(16, -1)
    small_own = lax.all_gather(packed, "fsdp", axis=0, tiled=False)
    small_swapped = swap_cores(small_own)
    heads_own = jnp.pad(head_params[0], ((0, 5), (0, LANES - head_count)))
    heads_swapped = swap_cores(heads_own)

    def section_weights(section):
        def pick(own, swapped):
            return by_core(own, swapped) if section == 0 else by_core(swapped, own)

        flat = pick(small_own, small_swapped).reshape(fsdp_count, -1)
        at = 0
        arrays = []
        for array in small:
            arrays.append(flat[:, at : at + array.size].reshape((fsdp_count,) + array.shape))
            at += array.size
        gain_parts, step_parts, conv_parts, shared_parts, scale_parts = arrays
        gain_vec = gain_parts.reshape(1, depth).astype(F32)
        step_full = jnp.pad(
            local_order(step_parts.reshape(depth, head_count)),
            ((0, 0), (0, LANES - head_count)),
        )
        conv_full = local_order(
            jnp.moveaxis(conv_parts, 0, 2).reshape(tap_rows, width).astype(F32)
        )
        shared_full = jnp.moveaxis(shared_parts, 0, 1).reshape(tap_rows, 2 * STATE).astype(F32)
        taps = jnp.pad(
            jnp.concatenate([conv_full, shared_full], axis=1), ((0, 8 - tap_rows), (0, 0))
        )
        scale = local_order(jnp.moveaxis(scale_parts, 0, 1).reshape(1, width).astype(F32))
        heads = pick(heads_own, heads_swapped)[:3, :head_count]
        heads = local_order(heads)
        skip = jnp.repeat(heads[2], head_size).reshape(1, width)
        head_rows = jnp.pad(
            jnp.stack([heads[0], jnp.exp(heads[1])]), ((0, 6), (0, LANES - head_count))
        )
        own = lax.all_gather(pick(mine, theirs), "fsdp", axis=0, tiled=True)
        out_own = lax.all_gather(pick(mine_out, theirs_out), "fsdp", axis=1, tiled=True)
        other = swap_cores(own)
        out_other = swap_cores(out_own)
        return gain_vec, (own, other, step_full, out_own, out_other, taps, scale, skip, head_rows)

    sections = [section_weights(0), section_weights(1)]

    cotangent_slots = gather_rows(cotangent)

    x = x_0
    saved = []
    results = []
    for section in range(2):
        gain_vec, weights = sections[section]
        normed = (x * rms_scale(x) * gain_vec).astype(BF16)
        slots = gather_rows(normed)
        part, sums, *kept = run_forward(
            scalars, slots, weights, cotangent_slots if section == 1 else None
        )
        sums = sum_tensor(sums[:2])
        scale_rows = lax.rsqrt(sums[0] / inner_total + NORM_EPSILON)
        own_scale = lax.dynamic_slice_in_dim(scale_rows, place * local_rows, local_rows, 0)
        summed = scatter_rows(part)
        y = x + summed * own_scale[:, None]
        saved.append((x, slots, kept, scale_rows, sums[1], summed))
        x_low = y.astype(BF16)
        results.append(x_low)
        x = x_low.astype(F32)

    def add_cores(own_part, other_part):
        got = swap_cores(other_part.astype(BF16))
        return (own_part + got.astype(F32)).astype(BF16)

    grad_low = cotangent
    grad_slots = cotangent_slots
    grads_x = [None, None]
    reduced = [None, None]
    for section in (1, 0):
        gain_vec, weights = sections[section]
        x, slots, kept, scale_rows, crossed, summed = saved[section]
        if section == 0:
            grad_slots = gather_rows(grad_low)
            own_cross = jnp.sum(grad_low.astype(F32) * summed, axis=1)
            crossed = lax.all_gather(own_cross, "tensor", axis=0, tiled=True)
        inner = scale_rows * scale_rows * scale_rows * crossed / inner_total
        row_values = jnp.pad(jnp.stack([scale_rows, inner]), ((0, 6), (0, 0)))
        back, own_grad, other_grad, step_grad, hidden, taps_grad, wide_grad, head_grad = (
            run_backward(scalars, grad_slots, row_values, weights, kept)
        )
        dnormed = scatter_rows(back)
        scale = rms_scale(x)
        weighted = dnormed * gain_vec
        dx = (
            grad_low.astype(F32)
            + weighted * scale
            - x * (scale * scale * scale * jnp.mean(weighted * x, axis=1, keepdims=True))
        )
        gain_grad = jnp.sum(dnormed * (x * scale), axis=0)
        all_rows = slots.shape[0] * slots.shape[1]
        flat_slots = slots.reshape(all_rows, depth)
        flat_grads = grad_slots.reshape(all_rows, depth)
        flat_hidden = hidden.reshape(all_rows, width)
        out_sum = add_cores(
            dot_tn(flat_hidden[:, :half], flat_grads), dot_tn(flat_hidden[:, half:], flat_grads)
        )
        out_reduced = lax.psum_scatter(out_sum, "fsdp", scatter_dimension=1, tiled=True)
        in_sum = add_cores(
            dot_tn(flat_slots, own_grad.reshape(all_rows, -1)),
            dot_tn(flat_slots, other_grad.reshape(all_rows, -1)),
        )
        in_reduced = lax.psum_scatter(in_sum, "fsdp", scatter_dimension=0, tiled=True)
        step_sum = local_order(
            dot_tn(flat_slots, step_grad.reshape(all_rows, LANES))[:, :head_count]
        )
        head_sum = local_order(
            jnp.concatenate(
                [
                    head_grad[:2, :head_count],
                    jnp.sum(wide_grad[1].reshape(head_count, head_size), axis=1)[None],
                ]
            )
        )
        split_small = [
            step_sum,
            local_order(taps_grad[:tap_rows, :width]),
            local_order(wide_grad[0:1]),
            head_sum,
        ]
        shared_small = [gain_grad, taps_grad[:tap_rows, width:]]
        split_sum = lax.psum(
            jnp.concatenate([a.reshape(-1) for a in split_small]), ("pipe", "fsdp")
        )
        shared_sum = lax.psum(
            jnp.concatenate([a.reshape(-1) for a in shared_small]), ("pipe", "fsdp", "tensor")
        )
        reduced[section] = (out_reduced, in_reduced, split_sum, shared_sum)
        grad_low = dx.astype(BF16)
        grads_x[section] = grad_low

    def both_micros(first, second):
        keep, send = by_core(first, second), by_core(second, first)
        got = swap_cores(send)
        return jnp.stack([by_core(keep, got), by_core(got, keep)])[None]

    section_out = both_micros(results[0], results[1])
    input_out = both_micros(grads_x[0], grads_x[1])

    def both_halves(first, second):
        keep, send = by_core(first, second), by_core(second, first)
        got = swap_cores(send)
        return by_core(keep, got), by_core(got, keep)

    out_low, out_high = both_halves(reduced[0][0], reduced[1][0])
    grad_out_weight = jnp.concatenate([out_low, out_high], axis=0).astype(F32)
    in_low, in_high = both_halves(reduced[0][1], reduced[1][1])
    grad_zx = jnp.stack(
        [
            jnp.concatenate([in_low[:, :half], in_high[:, :half]], axis=1),
            jnp.concatenate([in_low[:, half:width], in_high[:, half:width]], axis=1),
        ],
        axis=1,
    ).astype(F32)
    grad_bc = lax.psum_scatter(
        jnp.concatenate([in_low[:, width:], in_high[:, width:]], axis=1).astype(F32),
        "tensor",
        scatter_dimension=0,
        tiled=True,
    )
    flat = by_core(reduced[0][2], reduced[1][2])
    sizes = [depth * head_count, tap_rows * width, width]
    fsdp_at = lax.axis_index("fsdp")
    grad_dt = lax.dynamic_slice_in_dim(
        flat[: sizes[0]].reshape(depth, head_count), fsdp_at * local_depth, local_depth, 0
    )
    at = sizes[0]
    grad_conv = lax.dynamic_slice_in_dim(
        flat[at : at + sizes[1]].reshape(tap_rows, head_count, head_size),
        fsdp_at * local_head,
        local_head,
        2,
    )
    at += sizes[1]
    grad_scale = lax.dynamic_slice_in_dim(
        flat[at : at + sizes[2]].reshape(head_count, head_size),
        fsdp_at * local_head,
        local_head,
        1,
    )
    at += sizes[2]
    grad_heads = flat[at:].reshape(3, head_count)
    flat = by_core(reduced[0][3], reduced[1][3])
    all_at = fsdp_at * lax.axis_size("tensor") + place
    piece = depth // (fsdp_count * lax.axis_size("tensor"))
    grad_gain = lax.dynamic_slice_in_dim(flat[:depth], all_at * piece, piece, 0)
    piece = 2 * STATE // (fsdp_count * lax.axis_size("tensor"))
    grad_shared = lax.dynamic_slice_in_dim(
        flat[depth:].reshape(tap_rows, 2 * STATE), all_at * piece, piece, 1
    )
    return (
        section_out,
        input_out,
        grad_gain[None],
        grad_zx[None],
        grad_bc[None],
        grad_dt[None],
        grad_conv[None],
        grad_shared[None],
        grad_scale[None],
        grad_heads[None],
        grad_out_weight[None],
    )


def solution(mesh):
    return jax.shard_map(
        shards,
        mesh=mesh,
        in_specs=(
            P(None, ("fsdp", "tensor"), None),
            P(None, ("fsdp", "tensor"), None),
            P(None, "fsdp", None),
            P("pipe", "fsdp"),
            P("pipe", "fsdp", None, "tensor"),
            P("pipe", "fsdp", None),
            P("pipe", "fsdp", "tensor"),
            P("pipe", None, "tensor", "fsdp"),
            P("pipe", None, "fsdp"),
            P("pipe", "tensor", "fsdp"),
            P("pipe", None, "tensor"),
            P("pipe", "tensor", "fsdp"),
        ),
        out_specs=(
            P("pipe", None, ("fsdp", "tensor"), None),
            P("pipe", None, ("fsdp", "tensor"), None),
            P("pipe", ("fsdp", "tensor")),
            P("pipe", "fsdp", None, "tensor"),
            P("pipe", ("fsdp", "tensor"), None),
            P("pipe", "fsdp", "tensor"),
            P("pipe", None, "tensor", "fsdp"),
            P("pipe", None, ("fsdp", "tensor")),
            P("pipe", "tensor", "fsdp"),
            P("pipe", None, "tensor"),
            P("pipe", "tensor", "fsdp"),
        ),
        check_vma=False,
    )
```

time: 3080 us -> 744 us (0.24)
  local copies, waits for them, and re-layouts: 1080 us -> 100 us
  matrix products: 630 us -> 37.4 us
  waiting for transfers between devices: 746 us -> 243 us
  other arithmetic: 305 us -> 93.1 us
  blocking collectives: 201 us -> 65.7 us
  Pallas kernels: 0 us -> 133 us
  loops' own time: 51.3 us -> 0 us
  starting transfers between devices: 7.78 us -> 43.2 us
    dynamic_update_slice x108 -> x0, local copies, waits for them, and re-layouts: 692 us -> none  [mixer_local(): lax.scan(jax.checkpoint(block_step), start_carry, block_items)]
    dot_general x282 -> x10, matrix products: 630 us -> 37.4 us  [dot_tn(): lax.dot_general(a, b, (((0,), (0,)), ((), ())), preferred_element_type=F32)]
    unnamed x28 -> x12, waiting for transfers between devices: 354 us -> 0.17 us
    reduce_scatter x6 -> x3, waiting for transfers between devices: 264 us -> 91.6 us  [the longest x2 71.8 us: shards(): lax.psum_scatter(in_sum, 'fsdp', scatter_dimension=0, tiled=True)]
    pallas_call x0 -> x4, Pallas kernels: none -> 133 us  [the longest x2 79.9 us: run_backward(): pl.pallas_call(backward_kernel, grid_spec=pltpu.PrefetchScalarGridSpec(nu...]
    ppermute x4 -> x52, waiting for transfers between devices: 3.69 us -> 114 us  [the longest x36 114 us: exchange(): return lax.ppermute(block, 'tensor', crossing(bit))]
    mul x103 -> x2, other arithmetic: 96.4 us -> 0.02 us  [shards(): scale * scale * scale * jnp.mean(weighted * x, axis=1, keepdims=True)]
    reduce_sum x54 -> x7, other arithmetic: 98.9 us -> 3.82 us  [the longest x2 1.71 us: shards(): gain_grad = jnp.sum(dnormed * (x * scale), axis=0)]
  transfers between devices with their start and end apart: 25 -> 62, of which waited for: 16 -> 30; matrix products, arithmetic and copies ran while one was open for 27% -> 29% of each run, Pallas kernels for 0% -> 9%
where the time goes in v1:
time: 744 us; the launch traced here: 733 us
  waiting for transfers between devices  243 us (33%)
  Pallas kernels  133 us (18%)
  local copies, waits for them, and re-layouts  100 us (13%)
  other arithmetic  93.1 us (13%)
  blocking collectives  65.7 us (9%)
  starting transfers between devices  43.2 us (6%)
  matrix products  37.4 us (5%)
  between operations  17.2 us (2%)
    ppermute x36, waiting for transfers between devices, exchange(): return lax.ppermute(block, 'tensor', crossing(bit))  114 us
    pallas_call x2, Pallas kernels, run_backward(): pl.pallas_call(backward_kernel, grid_spec=pltpu.PrefetchScalarGridSpec(nu...  79.9 us
    reduce_scatter x2, waiting for transfers between devices, shards(): lax.psum_scatter(in_sum, 'fsdp', scatter_dimension=0, tiled=True)  71.8 us
    pallas_call x2, Pallas kernels, run_forward(): pl.pallas_call(forward_kernel, grid_spec=pltpu.PrefetchScalarGridSpec(num...  52.9 us
    psum x1, blocking collectives, shards(): lax.psum(jnp.concatenate([a.reshape(-1) for a in shared_small]), ('pipe',...  43.6 us
    ppermute x36, starting transfers between devices, exchange(): return lax.ppermute(block, 'tensor', crossing(bit))  39.7 us
    dot_general x10, matrix products, dot_tn(): lax.dot_general(a, b, (((0,), (0,)), ((), ())), preferred_element_type=F32)  37.4 us
    all_gather x2, waiting for transfers between devices, section_weights(): own = lax.all_gather(pick(mine, theirs), 'fsdp', axis=0, tiled=True)  30.9 us
  transfers between devices with their start and end apart: 62, of which 30 were waited for; matrix products, arithmetic and copies ran while one was open for 29% of the time, Pallas kernels for 9%

profile of v1, /device:TPU:0, one launch (start us, length us, event | category | flops | bytes accessed | tf_op | source)
XLA Modules:
  0.0 732.5 jit_solution(9761946355885220464)
XLA Ops:
  11.4 15.6 %all_gather.18 = bf16[4,16,512]{2,1,0:T(8,128)(2,1)} all-gather(bf16[1,16,512]{2,1,0:T(8,128)(2,1)S(1)} %all_gather_reshape.3), channel_id=1, replica_groups=mesh['pipe'=2,'fsdp'=4,'tensor'=4] {'fsdp'}, dimensions={0}, use_global_device_ids=true | all-gather | bytes 81920 | tf_op jit(solution)/shard_map/all_gather | solution.py:766
  27.1 3.8 fusion.70
  51.1 2.5 broadcast_select_fusion.8
  76.1 2.2 maximum_select_fusion.1
  78.9 30.9 %all-gather.6.cloned.1.call-done.own_ref = bf16[1536,896]{1,0:T(8,128)(2,1)} async-done(((bf16[384,896]{1,0:T(8,128)(2,1)}), bf16[1536,896]{1,0:T(8,128)(2,1)}) %all-gather.6.cloned.1.call-update) | async-done | bytes 2752528 | tf_op jit(solution)/shard_map/all_gather | solution.py:801
  134.3 5.9 all-gather.8.cloned.1.call-done.out_own_ref
  147.0 26.3 %forward_mixer.2 = (bf16[4,256,1536]{2,1,0:T(8,128)(2,1)}, f32[8,1024]{1,0:T(8,128)}, bf16[4,256,768]{2,1,0:T(8,128)(2,1)}, bf16[4,256,1024]{2,1,0:T(8,128)(2,1)...) custom-call(s32[4]{0:T(128)} %pad_add_fusion.scalars, ...), custom_call_target="tpu_custom_call" | custom-call | tf_op jit(solution)/shard_map/forward_mixer/pallas_call | solution.py:554
  184.7 12.2 %collective-permute-done.14 = f32[2,1024]{1,0:T(2,128)S(1)} collective-permute-done((f32[2,1024]{1,0:T(2,128)S(1)}, f32[2,1024]{1,0:T(2,128)S(1)}, u32[]{:S(2)}, u32[]{:S(2)}) %collective-permute-start.14) | collective-permute-done | bytes 8224 | tf_op jit(solution)/shard_map/ppermute | solution.py:654
  202.8 5.9 collective-permute-done.11
  219.7 3.5 collective-permute-done.17
  223.2 2.2 pad_maximum_fusion.10
  232.8 9.5 %collective-permute-done.18 = bf16[2,256,768]{2,1,0:T(8,128)(2,1)} collective-permute-done((bf16[2,256,768]{2,1,0:T(8,128)(2,1)}, bf16[2,256,768]{2,1,0:T(8,128)(2,1)}, u32[]{:S(2)}, u32[]{:S(2)}) %collective-permute-start.18) | collective-permute-done | bytes 786464 | tf_op jit(solution)/shard_map/ppermute | solution.py:654
  243.4 2.2 collective-permute-done.19
  251.8 26.7 %forward_mixer.3 = (bf16[4,256,1536]{2,1,0:T(8,128)(2,1)}, f32[8,1024]{1,0:T(8,128)}, bf16[4,256,768]{2,1,0:T(8,128)(2,1)}, bf16[4,256,1024]{2,1,0:T(8,128)(2,1)...) custom-call(s32[4]{0:T(128)} %pad_add_fusion.scalars, ...), custom_call_target="tpu_custom_call" | custom-call | tf_op jit(solution)/shard_map/forward_mixer/pallas_call | solution.py:554
  279.6 3.3 collective-permute-done.30
  284.4 3.0 collective-permute-done.31
  288.6 39.9 %backward_mixer.2 = (bf16[4,256,1536]{2,1,0:T(8,128)(2,1)}, bf16[4,256,896]{2,1,0:T(8,128)(2,1)}, bf16[4,256,896]{2,1,0:T(8,128)(2,1)}, bf16[4,256,128]{2,1,0:T(...) custom-call(s32[4]{0:T(128)} %pad_add_fusion.scalars, ...), custom_call_target="tpu_custom_call" | custom-call | tf_op jit(solution)/shard_map/backward_mixer/pallas_call | solution.py:605
  334.6 13.9 %collective-permute-done.33 = bf16[2,256,768]{2,1,0:T(8,128)(2,1)S(1)} collective-permute-done((bf16[2,256,768]{2,1,0:T(8,128)(2,1)S(1)}, bf16[2,256,768]{2,1,0:T(8,128)(2,1)S(1)}, u32[]{:S(2)}, u32[]{:S(2)}) %collective-permute-start.33) | collective-permute-done | bytes 786464 | tf_op jit(solution)/shard_map/ppermute | solution.py:654
  351.3 2.5 convolution_convert_fusion
  353.8 3.2 collective-permute-done.34
  365.4 2.6 collective-permute-start.37
  369.9 2.1 copy.162
  372.0 2.1 copy.136
  376.7 6.5 all-gather
  390.7 12.2 %collective-permute-done.39 = bf16[2,256,768]{2,1,0:T(8,128)(2,1)S(1)} collective-permute-done((bf16[2,256,768]{2,1,0:T(8,128)(2,1)S(1)}, bf16[2,256,768]{2,1,0:T(8,128)(2,1)S(1)}, u32[]{:S(2)}, u32[]{:S(2)}) %collective-permute-start.39) | collective-permute-done | bytes 786464 | tf_op jit(solution)/shard_map/ppermute | solution.py:654
  403.0 2.6 collective-permute-done.40
  407.7 2.3 pad_maximum_fusion.3.grad_ref
  410.0 40.0 %backward_mixer.3 = (bf16[4,256,1536]{2,1,0:T(8,128)(2,1)}, bf16[4,256,896]{2,1,0:T(8,128)(2,1)}, bf16[4,256,896]{2,1,0:T(8,128)(2,1)}, bf16[4,256,128]{2,1,0:T(...) custom-call(s32[4]{0:T(128)} %pad_add_fusion.scalars, ...), custom_call_target="tpu_custom_call" | custom-call | tf_op jit(solution)/shard_map/backward_mixer/pallas_call | solution.py:605
  456.6 2.7 broadcast_select_fusion.10
  464.8 4.0 fusion.3
  468.7 2.7 copy.152
  471.5 2.7 convolution_convert_fusion.1
  474.3 4.8 bitcast_convert_fusion
  479.6 2.4 fusion.2
  482.1 2.4 copy.150
  484.7 8.4 %fusion = bf16[1536,896]{1,0:T(8,128)(2,1)} fusion(bf16[1536,896]{1,0:T(8,128)(2,1)} %collective-permute-done.47, bf16[4,256,1536]{2,1,0:T(8,128)(2,1)} %pad_maximum_fusion.1.x_ref, bf16[4,256,896]{2,1,0:T(8,128)(2,1)} %get-tuple-element.65), kind=kOutput, calls=%fused_computation.2 | convolution fusion | flops 2822701056 | bytes 10485760 | tf_op jit(solution)/shard_map/dot_general | solution.py:28
  493.2 5.4 bitcast_convert_fusion.1
  502.1 16.7 %collective-permute-done.26 = bf16[2,256,768]{2,1,0:T(8,128)(2,1)S(1)} collective-permute-done((bf16[2,256,768]{2,1,0:T(8,128)(2,1)S(1)}, bf16[2,256,768]{2,1,0:T(8,128)(2,1)S(1)}, u32[]{:S(2)}, u32[]{:S(2)}) %collective-permute-start.26) | collective-permute-done | bytes 786464 | tf_op jit(solution)/shard_map/ppermute | solution.py:654
  522.1 4.9 fusion.1
  527.4 3.6 collective-permute-done.27
  544.8 12.0 %collective-permute-done.41 = bf16[2,256,768]{2,1,0:T(8,128)(2,1)} collective-permute-done((bf16[2,256,768]{2,1,0:T(8,128)(2,1)}, bf16[2,256,768]{2,1,0:T(8,128)(2,1)}, u32[]{:S(2)}, u32[]{:S(2)}) %collective-permute-start.41) | collective-permute-done | bytes 786464 | tf_op jit(solution)/shard_map/ppermute | solution.py:654
  556.7 2.5 collective-permute-done.43
  559.3 2.3 fusion.47
  577.0 43.6 %all-reduce.10 = (f32[2816]{0:T(1024)S(1)}, f32[2816]{0:T(1024)S(1)}) all-reduce(f32[2816]{0:T(1024)S(1)} %get-tuple-element.280, f32[2816]{0:T(1024)S(1)} %get-tuple-element.281), channel_id=1, replica_groups=mesh['pipe'=2,'fsdp'=4,'tensor'=4] {'pipe','fsdp','tensor'}, use_global_device_ids=true, to_apply=%region_6.7 | all-reduce | flops 5632 | bytes 45056 | tf_op jit(solution)/shard_map/psum | solution.py:894
  623.1 15.2 %reduce-scatter.12.cloned.1.call-done = bf16[384,896]{1,0:T(8,128)(2,1)} async-done(((bf16[1536,896]{1,0:T(8,128)(2,1)}), bf16[384,896]{1,0:T(8,128)(2,1)}) %reduce-scatter.12.cloned.1.call-update) | async-done | bytes 688144 | tf_op jit(solution)/shard_map/reduce_scatter | solution.py:872
  638.4 56.6 %reduce-scatter.10.cloned.1.call-done = bf16[384,896]{1,0:T(8,128)(2,1)} async-done(((bf16[1536,896]{1,0:T(8,128)(2,1)}), bf16[384,896]{1,0:T(8,128)(2,1)}) %reduce-scatter.10.cloned.1.call-update) | async-done | bytes 688144 | tf_op jit(solution)/shard_map/reduce_scatter | solution.py:872
  702.5 3.2 copy.138
  705.7 19.7 %reduce-scatter.14.cloned.1.call-done = f32[96,256]{1,0:T(8,128)} async-done(((f32[384,256]{1,0:T(8,128)}), f32[96,256]{1,0:T(8,128)}) %reduce-scatter.14.cloned.1.call-update) | async-done | bytes 98320 | tf_op jit(solution)/shard_map/reduce_scatter | solution.py:924
  (545 shorter events, 214.2 us)
Async XLA Ops:
  7.2 102.6 %all-gather.6.cloned.1.call-start = ((), (), s32[]{:S(2)}) async-start(), calls=%async_computation.5 | async-start | bytes 3440640 | tf_op jit(solution)/shard_map/all_gather | solution.py:801
  27.1 27.8 %collective-permute-start = (bf16[4,16,512]{2,1,0:T(8,128)(2,1)}, bf16[4,16,512]{2,1,0:T(8,128)(2,1)}, u32[]{:S(2)}, u32[]{:S(2)}) collective-permute-start(bf16[4,16,512]{2,1,0:T(8,128)(2,1)} %all_gather.18), channel_id=1, source_target_pairs={{0,16},{16,0},{1,17},{17,1},{2,18},{18,2},{3,19},{19,3},{4,20},{20... | collective-permute-start | bytes 196616 | tf_op jit(solution)/shard_map/ppermute | solution.py:658
  36.6 14.5 %collective-permute-start.5 = (bf16[384,896]{1,0:T(8,128)(2,1)}, bf16[384,896]{1,0:T(8,128)(2,1)}, u32[]{:S(2)}, u32[]{:S(2)}) collective-permute-start(bf16[384,896]{1,0:T(8,128)(2,1)} %pad_maximum_fusion.20), channel_id=1, source_target_pairs={{0,16},{16,0},{1,17},{17,1},{2,18},{18,2},{3,19},{19,3},{4,20},{20... | collective-permute-start | bytes 2064392 | tf_op jit(solution)/shard_map/ppermute | solution.py:658
  37.8 25.8 %collective-permute-start.7 = (bf16[384,384]{1,0:T(8,128)(2,1)}, bf16[384,384]{1,0:T(8,128)(2,1)}, u32[]{:S(2)}, u32[]{:S(2)}) collective-permute-start(bf16[384,384]{1,0:T(8,128)(2,1)} %dynamic-slice_bitcast_fusion), channel_id=1, source_target_pairs={{0,16},{16,0},{1,17},{17,1},{2,18},{18,2},{3,19},{19,3},{4,20},{20... | collective-permute-start | bytes 884744 | tf_op jit(solution)/shard_map/ppermute | solution.py:658
  39.6 86.2 %collective-permute-start.23 = (bf16[256,768]{1,0:T(8,128)(2,1)}, bf16[256,768]{1,0:T(8,128)(2,1)}, u32[]{:S(2)}, u32[]{:S(2)}) collective-permute-start(bf16[256,768]{1,0:T(8,128)(2,1)} %get-tuple-element.212), channel_id=1, source_target_pairs={{0,2},{1,3},{2,0},{3,1},{4,6},{5,7},{6,4},{7,5},{8,10},{9,11},{10,... | collective-permute-start | bytes 1179656 | tf_op jit(solution)/shard_map/ppermute | solution.py:654
  47.7 80.6 %collective-permute-start.22 = (bf16[256,768]{1,0:T(8,128)(2,1)}, bf16[256,768]{1,0:T(8,128)(2,1)}, u32[]{:S(2)}, u32[]{:S(2)}) collective-permute-start(bf16[256,768]{1,0:T(8,128)(2,1)} %get-tuple-element.213), channel_id=1, source_target_pairs={{0,1},{1,0},{2,3},{3,2},{4,5},{5,4},{6,7},{7,6},{8,9},{9,8},{10,11... | collective-permute-start | bytes 1179656 | tf_op jit(solution)/shard_map/ppermute | solution.py:654
  53.5 86.7 %all-gather.8.cloned.1.call-start = ((), (), s32[]{:S(2)}) async-start(), calls=%async_computation.6 | async-start | bytes 1474560 | tf_op jit(solution)/shard_map/all_gather | solution.py:802
  57.3 52.5 %collective-permute-start.2 = (bf16[256,768]{1,0:T(8,128)(2,1)}, bf16[256,768]{1,0:T(8,128)(2,1)}, u32[]{:S(2)}, u32[]{:S(2)}) collective-permute-start(bf16[256,768]{1,0:T(8,128)(2,1)} %get-tuple-element.228), channel_id=1, source_target_pairs={{0,2},{1,3},{2,0},{3,1},{4,6},{5,7},{6,4},{7,5},{8,10},{9,11},{10,... | collective-permute-start | bytes 1179656 | tf_op jit(solution)/shard_map/ppermute | solution.py:654
  61.9 56.1 %collective-permute-start.1 = (bf16[256,768]{1,0:T(8,128)(2,1)}, bf16[256,768]{1,0:T(8,128)(2,1)}, u32[]{:S(2)}, u32[]{:S(2)}) collective-permute-start(bf16[256,768]{1,0:T(8,128)(2,1)} %get-tuple-element.229), channel_id=1, source_target_pairs={{0,1},{1,0},{2,3},{3,2},{4,5},{5,4},{6,7},{7,6},{8,9},{9,8},{10,11... | collective-permute-start | bytes 1179656 | tf_op jit(solution)/shard_map/ppermute | solution.py:654
  65.7 154.1 %all-gather.10.cloned.1.call-start = ((), (), s32[]{:S(2)}) async-start(), calls=%async_computation.7 | async-start | bytes 3440640 | tf_op jit(solution)/shard_map/all_gather | solution.py:801
  75.8 155.6 %all-gather.12.cloned.1.call-start = ((), (), s32[]{:S(2)}) async-start(), calls=%async_computation.8 | async-start | bytes 1474560 | tf_op jit(solution)/shard_map/all_gather | solution.py:802
  109.8 36.2 %collective-permute-start.6 = (bf16[1536,896]{1,0:T(8,128)(2,1)}, bf16[1536,896]{1,0:T(8,128)(2,1)}, u32[]{:S(2)}, u32[]{:S(2)}) collective-permute-start(bf16[1536,896]{1,0:T(8,128)(2,1)} %all-gather.6.cloned.1.call-done.own_ref), channel_id=1, source_target_pairs={{0,16},{16,0},{1,17},{17,1},{2,18},{18,2},{3,19},{19,3},{4,20},{20... | collective-permute-start | bytes 8257544 | tf_op jit(solution)/shard_map/ppermute | solution.py:658
  111.8 20.7 %collective-permute-start.3 = (bf16[2,256,768]{2,1,0:T(8,128)(2,1)}, bf16[2,256,768]{2,1,0:T(8,128)(2,1)}, u32[]{:S(2)}, u32[]{:S(2)}) collective-permute-start(bf16[2,256,768]{2,1,0:T(8,128)(2,1)} %pad_maximum_fusion.7), channel_id=1, source_target_pairs={{0,1},{1,0},{2,3},{3,2},{4,5},{5,4},{6,7},{7,6},{8,9},{9,8},{10,11... | collective-permute-start | bytes 2359304 | tf_op jit(solution)/shard_map/ppermute | solution.py:654
  120.0 20.7 %collective-permute-start.4 = (bf16[2,256,768]{2,1,0:T(8,128)(2,1)}, bf16[2,256,768]{2,1,0:T(8,128)(2,1)}, u32[]{:S(2)}, u32[]{:S(2)}) collective-permute-start(bf16[2,256,768]{2,1,0:T(8,128)(2,1)} %pad_maximum_fusion.8), channel_id=1, source_target_pairs={{0,2},{1,3},{2,0},{3,1},{4,6},{5,7},{6,4},{7,5},{8,10},{9,11},{10,... | collective-permute-start | bytes 2359304 | tf_op jit(solution)/shard_map/ppermute | solution.py:654
  127.7 53.5 %collective-permute-start.24 = (bf16[2,256,768]{2,1,0:T(8,128)(2,1)}, bf16[2,256,768]{2,1,0:T(8,128)(2,1)}, u32[]{:S(2)}, u32[]{:S(2)}) collective-permute-start(bf16[2,256,768]{2,1,0:T(8,128)(2,1)} %pad_maximum_fusion.12), channel_id=1, source_target_pairs={{0,1},{1,0},{2,3},{3,2},{4,5},{5,4},{6,7},{7,6},{8,9},{9,8},{10,11... | collective-permute-start | bytes 2359304 | tf_op jit(solution)/shard_map/ppermute | solution.py:654
  130.2 53.3 %collective-permute-start.25 = (bf16[2,256,768]{2,1,0:T(8,128)(2,1)}, bf16[2,256,768]{2,1,0:T(8,128)(2,1)}, u32[]{:S(2)}, u32[]{:S(2)}) collective-permute-start(bf16[2,256,768]{2,1,0:T(8,128)(2,1)} %pad_maximum_fusion.13), channel_id=1, source_target_pairs={{0,2},{1,3},{2,0},{3,1},{4,6},{5,7},{6,4},{7,5},{8,10},{9,11},{10,... | collective-permute-start | bytes 2359304 | tf_op jit(solution)/shard_map/ppermute | solution.py:654
  174.5 22.9 %collective-permute-start.10 = (bf16[2,256,768]{2,1,0:T(8,128)(2,1)S(1)}, bf16[2,256,768]{2,1,0:T(8,128)(2,1)}, u32[]{:S(2)}, u32[]{:S(2)}) collective-permute-start(bf16[2,256,768]{2,1,0:T(8,128)(2,1)S(1)} %slice.583), channel_id=1, source_target_pairs={{0,2},{1,3},{2,0},{3,1},{4,6},{5,7},{6,4},{7,5},{8,10},{9,11},{10,... | collective-permute-start | bytes 2359304 | tf_op jit(solution)/shard_map/ppermute | solution.py:654
  177.3 20.1 %collective-permute-start.12 = (bf16[2,256,768]{2,1,0:T(8,128)(2,1)S(1)}, bf16[2,256,768]{2,1,0:T(8,128)(2,1)}, u32[]{:S(2)}, u32[]{:S(2)}) collective-permute-start(bf16[2,256,768]{2,1,0:T(8,128)(2,1)S(1)} %pad_maximum_fusion.9), channel_id=1, source_target_pairs={{0,1},{1,0},{2,3},{3,2},{4,5},{5,4},{6,7},{7,6},{8,9},{9,8},{10,11... | collective-permute-start | bytes 2359304 | tf_op jit(solution)/shard_map/ppermute | solution.py:654
  180.7 383.3 %all-reduce.14.cloned.1.call-start = ((), (), s32[]{:S(2)}) async-start(), calls=%async_computation.14 | async-start | bytes 376832 | tf_op jit(solution)/shard_map/psum | solution.py:891
  182.6 14.3 %collective-permute-start.14 = (f32[2,1024]{1,0:T(2,128)S(1)}, f32[2,1024]{1,0:T(2,128)S(1)}, u32[]{:S(2)}, u32[]{:S(2)}) collective-permute-start(f32[2,1024]{1,0:T(2,128)S(1)} %slice.593), channel_id=1, source_target_pairs={{0,1},{1,0},{2,3},{3,2},{4,5},{5,4},{6,7},{7,6},{8,9},{9,8},{10,11... | collective-permute-start | bytes 24584 | tf_op jit(solution)/shard_map/ppermute | solution.py:654
  198.7 10.0 %collective-permute-start.11 = (bf16[256,768]{1,0:T(8,128)(2,1)S(1)}, bf16[256,768]{1,0:T(8,128)(2,1)S(1)}, u32[]{:S(2)}, u32[]{:S(2)}) collective-permute-start(bf16[256,768]{1,0:T(8,128)(2,1)S(1)} %get-tuple-element.174), channel_id=1, source_target_pairs={{0,1},{1,0},{2,3},{3,2},{4,5},{5,4},{6,7},{7,6},{8,9},{9,8},{10,11... | collective-permute-start | bytes 1179656 | tf_op jit(solution)/shard_map/ppermute | solution.py:654
  215.5 10.6 %collective-permute-start.16 = (bf16[256,768]{1,0:T(8,128)(2,1)}, bf16[256,768]{1,0:T(8,128)(2,1)}, u32[]{:S(2)}, u32[]{:S(2)}) collective-permute-start(bf16[256,768]{1,0:T(8,128)(2,1)} %get-tuple-element.221), channel_id=1, source_target_pairs={{0,1},{1,0},{2,3},{3,2},{4,5},{5,4},{6,7},{7,6},{8,9},{9,8},{10,11... | collective-permute-start | bytes 1179656 | tf_op jit(solution)/shard_map/ppermute | solution.py:654
  219.7 31.0 %collective-permute-start.20 = (bf16[1536,896]{1,0:T(8,128)(2,1)}, bf16[1536,896]{1,0:T(8,128)(2,1)}, u32[]{:S(2)}, u32[]{:S(2)}) collective-permute-start(bf16[1536,896]{1,0:T(8,128)(2,1)} %all-gather.10.cloned.1.call-done.own_ref), channel_id=1, source_target_pairs={{0,16},{16,0},{1,17},{17,1},{2,18},{18,2},{3,19},{19,3},{4,20},{20... | collective-permute-start | bytes 8257544 | tf_op jit(solution)/shard_map/ppermute | solution.py:658
  225.5 16.8 %collective-permute-start.18 = (bf16[2,256,768]{2,1,0:T(8,128)(2,1)}, bf16[2,256,768]{2,1,0:T(8,128)(2,1)}, u32[]{:S(2)}, u32[]{:S(2)}) collective-permute-start(bf16[2,256,768]{2,1,0:T(8,128)(2,1)} %pad_maximum_fusion.10), channel_id=1, source_target_pairs={{0,1},{1,0},{2,3},{3,2},{4,5},{5,4},{6,7},{7,6},{8,9},{9,8},{10,11... | collective-permute-start | bytes 2359304 | tf_op jit(solution)/shard_map/ppermute | solution.py:654
  228.0 17.6 %collective-permute-start.19 = (bf16[2,256,768]{2,1,0:T(8,128)(2,1)}, bf16[2,256,768]{2,1,0:T(8,128)(2,1)}, u32[]{:S(2)}, u32[]{:S(2)}) collective-permute-start(bf16[2,256,768]{2,1,0:T(8,128)(2,1)} %pad_maximum_fusion.11), channel_id=1, source_target_pairs={{0,2},{1,3},{2,0},{3,1},{4,6},{5,7},{6,4},{7,5},{8,10},{9,11},{10,... | collective-permute-start | bytes 2359304 | tf_op jit(solution)/shard_map/ppermute | solution.py:654
  231.4 19.3 %collective-permute-start.21 = (bf16[384,1536]{1,0:T(8,128)(2,1)}, bf16[384,1536]{1,0:T(8,128)(2,1)S(1)}, u32[]{:S(2)}, u32[]{:S(2)}) collective-permute-start(bf16[384,1536]{1,0:T(8,128)(2,1)} %all-gather.12.cloned.1.call-done.out_own_ref), channel_id=1, source_target_pairs={{0,16},{16,0},{1,17},{17,1},{2,18},{18,2},{3,19},{19,3},{4,20},{20... | collective-permute-start | bytes 3538952 | tf_op jit(solution)/shard_map/ppermute | solution.py:658
  331.1 17.4 %collective-permute-start.33 = (bf16[2,256,768]{2,1,0:T(8,128)(2,1)S(1)}, bf16[2,256,768]{2,1,0:T(8,128)(2,1)S(1)}, u32[]{:S(2)}, u32[]{:S(2)}) collective-permute-start(bf16[2,256,768]{2,1,0:T(8,128)(2,1)S(1)} %slice.639), channel_id=1, source_target_pairs={{0,2},{1,3},{2,0},{3,1},{4,6},{5,7},{6,4},{7,5},{8,10},{9,11},{10,... | collective-permute-start | bytes 2359304 | tf_op jit(solution)/shard_map/ppermute | solution.py:654
  331.9 17.0 %collective-permute-start.35 = (bf16[2,256,768]{2,1,0:T(8,128)(2,1)S(1)}, bf16[2,256,768]{2,1,0:T(8,128)(2,1)S(1)}, u32[]{:S(2)}, u32[]{:S(2)}) collective-permute-start(bf16[2,256,768]{2,1,0:T(8,128)(2,1)S(1)} %pad_maximum_fusion.15), channel_id=1, source_target_pairs={{0,1},{1,0},{2,3},{3,2},{4,5},{5,4},{6,7},{7,6},{8,9},{9,8},{10,11... | collective-permute-start | bytes 2359304 | tf_op jit(solution)/shard_map/ppermute | solution.py:654
  363.5 19.7 %collective-permute-start.38 = (bf16[256,768]{1,0:T(8,128)(2,1)}, bf16[256,768]{1,0:T(8,128)(2,1)}, u32[]{:S(2)}, u32[]{:S(2)}) collective-permute-start(bf16[256,768]{1,0:T(8,128)(2,1)} %get-tuple-element.203), channel_id=1, source_target_pairs={{0,2},{1,3},{2,0},{3,1},{4,6},{5,7},{6,4},{7,5},{8,10},{9,11},{10,... | collective-permute-start | bytes 1179656 | tf_op jit(solution)/shard_map/ppermute | solution.py:654
  365.4 21.3 %collective-permute-start.37 = (bf16[256,768]{1,0:T(8,128)(2,1)}, bf16[256,768]{1,0:T(8,128)(2,1)}, u32[]{:S(2)}, u32[]{:S(2)}) collective-permute-start(bf16[256,768]{1,0:T(8,128)(2,1)} %get-tuple-element.204), channel_id=1, source_target_pairs={{0,1},{1,0},{2,3},{3,2},{4,5},{5,4},{6,7},{7,6},{8,9},{9,8},{10,11... | collective-permute-start | bytes 1179656 | tf_op jit(solution)/shard_map/ppermute | solution.py:654
  376.7 88.1 %collective-permute-start.50 = (bf16[384,1536]{1,0:T(8,128)(2,1)}, bf16[384,1536]{1,0:T(8,128)(2,1)}, u32[]{:S(2)}, u32[]{:S(2)}) collective-permute-start(bf16[384,1536]{1,0:T(8,128)(2,1)} %convolution_convert_fusion), channel_id=1, source_target_pairs={{0,16},{16,0},{1,17},{17,1},{2,18},{18,2},{3,19},{19,3},{4,20},{20... | collective-permute-start | bytes 3538952 | tf_op jit(solution)/shard_map/ppermute | solution.py:658
  384.6 18.3 %collective-permute-start.39 = (bf16[2,256,768]{2,1,0:T(8,128)(2,1)S(1)}, bf16[2,256,768]{2,1,0:T(8,128)(2,1)S(1)}, u32[]{:S(2)}, u32[]{:S(2)}) collective-permute-start(bf16[2,256,768]{2,1,0:T(8,128)(2,1)S(1)} %pad_maximum_fusion.16), channel_id=1, source_target_pairs={{0,1},{1,0},{2,3},{3,2},{4,5},{5,4},{6,7},{7,6},{8,9},{9,8},{10,11... | collective-permute-start | bytes 2359304 | tf_op jit(solution)/shard_map/ppermute | solution.py:654
  387.8 17.7 %collective-permute-start.40 = (bf16[2,256,768]{2,1,0:T(8,128)(2,1)S(1)}, bf16[2,256,768]{2,1,0:T(8,128)(2,1)S(1)}, u32[]{:S(2)}, u32[]{:S(2)}) collective-permute-start(bf16[2,256,768]{2,1,0:T(8,128)(2,1)S(1)} %pad_maximum_fusion.17), channel_id=1, source_target_pairs={{0,2},{1,3},{2,0},{3,1},{4,6},{5,7},{6,4},{7,5},{8,10},{9,11},{10,... | collective-permute-start | bytes 2359304 | tf_op jit(solution)/shard_map/ppermute | solution.py:654
  464.7 105.9 %reduce-scatter.18.cloned.1.call-start = ((), (), s32[]{:S(2)}) async-start(), calls=%async_computation.13 | async-start | bytes 1474560
  471.4 150.4 %reduce-scatter.16.cloned.1.call-start = ((), (), s32[]{:S(2)}) async-start(), calls=%async_computation.12 | async-start | bytes 1474560
  484.5 153.9 %reduce-scatter.12.cloned.1.call-start = ((), (), s32[]{:S(2)}) async-start(), calls=%async_computation.10 | async-start | bytes 3440640 | tf_op jit(solution)/shard_map/reduce_scatter | solution.py:872
  493.2 201.8 %reduce-scatter.10.cloned.1.call-start = ((), (), s32[]{:S(2)}) async-start(), calls=%async_computation.9 | async-start | bytes 3440640 | tf_op jit(solution)/shard_map/reduce_scatter | solution.py:872
  498.6 23.5 %collective-permute-start.46 = (bf16[1536,896]{1,0:T(8,128)(2,1)S(1)}, bf16[1536,896]{1,0:T(8,128)(2,1)S(1)}, u32[]{:S(2)}, u32[]{:S(2)}) collective-permute-start(bf16[1536,896]{1,0:T(8,128)(2,1)S(1)} %bitcast_convert_fusion.1), channel_id=1, source_target_pairs={{0,16},{16,0},{1,17},{17,1},{2,18},{18,2},{3,19},{19,3},{4,20},{20... | collective-permute-start | bytes 8257544 | tf_op jit(solution)/shard_map/ppermute | solution.py:658
  499.1 19.7 %collective-permute-start.26 = (bf16[2,256,768]{2,1,0:T(8,128)(2,1)S(1)}, bf16[2,256,768]{2,1,0:T(8,128)(2,1)S(1)}, u32[]{:S(2)}, u32[]{:S(2)}) collective-permute-start(bf16[2,256,768]{2,1,0:T(8,128)(2,1)S(1)} %slice.625), channel_id=1, source_target_pairs={{0,2},{1,3},{2,0},{3,1},{4,6},{5,7},{6,4},{7,5},{8,10},{9,11},{10,... | collective-permute-start | bytes 2359304 | tf_op jit(solution)/shard_map/ppermute | solution.py:654
  500.2 19.4 %collective-permute-start.28 = (bf16[2,256,768]{2,1,0:T(8,128)(2,1)S(1)}, bf16[2,256,768]{2,1,0:T(8,128)(2,1)S(1)}, u32[]{:S(2)}, u32[]{:S(2)}) collective-permute-start(bf16[2,256,768]{2,1,0:T(8,128)(2,1)S(1)} %pad_maximum_fusion.14), channel_id=1, source_target_pairs={{0,1},{1,0},{2,3},{3,2},{4,5},{5,4},{6,7},{7,6},{8,9},{9,8},{10,11... | collective-permute-start | bytes 2359304 | tf_op jit(solution)/shard_map/ppermute | solution.py:654
  520.7 10.3 %collective-permute-start.27 = (bf16[256,768]{1,0:T(8,128)(2,1)}, bf16[256,768]{1,0:T(8,128)(2,1)}, u32[]{:S(2)}, u32[]{:S(2)}) collective-permute-start(bf16[256,768]{1,0:T(8,128)(2,1)} %get-tuple-element.168), channel_id=1, source_target_pairs={{0,1},{1,0},{2,3},{3,2},{4,5},{5,4},{6,7},{7,6},{8,9},{9,8},{10,11... | collective-permute-start | bytes 1179656 | tf_op jit(solution)/shard_map/ppermute | solution.py:654
  527.1 198.3 %reduce-scatter.14.cloned.1.call-start = ((), (), s32[]{:S(2)}) async-start(), calls=%async_computation.11 | async-start | bytes 491520 | tf_op jit(solution)/shard_map/reduce_scatter | solution.py:924
  536.5 20.3 %collective-permute-start.41 = (bf16[2,256,768]{2,1,0:T(8,128)(2,1)}, bf16[2,256,768]{2,1,0:T(8,128)(2,1)}, u32[]{:S(2)}, u32[]{:S(2)}) collective-permute-start(bf16[2,256,768]{2,1,0:T(8,128)(2,1)} %slice.656), channel_id=1, source_target_pairs={{0,2},{1,3},{2,0},{3,1},{4,6},{5,7},{6,4},{7,5},{8,10},{9,11},{10,... | collective-permute-start | bytes 2359304 | tf_op jit(solution)/shard_map/ppermute | solution.py:654
  539.3 20.0 %collective-permute-start.43 = (bf16[2,256,768]{2,1,0:T(8,128)(2,1)}, bf16[2,256,768]{2,1,0:T(8,128)(2,1)}, u32[]{:S(2)}, u32[]{:S(2)}) collective-permute-start(bf16[2,256,768]{2,1,0:T(8,128)(2,1)} %pad_maximum_fusion.18), channel_id=1, source_target_pairs={{0,1},{1,0},{2,3},{3,2},{4,5},{5,4},{6,7},{7,6},{8,9},{9,8},{10,11... | collective-permute-start | bytes 2359304 | tf_op jit(solution)/shard_map/ppermute | solution.py:654
  561.5 10.8 %collective-permute-start.42 = (bf16[256,768]{1,0:T(8,128)(2,1)}, bf16[256,768]{1,0:T(8,128)(2,1)}, u32[]{:S(2)}, u32[]{:S(2)}) collective-permute-start(bf16[256,768]{1,0:T(8,128)(2,1)} %get-tuple-element.156), channel_id=1, source_target_pairs={{0,1},{1,0},{2,3},{3,2},{4,5},{5,4},{6,7},{7,6},{8,9},{9,8},{10,11... | collective-permute-start | bytes 1179656 | tf_op jit(solution)/shard_map/ppermute | solution.py:654
  563.0 10.5 %collective-permute-start.44 = (bf16[256,768]{1,0:T(8,128)(2,1)}, bf16[256,768]{1,0:T(8,128)(2,1)}, u32[]{:S(2)}, u32[]{:S(2)}) collective-permute-start(bf16[256,768]{1,0:T(8,128)(2,1)} %get-tuple-element.157), channel_id=1, source_target_pairs={{0,2},{1,3},{2,0},{3,1},{4,6},{5,7},{6,4},{7,5},{8,10},{9,11},{10,... | collective-permute-start | bytes 1179656 | tf_op jit(solution)/shard_map/ppermute | solution.py:654
  576.8 119.4 %collective-permute-start.45 = (bf16[256,1536]{1,0:T(8,128)(2,1)S(1)}, bf16[256,1536]{1,0:T(8,128)(2,1)}, u32[]{:S(2)}, u32[]{:S(2)}) collective-permute-start(bf16[256,1536]{1,0:T(8,128)(2,1)S(1)} %get-tuple-element.142), channel_id=1, source_target_pairs={{0,16},{16,0},{1,17},{17,1},{2,18},{18,2},{3,19},{19,3},{4,20},{20... | collective-permute-start | bytes 2359304 | tf_op jit(solution)/shard_map/ppermute | solution.py:658
  623.0 75.8 %collective-permute-start.51 = (bf16[384,384]{1,0:T(8,128)(2,1)S(1)}, bf16[384,384]{1,0:T(8,128)(2,1)}, u32[]{:S(2)}, u32[]{:S(2)}) collective-permute-start(bf16[384,384]{1,0:T(8,128)(2,1)S(1)} %broadcast_select_fusion.12), channel_id=1, source_target_pairs={{0,16},{16,0},{1,17},{17,1},{2,18},{18,2},{3,19},{19,3},{4,20},{20... | collective-permute-start | bytes 884744 | tf_op jit(solution)/shard_map/ppermute | solution.py:658
  (104 other events, 764.5 us)
Sparse Core Ops, SparseCore 0:
  53.7 56.0 all-gather.5
  111.4 28.8 all-gather.7
  141.8 56.4 all-gather.9
  199.8 28.8 all-gather.11
  464.8 53.8 all-reduce.13
  521.6 29.7 reduce-scatter.17
  554.4 27.8 reduce-scatter.15
  584.7 53.5 reduce-scatter.11
  640.8 54.1 reduce-scatter.9
  701.1 24.2 reduce-scatter.13

commit v2 on v1

v2 whole, which is shorter than its diff:
```python
import functools

import jax
import jax.numpy as jnp
import numpy as np
from jax import lax
from jax.experimental import pallas as pl
from jax.experimental.pallas import tpu as pltpu
from jax.sharding import PartitionSpec as P

STATE = 128
CHUNK = 256
EXTRA = 16
HALF = 128
LANES = 128
NORM_EPSILON = 1e-05
LOG2E = 1.4426950408889634
F32 = jnp.float32
BF16 = jnp.bfloat16
VMEM_LIMIT = 56 * 1024 * 1024


def dot(a, b):
    return lax.dot_general(a, b, (((1,), (0,)), ((), ())), preferred_element_type=F32)


def dot_nt(a, b):
    return lax.dot_general(a, b, (((1,), (1,)), ((), ())), preferred_element_type=F32)


def dot_tn(a, b):
    return lax.dot_general(a, b, (((0,), (0,)), ((), ())), preferred_element_type=F32)


def pieces(value, count):
    found = []
    for _ in range(count):
        part = value.astype(BF16)
        found.append(part)
        value = value - part.astype(F32)
    return found


def dot_exact(ones, value):
    first, second, third = pieces(value, 3)
    return dot(ones, first) + (dot(ones, second) + dot(ones, third))


def spread(value, expander):
    first, second = pieces(value, 2)
    return dot(first, expander) + dot(second, expander)


def sigmoid(value):
    return 0.5 * jnp.tanh(0.5 * value) + 0.5


def softplus(value):
    return jnp.maximum(value, 0.0) + jnp.log1p(jnp.exp(-jnp.abs(value)))


def iota(shape, axis):
    return lax.broadcasted_iota(jnp.int32, shape, axis)


def segment_of(rows, first_end, second_end):
    return (rows >= first_end).astype(jnp.int32) + (rows >= second_end).astype(jnp.int32)


def head_expander(width):
    size = (LANES, width)
    return (iota(size, 0) == iota(size, 1) // 64).astype(BF16)


def head_folder(width):
    size = (width, LANES)
    return (iota(size, 1) == iota(size, 0) // 64).astype(BF16)


def lower_ones():
    size = (CHUNK, CHUNK)
    return (iota(size, 0) >= iota(size, 1)).astype(BF16)


def upper_ones():
    size = (CHUNK, CHUNK)
    return (iota(size, 0) <= iota(size, 1)).astype(BF16)


def decays(raw, head_ref, base, first_end, second_end, chunk):
    pre = raw + head_ref[0:1, :]
    step = softplus(pre)
    log_decay = -step * jnp.exp(head_ref[1:2, :])
    total = dot_exact(lower_ones(), log_decay) * LOG2E
    rows = base + iota((CHUNK, LANES), 0)
    segment = segment_of(rows, first_end, second_end)
    previous = jnp.where(chunk == 0, -1, segment_of(base - 1, first_end, second_end))
    final = segment_of(base + CHUNK - 1, first_end, second_end)
    last = total[CHUNK - 1 : CHUNK, :]
    start = jnp.where(segment == previous, jnp.exp2(total), 0.0)
    ending = jnp.where(segment == final, jnp.exp2(last - total), 0.0)
    kept = jnp.where(final == previous, jnp.exp2(last), 0.0)
    return pre, step, log_decay, total, start, ending, kept


def same_block(row_base, col_base, first_end, second_end):
    size = (HALF, HALF)
    rows = row_base + iota(size, 0)
    cols = col_base + iota(size, 1)
    return (
        (segment_of(rows, first_end, second_end) == segment_of(cols, first_end, second_end)),
        rows,
        cols,
    )


def pick_rows(target, blocks, slot, extra=None):
    rows, cols = target.shape[0], target.shape[1] // 2
    for at in range(3):

        @pl.when(slot == at)
        def _():
            target[...] = blocks[at][:rows, :]
            if extra is not None:
                extra[...] = blocks[at][rows:, :cols]

    @pl.when(slot == 3)
    def _():
        target[:, :cols] = blocks[3][:rows, :]
        target[:, cols:] = blocks[4][:rows, :]
        if extra is not None:
            extra[...] = blocks[3][rows:, :]


def put_rows(targets, value, slot):
    parts = len(targets) // 4
    cols = value.shape[1] // parts
    for at in range(4):

        @pl.when(slot == at)
        def _():
            for part in range(parts):
                targets[4 * part + at][...] = value[:, part * cols : (part + 1) * cols].astype(
                    BF16
                )


def normalise(x_rows, norm_ref):
    depth = x_rows.shape[1]
    squares = jnp.zeros((CHUNK, LANES), F32)
    for tile in range(depth // LANES):
        lanes = slice(tile * LANES, (tile + 1) * LANES)
        x = x_rows[:, lanes].astype(F32)
        squares = squares + x * x
    scale = lax.rsqrt(jnp.sum(squares, axis=1, keepdims=True) / depth + NORM_EPSILON)
    scale = jnp.broadcast_to(scale, (CHUNK, LANES))
    for tile in range(depth // LANES):
        lanes = slice(tile * LANES, (tile + 1) * LANES)
        x = x_rows[:, lanes].astype(F32)
        x_rows[:, lanes] = (x * scale * norm_ref[0:1, lanes]).astype(BF16)


def padded_step(step_ref):
    rows, cols = step_ref.shape
    return jnp.concatenate([step_ref[...], jnp.zeros((LANES - rows, cols), BF16)], axis=0)


def mixer_kernel(scalars, *refs):
    blocks = refs[:5]
    (
        own_ref,
        other_ref,
        step_ref,
        norm_ref,
        taps_ref,
        head_ref,
        slots_ref,
        conv_ref,
        input_ref,
        y_ref,
        raw_ref,
        state_ref,
        x_rows,
        joined,
        state,
        end_x,
        from_state,
        step_wide,
        start_wide,
        end_wide,
    ) = refs[5:]
    chunk = pl.program_id(0)
    side, first_end, second_end = scalars[0], scalars[1], scalars[2]
    base = chunk * CHUNK
    width = end_x.shape[1]
    half = width // 2

    @pl.when(chunk == 0)
    def _():
        state[...] = jnp.zeros_like(state)
        joined[0:8, :] = jnp.zeros((8, joined.shape[1]), F32)

    pick_rows(x_rows, blocks, chunk ^ scalars[3])
    normalise(x_rows, norm_ref)
    x = x_rows[...]
    slots_ref[0] = x
    shared = half + STATE
    own = dot(x, own_ref[:, :shared])
    other = dot(x, other_ref[:, :shared])
    raw = dot_nt(x, padded_step(step_ref))
    raw_ref[0] = raw
    joined[8:, :half] = own[:, :half]
    joined[8:, half:width] = other[:, :half]
    joined[8:, width : width + STATE] = jnp.where(side == 0, own[:, half:], other[:, half:])
    joined[8:, width + STATE :] = jnp.where(side == 0, other[:, half:], own[:, half:])

    _, step, _, total, start, ending, kept = decays(
        raw, head_ref, base, first_end, second_end, chunk
    )
    expander = head_expander(width)
    step_wide[...] = spread(step, expander)
    start_wide[...] = spread(start, expander)
    end_wide[...] = spread(ending, expander)
    kept_wide = spread(jnp.broadcast_to(kept, (8, LANES)), expander)[0:1]
    skip = spread(jnp.broadcast_to(head_ref[2:3, :], (8, LANES)), expander)[0:1]
    total_rows = total.T

    rows = base + iota((CHUNK, LANES), 0)
    inside = rows - jnp.where(
        rows >= second_end, second_end, jnp.where(rows >= first_end, first_end, 0)
    )
    masks = [(inside >= lag).astype(F32) for lag in range(1, 4)]

    def activate(lanes):
        current = joined[8:, lanes]
        found = taps_ref[4:5, lanes] + taps_ref[3:4, lanes] * current
        for lag in range(1, 4):
            shifted = joined[8 - lag : 8 - lag + CHUNK, lanes] * masks[lag - 1]
            found = found + taps_ref[3 - lag : 4 - lag, lanes] * shifted
        conv_ref[0, :, lanes] = found.astype(BF16)
        input_ref[0, :, lanes] = current.astype(BF16)
        return found * sigmoid(found)

    b_f32 = activate(slice(width, width + STATE))
    b_low = b_f32.astype(BF16)
    c_low = activate(slice(width + STATE, width + 2 * STATE)).astype(BF16)
    state_ref[0] = state[...].astype(BF16)
    from_state[...] = dot(c_low, state[...].astype(BF16))
    inter = dot_nt(c_low, b_low)

    def masked(row_at, col_at):
        same, row_ids, col_ids = same_block(base + row_at, base + col_at, first_end, second_end)
        if row_at == col_at:
            same = same & (row_ids >= col_ids)
        return jnp.where(same, inter[row_at : row_at + HALF, col_at : col_at + HALF], 0.0)

    inter_00, inter_10, inter_11 = masked(0, 0), masked(HALF, 0), masked(HALF, HALF)
    low_lanes = iota((CHUNK, LANES), 1) < 64
    for tile in range(width // LANES):
        lanes = slice(tile * LANES, (tile + 1) * LANES)
        values = activate(lanes)
        scaled = values * step_wide[:, lanes]
        end_x[:, lanes] = (scaled * end_wide[:, lanes]).astype(BF16)
        scaled_parts = [
            jnp.where(low_lanes, scaled, 0.0).astype(BF16),
            jnp.where(low_lanes, 0.0, scaled).astype(BF16),
        ]
        top, bottom = [], []
        for side_at in range(2):
            head = 2 * tile + side_at
            column = total[:, head : head + 1]
            row = total_rows[head : head + 1, :]
            top_col, low_col = column[:HALF], column[HALF:]
            top_row, low_row = row[:, :HALF], row[:, HALF:]
            top.append((inter_00 * jnp.exp2(jnp.minimum(top_col - top_row, 0.0))).astype(BF16))
            bottom.append((inter_10 * jnp.exp2(low_col - top_row)).astype(BF16))
            bottom.append((inter_11 * jnp.exp2(jnp.minimum(low_col - low_row, 0.0))).astype(BF16))
        local_top = dot(
            jnp.concatenate(top, axis=1),
            jnp.concatenate([scaled_parts[0][:HALF], scaled_parts[1][:HALF]], axis=0),
        )
        local_bottom = dot(
            jnp.concatenate(bottom, axis=1), jnp.concatenate(scaled_parts, axis=0)
        )
        local = jnp.concatenate([local_top, local_bottom], axis=0)
        y = local + from_state[:, lanes] * start_wide[:, lanes] + skip[:, lanes] * values
        y_ref[0, :, lanes] = y.astype(BF16)
    state[...] = kept_wide * state[...] + dot(b_f32.T.astype(BF16), end_x[...])
    joined[0:8, :] = joined[CHUNK : CHUNK + 8, :]


def gate_kernel(scalars, x_ref, own_ref, other_ref, gain_ref, y_ref, *rest):
    z_ref, hidden_ref, sums_ref = rest
    width = hidden_ref.shape[2]
    half = width // 2
    x = x_ref[0]
    offset = own_ref.shape[1] - half
    gates = [dot(x, own_ref[:, offset:]), dot(x, other_ref[:, offset:])]
    squares = jnp.zeros((CHUNK, LANES), F32)
    for tile in range(width // LANES):
        lanes = slice(tile * LANES, (tile + 1) * LANES)
        at = tile * LANES % half
        z = gates[tile * LANES // half][:, at : at + LANES]
        z_ref[0, :, lanes] = z.astype(BF16)
        mixed = y_ref[0, :, lanes].astype(F32) * (z * sigmoid(z))
        squares = squares + mixed * mixed
        hidden_ref[0, :, lanes] = (mixed * gain_ref[5:6, lanes]).astype(BF16)
    ones = jnp.ones((8, LANES), BF16)
    first, second = pieces(squares, 2)
    sums_ref[...] = dot_nt(ones, first) + dot_nt(ones, second)


def project_kernel(scalars, hidden_ref, own_ref, other_ref, *out_refs):
    hidden = hidden_ref[0]
    half = hidden.shape[1] // 2
    found = dot(hidden[:, :half], own_ref[...]) + dot(hidden[:, half:], other_ref[...])
    if len(out_refs) == 8:
        put_rows(out_refs, found, pl.program_id(0))
    else:
        grad_ref, *out_refs, sums_ref = out_refs
        put_rows(out_refs, found, pl.program_id(0))
        crossed = jnp.zeros((CHUNK, LANES), F32)
        for tile in range(found.shape[1] // LANES):
            lanes = slice(tile * LANES, (tile + 1) * LANES)
            crossed = crossed + found[:, lanes] * grad_ref[0, :, lanes].astype(F32)
        ones = jnp.ones((8, LANES), BF16)
        first, second = pieces(crossed, 2)
        sums_ref[...] = dot_nt(ones, first) + dot_nt(ones, second)


def gate_backward_kernel(inner_factor, scalars, *refs):
    early = len(refs) < 15
    if early:
        back_refs, refs = refs[:2], refs[2:]
        backs = [ref[0].astype(F32) for ref in back_refs]
    else:
        blocks, (out_own_ref, out_other_ref), refs = refs[:5], refs[5:7], refs[7:]
        refs, (natural_ref, grad_rows, extra) = refs[:-3], refs[-3:]
        pick_rows(grad_rows, blocks, pl.program_id(0), extra)
        grad = grad_rows[...]
        natural_ref[0] = grad
        backs = [dot_nt(grad, out_own_ref[...]), dot_nt(grad, out_other_ref[...])]
    (
        rows_ref,
        gain_ref,
        z_ref,
        y_ref,
        own_grad_ref,
        other_grad_ref,
        hidden_ref,
        grad_y_ref,
        gain_grad_ref,
    ) = refs
    width = hidden_ref.shape[2]
    half = width // 2

    @pl.when(pl.program_id(0) == 0)
    def _():
        gain_grad_ref[...] = jnp.zeros_like(gain_grad_ref)

    scale_row = rows_ref[0:1, :]
    if early:
        crossed = rows_ref[1:2, :]
    else:
        parts = extra[0:1, : 3 * CHUNK].astype(F32)
        crossed = parts[:, :CHUNK] + (parts[:, CHUNK : 2 * CHUNK] + parts[:, 2 * CHUNK :])
    inner_row = scale_row * scale_row * scale_row * crossed * inner_factor
    columns = jnp.concatenate(
        [scale_row, inner_row, jnp.zeros((LANES - 2, CHUNK), F32)], axis=0
    ).T
    scale = jnp.broadcast_to(columns[:, 0:1], (CHUNK, LANES))
    inner = jnp.broadcast_to(columns[:, 1:2], (CHUNK, LANES))
    for tile in range(width // LANES):
        lanes = slice(tile * LANES, (tile + 1) * LANES)
        at = tile * LANES % half
        back = backs[tile * LANES // half][:, at : at + LANES]
        gain = gain_ref[5:6, lanes]
        z = z_ref[0, :, lanes].astype(F32)
        gate = sigmoid(z)
        gated = z * gate
        y = y_ref[0, :, lanes].astype(F32)
        mixed = y * gated
        scaled_mixed = mixed * scale
        hidden_ref[0, :, lanes] = (scaled_mixed * gain).astype(BF16)
        gain_grad_ref[0:1, lanes] += jnp.sum(back * scaled_mixed, axis=0, keepdims=True)
        grad_mixed = scale * (back * gain) - mixed * inner
        grad_y_ref[0, :, lanes] = (grad_mixed * gated).astype(BF16)
        dz = (grad_mixed * y * (gate + gated * (1.0 - gate))).astype(BF16)
        if tile * LANES < half:
            own_grad_ref[0, :, at : at + LANES] = dz
        else:
            other_grad_ref[0, :, at : at + LANES] = dz


def mixer_backward_kernel(
    scalars,
    grad_y_ref,
    gate_own_grad_ref,
    gate_other_grad_ref,
    own_ref,
    other_ref,
    gate_own_ref,
    gate_other_ref,
    step_ref,
    norm_ref,
    taps_ref,
    head_ref,
    gain_grad_ref,
    slots_ref,
    conv_ref,
    input_ref,
    raw_ref,
    state_ref,
    *rest,
):
    back_refs = rest[:8]
    (
        own_grad_ref,
        other_grad_ref,
        small_grad_ref,
        step_grad,
        grad_state,
        grad_conv,
        step_wide,
        start_wide,
        end_wide,
        from_state,
        to_state,
        end_x,
        start_dy,
        sum_end,
        sum_start,
        sum_step,
        grad_inter,
    ) = rest[8:]
    rows_grad_ref = small_grad_ref.at[0:24]
    wide_grad_ref = small_grad_ref.at[24:32]
    turn = pl.program_id(0)
    chunk = pl.num_programs(0) - 1 - turn
    side, first_end, second_end = scalars[0], scalars[1], scalars[2]
    base = chunk * CHUNK
    width = end_x.shape[1]
    half = width // 2

    @pl.when(turn == 0)
    def _():
        grad_state[...] = jnp.zeros_like(grad_state)
        grad_conv[CHUNK:, :] = jnp.zeros((8, grad_conv.shape[1]), F32)
        small_grad_ref[...] = jnp.zeros_like(small_grad_ref)

    pre, step, log_decay, total, start, ending, kept = decays(
        raw_ref[0], head_ref, base, first_end, second_end, chunk
    )
    expander = head_expander(width)
    step_wide[...] = spread(step, expander)
    start_wide[...] = spread(start, expander)
    end_wide[...] = spread(ending, expander)
    kept_wide = spread(jnp.broadcast_to(kept, (8, LANES)), expander)[0:1]
    skip = spread(jnp.broadcast_to(head_ref[2:3, :], (8, LANES)), expander)[0:1]
    total_rows = total.T

    def activated(lanes):
        conv = conv_ref[0, :, lanes].astype(F32)
        gate = sigmoid(conv)
        value = conv * gate
        return value, gate + value * (1.0 - gate)

    b_lanes, c_lanes = slice(width, width + STATE), slice(width + STATE, width + 2 * STATE)
    b_f32, b_slope = activated(b_lanes)
    c_f32, c_slope = activated(c_lanes)
    b_low, c_low = b_f32.astype(BF16), c_f32.astype(BF16)
    state_low = state_ref[0]
    grad_state_low = grad_state[...].astype(BF16)
    from_state[...] = dot(c_low, state_low)
    to_state[...] = dot(b_low, grad_state_low)
    inter = dot_nt(b_low, c_low)

    def same_pairs(row_at, col_at):
        same, row_ids, col_ids = same_block(base + row_at, base + col_at, first_end, second_end)
        if row_at == col_at:
            same = same & (row_ids <= col_ids)
        return same

    same_00, same_01, same_11 = same_pairs(0, 0), same_pairs(0, HALF), same_pairs(HALF, HALF)
    inter_00 = jnp.where(same_00, inter[:HALF, :HALF], 0.0)
    inter_01 = jnp.where(same_01, inter[:HALF, HALF:], 0.0)
    inter_11 = jnp.where(same_11, inter[HALF:, HALF:], 0.0)
    low_lanes = iota((CHUNK, LANES), 1) < 64
    lane_ids = iota((CHUNK, LANES), 1)
    row_ids = iota((LANES, CHUNK), 0)
    col_sums = jnp.zeros((CHUNK, LANES), F32)
    row_sum_list = []
    grad_inter[...] = jnp.zeros_like(grad_inter)
    for tile in range(width // LANES):
        lanes = slice(tile * LANES, (tile + 1) * LANES)
        values, slope = activated(lanes)
        scaled = values * step_wide[:, lanes]
        scaled_low = scaled.astype(BF16)
        dy_low = grad_y_ref[0, :, lanes]
        dy = dy_low.astype(F32)
        top, bottom = [], []
        for side_at in range(2):
            head = 2 * tile + side_at
            picked = low_lanes if side_at == 0 else ~low_lanes
            lhs = jnp.where(picked, scaled, 0.0).astype(BF16)
            pair_grad = dot_nt(lhs, dy_low)
            column = total[:, head : head + 1]
            row = total_rows[head : head + 1, :]
            top_col, low_col = column[:HALF], column[HALF:]
            top_row, low_row = row[:, :HALF], row[:, HALF:]
            decay_00 = jnp.exp2(jnp.minimum(top_row - top_col, 0.0))
            decay_01 = jnp.exp2(low_row - top_col)
            decay_11 = jnp.exp2(jnp.minimum(low_row - low_col, 0.0))
            part_00 = pair_grad[:HALF, :HALF] * decay_00
            part_01 = pair_grad[:HALF, HALF:] * decay_01
            part_11 = pair_grad[HALF:, HALF:] * decay_11
            grad_inter[:HALF, :HALF] += part_00
            grad_inter[:HALF, HALF:] += part_01
            grad_inter[HALF:, HALF:] += part_11
            full_00, full_01, full_11 = part_00 * inter_00, part_01 * inter_01, part_11 * inter_11
            top.append((inter_00 * decay_00).astype(BF16))
            top.append((inter_01 * decay_01).astype(BF16))
            bottom.append((inter_11 * decay_11).astype(BF16))
            col_sum = jnp.concatenate(
                [
                    jnp.sum(full_00 + full_01, axis=1, keepdims=True),
                    jnp.sum(full_11, axis=1, keepdims=True),
                ],
                axis=0,
            )
            col_sums = jnp.where(lane_ids == head, col_sum, col_sums)
            row_sum_list.append(
                jnp.concatenate(
                    [
                        jnp.sum(full_00, axis=0, keepdims=True),
                        jnp.sum(full_01 + full_11, axis=0, keepdims=True),
                    ],
                    axis=1,
                )
            )
        dy_parts = [
            jnp.where(low_lanes, dy, 0.0).astype(BF16),
            jnp.where(low_lanes, 0.0, dy).astype(BF16),
        ]
        local_top = dot(jnp.concatenate(top, axis=1), jnp.concatenate(dy_parts, axis=0))
        local_bottom = dot(
            jnp.concatenate(bottom, axis=1),
            jnp.concatenate([dy_parts[0][HALF:], dy_parts[1][HALF:]], axis=0),
        )
        local = jnp.concatenate([local_top, local_bottom], axis=0)
        tail = end_wide[:, lanes]
        back_state = to_state[:, lanes]
        grad_scaled = local + tail * back_state
        ended = scaled * tail
        end_x[:, lanes] = ended.astype(BF16)
        sum_end[:, lanes] = (ended * back_state).astype(BF16)
        started = dy * start_wide[:, lanes]
        start_dy[:, lanes] = started.astype(BF16)
        sum_start[:, lanes] = (started * from_state[:, lanes]).astype(BF16)
        sum_step[:, lanes] = (grad_scaled * values).astype(BF16)
        grad_values = step_wide[:, lanes] * grad_scaled + skip[:, lanes] * dy
        wide_grad_ref[6:7, lanes] += jnp.sum(dy * values, axis=0, keepdims=True)
        grad_conv[:CHUNK, lanes] = grad_values * slope

    grad_inter_00 = jnp.where(same_00, grad_inter[:HALF, :HALF], 0.0)
    grad_inter_01 = jnp.where(same_01, grad_inter[:HALF, HALF:], 0.0)
    grad_inter_11 = jnp.where(same_11, grad_inter[HALF:, HALF:], 0.0)
    pair_t = jnp.concatenate(
        [
            jnp.concatenate([grad_inter_00, grad_inter_01], axis=1),
            jnp.concatenate([jnp.zeros((HALF, HALF), F32), grad_inter_11], axis=1),
        ],
        axis=0,
    )
    grad_b = dot(pair_t.astype(BF16), c_low) + dot_nt(end_x[...], grad_state_low)
    grad_c = dot(pair_t.T.astype(BF16), b_low) + dot_nt(start_dy[...], state_low)
    grad_conv[:CHUNK, b_lanes] = grad_b * b_slope
    grad_conv[:CHUNK, c_lanes] = grad_c * c_slope

    folder = head_folder(width)
    end_sums = dot(sum_end[...], folder)
    start_sums = dot(sum_start[...], folder)
    step_sums = dot(sum_step[...], folder)
    state_pairs = jnp.sum(grad_state[...] * state_low.astype(F32), axis=0, keepdims=True)
    first, second = pieces(jnp.broadcast_to(state_pairs, (8, width)), 2)
    state_sums = (dot(first, folder) + dot(second, folder))[0:1] * kept
    row_sums = jnp.concatenate(
        row_sum_list + [jnp.zeros((LANES - len(row_sum_list), CHUNK), F32)], axis=0
    ).T
    grad_total = row_sums - col_sums + start_sums - end_sums
    last = state_sums + jnp.sum(end_sums, axis=0, keepdims=True)
    grad_total = grad_total + jnp.where(iota((CHUNK, LANES), 0) == CHUNK - 1, last, 0.0)
    grad_decay = dot_exact(upper_ones(), grad_total)
    grad_step = step_sums - grad_decay * jnp.exp(head_ref[1:2, :])
    grad_raw = grad_step * sigmoid(pre)
    wide_grad_ref[7:8, :LANES] += jnp.sum(grad_raw, axis=0, keepdims=True)
    wide_grad_ref[7:8, LANES : 2 * LANES] += jnp.sum(grad_decay * log_decay, axis=0, keepdims=True)
    step_grad[...] = grad_raw.astype(BF16)
    rows_grad_ref[0:16, :] += dot(grad_raw.T[0:16, :].astype(BF16), slots_ref[0])
    grad_state[...] = kept_wide * grad_state[...] + dot(c_f32.T.astype(BF16), start_dy[...])

    rows = base + iota((CHUNK, LANES), 0)
    segment = segment_of(rows, first_end, second_end)
    masks = [
        (segment_of(rows + lag, first_end, second_end) == segment).astype(F32)
        for lag in range(1, 4)
    ]
    for tile in range((width + 2 * STATE) // LANES):
        lanes = slice(tile * LANES, (tile + 1) * LANES)
        inputs = input_ref[0, :, lanes].astype(F32)
        current = grad_conv[:CHUNK, lanes]
        found = taps_ref[3:4, lanes] * current
        wide_grad_ref[4:5, lanes] += jnp.sum(current, axis=0, keepdims=True)
        wide_grad_ref[3:4, lanes] += jnp.sum(current * inputs, axis=0, keepdims=True)
        for lag in range(1, 4):
            shifted = grad_conv[lag : lag + CHUNK, lanes] * masks[lag - 1]
            found = found + taps_ref[3 - lag : 4 - lag, lanes] * shifted
            wide_grad_ref[3 - lag : 4 - lag, lanes] += jnp.sum(
                shifted * inputs, axis=0, keepdims=True
            )
        found = found.astype(BF16)
        if tile * LANES < half:
            own_grad_ref[0, :, lanes] = found
        elif tile * LANES < width:
            other_grad_ref[0, :, tile * LANES - half : (tile + 1) * LANES - half] = found
        elif tile * LANES == width:
            shared_b = found
        else:
            own_grad_ref[0, :, half:] = jnp.where(side == 0, shared_b, found)
            other_grad_ref[0, :, half:] = jnp.where(side == 0, found, shared_b)
    grad_conv[CHUNK:, :] = grad_conv[0:8, :]
    shared, offset = half + STATE, gate_own_ref.shape[1] - half
    back = (
        dot_nt(own_grad_ref[0], own_ref[:, :shared])
        + dot_nt(other_grad_ref[0], other_ref[:, :shared])
        + dot(step_grad[...], padded_step(step_ref))
        + dot_nt(gate_own_grad_ref[0], gate_own_ref[:, offset:])
        + dot_nt(gate_other_grad_ref[0], gate_other_ref[:, offset:])
    )
    for tile in range(back.shape[1] // LANES):
        lanes = slice(tile * LANES, (tile + 1) * LANES)
        products = back[:, lanes] * slots_ref[0, :, lanes].astype(F32)
        rows_grad_ref[16:17, lanes] += jnp.sum(products, axis=0, keepdims=True)

    @pl.when(turn == pl.num_programs(0) - 1)
    def _():
        rows_grad_ref[16:17, :] = rows_grad_ref[16:17, :] / norm_ref[0:1, :]
        wide_grad_ref[5:6, :width] = gain_grad_ref[0:1, :]
        heads = width // 64
        wide = wide_grad_ref[...]
        turned = jnp.concatenate([wide[:7, half:width], wide[:7, :half]], axis=1)
        wide_grad_ref[0:7, :width] = jnp.where(side == 0, wide[:7, :width], turned)
        for lanes in (slice(0, LANES), slice(LANES, 2 * LANES)):
            row = wide_grad_ref[7:8, lanes]
            turned = jnp.where(
                iota((1, LANES), 1) < heads // 2,
                pltpu.roll(row, LANES - heads // 2, axis=1),
                pltpu.roll(row, heads // 2, axis=1),
            )
            wide_grad_ref[7:8, lanes] = jnp.where(side == 0, row, turned)
        rows = rows_grad_ref[0:16, :]
        turned = jnp.concatenate(
            [rows[heads // 2 : heads], rows[: heads // 2], rows[heads:]], axis=0
        )
        rows_grad_ref[0:16, :] = jnp.where(side == 0, rows, turned)

    put_rows(back_refs, back, chunk ^ scalars[3])


def whole(shape):
    return pl.BlockSpec(shape, lambda i, s: (0,) * len(shape))


def forward_slot(cols, height=CHUNK):
    return pl.BlockSpec((1, height, cols), lambda i, s: (i ^ s[3], 0, 0))


def same_slot(cols, height=CHUNK):
    return pl.BlockSpec((1, height, cols), lambda i, s: (i, 0, 0))


def low(*shape):
    return jax.ShapeDtypeStruct(shape, BF16)


def full(*shape):
    return jax.ShapeDtypeStruct(shape, F32)


def call(kernel, name, count, scalars, inputs, outputs, scratch=(), events=(), cost=100):
    taken = len(inputs)

    def body(scalars, *refs):
        kernel(scalars, *refs[:taken], *refs[taken + len(events) :])

    anywhere = pl.BlockSpec(memory_space=pl.ANY)
    return pl.pallas_call(
        body,
        grid_spec=pltpu.PrefetchScalarGridSpec(
            num_scalar_prefetch=1,
            grid=(count,),
            in_specs=[spec for _, spec in inputs] + [anywhere] * len(events),
            out_specs=[spec for _, spec in outputs],
            scratch_shapes=list(scratch),
        ),
        out_shape=[shape for shape, _ in outputs],
        compiler_params=pltpu.CompilerParams(vmem_limit_bytes=VMEM_LIMIT),
        cost_estimate=pl.CostEstimate(
            flops=cost * 1_000_000_000, bytes_accessed=1, transcendentals=0
        ),
        name=name,
    )(scalars, *[array for array, _ in inputs], *events)


def constants(*arrays):
    return [(array, whole(array.shape)) for array in arrays]


def run_mixer(scalars, blocks, weights, events=()):
    count = 4
    depth = blocks[0].shape[1]
    joined = weights["wide"].shape[1]
    width = joined - 2 * STATE
    inputs = constants(
        *blocks,
        weights["own"],
        weights["other"],
        weights["step"],
        weights["norm"],
        weights["wide"],
        weights["head"],
    )
    outputs = [
        (low(count, CHUNK, depth), forward_slot(depth)),
        (low(count, CHUNK, joined), forward_slot(joined)),
        (low(count, CHUNK, joined), forward_slot(joined)),
        (low(count, CHUNK, width), forward_slot(width)),
        (full(count, CHUNK, LANES), forward_slot(LANES)),
        (low(count, STATE, width), forward_slot(width, STATE)),
    ]
    scratch = [
        pltpu.VMEM((CHUNK, depth), BF16),
        pltpu.VMEM((CHUNK + 8, joined), F32),
        pltpu.VMEM((STATE, width), F32),
        pltpu.VMEM((CHUNK, width), BF16),
    ] + [pltpu.VMEM((CHUNK, width), F32)] * 4
    return call(
        mixer_kernel, "mixer", count, scalars, inputs, outputs, scratch, events=events
    )


def run_gate(scalars, slots, y, weights, events=()):
    count, _, depth = slots.shape
    width = y.shape[2]
    inputs = (
        [(slots, same_slot(depth))]
        + constants(weights["gate_own"], weights["gate_other"], weights["wide"])
        + [(y, same_slot(width))]
    )
    outputs = [
        (low(count, CHUNK, width), same_slot(width)),
        (low(count, CHUNK, width), same_slot(width)),
        (full(8, count * CHUNK), pl.BlockSpec((8, CHUNK), lambda i, s: (0, i ^ s[3]))),
    ]
    return call(gate_kernel, "gate", count, scalars, inputs, outputs, events=events, cost=20)


def run_project(scalars, hidden, weights, grads=None, events=()):
    count, _, width = hidden.shape
    depth = weights["out_own"].shape[1]
    inputs = [(hidden, same_slot(width))] + constants(weights["out_own"], weights["out_other"])
    if grads is None:
        outputs = [(low(CHUNK, depth // 2), whole((CHUNK, depth // 2)))] * 8
    else:
        inputs.append((grads, forward_slot(depth)))
        outputs = [(low(CHUNK, depth), whole((CHUNK, depth)))] * 4 + [
            (full(8, count * CHUNK), pl.BlockSpec((8, CHUNK), lambda i, s: (0, i ^ s[3])))
        ]
    return call(
        project_kernel,
        "project",
        count,
        scalars,
        inputs,
        outputs,
        events=events,
        cost=1 if grads is None else 20,
    )


def run_gate_backward(scalars, grads, row_values, weights, z, y, inner_total, events=()):
    count, _, width = z.shape
    half = width // 2
    if len(grads) == 2:
        inputs = [(back, forward_slot(half)) for back in grads]
    else:
        inputs = constants(*grads, weights["out_own"], weights["out_other"])
    inputs = (
        inputs
        + [(row_values, pl.BlockSpec((8, CHUNK), lambda i, s: (0, i ^ s[3])))]
        + constants(weights["wide"])
        + [(z, same_slot(width)), (y, same_slot(width))]
    )
    outputs = [
        (low(count, CHUNK, half), same_slot(half)),
        (low(count, CHUNK, half), same_slot(half)),
        (low(count, CHUNK, width), forward_slot(width)),
        (low(count, CHUNK, width), same_slot(width)),
        (full(8, width), whole((8, width))),
    ]
    scratch = []
    if len(grads) != 2:
        depth = grads[0].shape[1]
        outputs.append((low(count, CHUNK, depth), forward_slot(depth)))
        scratch.append(pltpu.VMEM((CHUNK, depth), BF16))
        scratch.append(pltpu.VMEM((EXTRA, depth // 2), BF16))
    return call(
        functools.partial(gate_backward_kernel, 1.0 / inner_total),
        "gate_backward",
        count,
        scalars,
        inputs,
        outputs,
        scratch,
        events=events,
        cost=1,
    )


def run_mixer_backward(scalars, grad_y, gate_grads, gain_grad, weights, slots, kept, events=()):
    count, _, width = grad_y.shape
    half = width // 2
    joined = width + 2 * STATE
    depth = slots.shape[2]
    shared = half + STATE
    final = count - 1

    def slot(cols, height=CHUNK):
        return pl.BlockSpec((1, height, cols), lambda i, s: ((final - i) ^ s[3], 0, 0))

    conv, inputs, raw, states = kept
    operands = (
        [(grad_y, slot(width))]
        + [(grad, slot(half)) for grad in gate_grads]
        + constants(
            weights["own"],
            weights["other"],
            weights["gate_own"],
            weights["gate_other"],
            weights["step"],
            weights["norm"],
            weights["wide"],
            weights["head"],
            gain_grad,
        )
        + [(slots, slot(depth)), (conv, slot(joined)), (inputs, slot(joined))]
        + [(raw, slot(LANES)), (states, slot(width, STATE))]
    )
    outputs = [(low(CHUNK, depth // 2), whole((CHUNK, depth // 2)))] * 8 + [
        (low(count, CHUNK, shared), slot(shared)),
        (low(count, CHUNK, shared), slot(shared)),
        (full(32, depth), whole((32, depth))),
    ]
    scratch = (
        [pltpu.VMEM((CHUNK, LANES), BF16)]
        + [pltpu.VMEM((STATE, width), F32), pltpu.VMEM((CHUNK + 8, joined), F32)]
        + [pltpu.VMEM((CHUNK, width), F32)] * 5
        + [pltpu.VMEM((CHUNK, width), BF16)] * 5
        + [pltpu.VMEM((CHUNK, CHUNK), F32)]
    )
    return call(
        mixer_backward_kernel,
        "mixer_backward",
        count,
        scalars,
        operands,
        outputs,
        scratch,
        events=events,
    )


def weight_grad_kernel(pairs, scalars, *refs):
    own_ref, other_ref = refs[-2:]
    at = 0
    for left_at, own_at, other_at in pairs:
        left_ref = refs[left_at]
        rows = left_ref.shape[0] * left_ref.shape[1]
        left = left_ref[...].reshape(rows, left_ref.shape[2])
        if other_at is None:
            both = refs[own_at][...].reshape(rows, refs[own_at].shape[2])
            cols = both.shape[1] // 2
            own, other = both[:, :cols], both[:, cols:]
        else:
            cols = refs[own_at].shape[2]
            own = refs[own_at][...].reshape(rows, cols)
            other = refs[other_at][...].reshape(rows, cols)
        own_ref[:, at : at + cols] = dot_tn(left, own).astype(BF16)
        other_ref[:, at : at + cols] = dot_tn(left, other).astype(BF16)
        at += cols


def run_weight_grad(scalars, slots, grads, rows_out=None, hidden=None, events=(), cost=100):
    inputs, pairs, cols = [], [], 0

    def left(array):
        count, rows, depth = array.shape
        inputs.append((array, pl.BlockSpec((count, rows, depth // 4), lambda i, s: (0, 0, i))))
        return len(inputs) - 1

    if grads:
        at = left(slots)
        for own, other in zip(grads[::2], grads[1::2]):
            inputs.extend(constants(own, other))
            pairs.append((at, len(inputs) - 2, len(inputs) - 1))
            cols += own.shape[2]
    if hidden is not None:
        at = left(rows_out)
        inputs.extend(constants(hidden))
        pairs.append((at, len(inputs) - 1, None))
        cols += hidden.shape[2] // 2
    depth = inputs[0][0].shape[2]
    outputs = [(low(depth, cols), pl.BlockSpec((depth // 4, cols), lambda i, s: (i, 0)))] * 2
    return call(
        functools.partial(weight_grad_kernel, tuple(pairs)),
        "weight_grad",
        4,
        scalars,
        inputs,
        outputs,
        events=events,
        cost=cost,
    )


def early_back_kernel(scalars, grad_ref, own_ref, other_ref, own_back_ref, other_back_ref):
    grad = grad_ref[0]
    own_back_ref[0] = dot_nt(grad, own_ref[...]).astype(BF16)
    other_back_ref[0] = dot_nt(grad, other_ref[...]).astype(BF16)


def run_early_back(scalars, grads, weights, events=()):
    count, rows, depth = grads.shape
    half = weights["out_own"].shape[0]
    inputs = [(grads, same_slot(depth))] + constants(weights["out_own"], weights["out_other"])
    outputs = [(low(count, rows, half), same_slot(half))] * 2
    return call(
        early_back_kernel, "early_back", count, scalars, inputs, outputs, events=events, cost=20
    )


def norm_backward_kernel(scalars, x_ref, norm_ref, grad_ref, left_ref, right_ref, sum_ref, out_ref):
    depth = x_ref.shape[1]
    half = depth // 2
    squares = jnp.zeros((CHUNK, LANES), F32)
    inner = jnp.zeros((CHUNK, LANES), F32)

    def weighted(tile):
        at = tile * LANES
        source = left_ref if at < half else right_ref
        at = at % half
        return source[:, at : at + LANES] * norm_ref[0:1, tile * LANES : (tile + 1) * LANES]

    for tile in range(depth // LANES):
        x = x_ref[:, tile * LANES : (tile + 1) * LANES].astype(F32)
        squares = squares + x * x
        inner = inner + weighted(tile) * x
    scale = lax.rsqrt(jnp.sum(squares, axis=1, keepdims=True) / depth + NORM_EPSILON)
    factor = scale * scale * scale * (jnp.sum(inner, axis=1, keepdims=True) / depth)
    scale = jnp.broadcast_to(scale, (CHUNK, LANES))
    factor = jnp.broadcast_to(factor, (CHUNK, LANES))
    crossed = jnp.zeros((CHUNK, LANES), F32)
    for tile in range(depth // LANES):
        lanes = slice(tile * LANES, (tile + 1) * LANES)
        x = x_ref[:, lanes].astype(F32)
        found = (grad_ref[:CHUNK, lanes].astype(F32) + weighted(tile) * scale - x * factor).astype(BF16)
        out_ref[:CHUNK, lanes] = found
        crossed = crossed + found.astype(F32) * sum_ref[:, lanes]
    ones = jnp.ones((EXTRA, LANES), BF16)
    first, second = pieces(crossed, 2)
    out_ref[CHUNK:, :] = jnp.zeros((EXTRA, depth), BF16)
    out_ref[CHUNK:, : 3 * CHUNK] = jnp.concatenate(
        pieces(dot_nt(ones, first) + dot_nt(ones, second), 3), axis=1
    )


def run_norm_backward(scalars, x, norm, grad, dnormed, summed, events=(), cost=1):
    rows, depth = x.shape
    (found,) = call(
        norm_backward_kernel,
        "norm_backward",
        1,
        scalars,
        constants(x, norm, grad, *dnormed, summed),
        [(low(rows + EXTRA, depth), whole((rows + EXTRA, depth)))],
        events=events,
        cost=cost,
    )
    return found


def crossing(bit):
    return [(i, i ^ bit) for i in range(4)]


def exchange(block, bit):
    return lax.ppermute(block, "tensor", crossing(bit))


def swap_cores(block):
    return lax.ppermute(block, "pipe", [(0, 1), (1, 0)])


def shift_groups(block, distance):
    count = lax.axis_size("fsdp")
    return lax.ppermute(block, "fsdp", [(i, (i + distance) % count) for i in range(count)])


def after(values, *events, cost=0):
    single = not isinstance(values, (tuple, list))
    values = [values] if single else list(values)
    anywhere = pl.BlockSpec(memory_space=pl.ANY)
    found = pl.pallas_call(
        lambda *refs: None,
        out_shape=[jax.ShapeDtypeStruct(v.shape, v.dtype) for v in values],
        in_specs=[anywhere] * (len(values) + len(events)),
        out_specs=[anywhere] * len(values),
        input_output_aliases={at: at for at in range(len(values))},
        cost_estimate=pl.CostEstimate(
            flops=cost * 1_000_000_000, bytes_accessed=1, transcendentals=0
        ),
        name="fence",
    )(*values, *events)
    return found[0] if single else found


def gather_begin(block):
    return block, exchange(block, 1), exchange(block, 2)


def gather_end(begun, *others):
    block, from_1, from_2 = begun
    cols = block.shape[1] // 2
    left, right = from_1[:, :cols], from_2[:, cols:]
    if others:
        left, right = after((left, right), *others)
    left_3, right_3 = exchange(left, 2), exchange(right, 1)
    return [block, from_1, from_2, left_3, right_3]


def scatter_begin(halves):
    left, right = halves[:4], halves[4:]
    left_3, right_3 = exchange(left[3], 2), exchange(right[3], 1)
    right_1, left_2 = exchange(right[1], 1), exchange(left[2], 2)
    return left, right, left_3, right_3, right_1, left_2


def scatter_middle(begun, *others):
    left, right, left_3, right_3, right_1, left_2 = begun
    if others:
        left_3, right_3 = after((left_3, right_3), *others)
    left_1 = (left[1].astype(F32) + left_3.astype(F32)).astype(BF16)
    right_2 = (right[2].astype(F32) + right_3.astype(F32)).astype(BF16)
    sent = (left_1, right_2)
    left_1, right_2 = exchange(left_1, 1), exchange(right_2, 2)
    return (left[0], left_1, left_2, right[0], right_1, right_2), sent


def scatter_end(middle, *others):
    left_0, left_1, left_2, right_0, right_1, right_2 = middle
    if others:
        left_0 = after(left_0, *others)
    return (
        left_0.astype(F32) + left_1.astype(F32) + left_2.astype(F32),
        right_0.astype(F32) + right_1.astype(F32) + right_2.astype(F32),
    )


def sum_tensor(value):
    return value + exchange(value, 1) + exchange(value, 2) + exchange(value, 3)


def sum_groups(value, part):
    count = lax.axis_size("fsdp")
    bit = 2 if part else 1
    while bit < (count if part else 2):
        value = value + lax.ppermute(value, "fsdp", [(i, i ^ bit) for i in range(count)])
        bit *= 2
    return value


def spread_parts(value, axis_name):
    count, at = lax.axis_size(axis_name), lax.axis_index(axis_name)
    parts = [lax.dynamic_index_in_dim(value, at, 0, keepdims=False)]
    for distance in range(1, count):
        block = lax.dynamic_index_in_dim(value, (at + distance) % count, 0, keepdims=False)
        pairs = [(i, (i + distance) % count) for i in range(count)]
        parts.append(lax.ppermute(block, axis_name, pairs))
    return parts


def add_up(parts):
    total = parts[0].astype(F32)
    for part in parts[1:]:
        total = total + part.astype(F32)
    return total.astype(parts[0].dtype)


def gather_groups_begin(block):
    return [block] + [shift_groups(block, k) for k in range(1, lax.axis_size("fsdp"))]


def gather_groups_end(found, axis):
    count, place = lax.axis_size("fsdp"), lax.axis_index("fsdp")
    size = found[0].shape[axis]
    shape = list(found[0].shape)
    shape[axis] = size * count
    total = jnp.zeros(shape, found[0].dtype)
    for distance, piece in enumerate(found):
        total = lax.dynamic_update_slice_in_dim(
            total, piece, (place - distance) % count * size, axis
        )
    return total


def gather_groups(block, axis):
    return gather_groups_end(gather_groups_begin(block), axis)


def ring_groups(block, rows, waits):
    count, place = lax.axis_size("fsdp"), lax.axis_index("fsdp")
    cols = block.shape[1]
    found = jnp.zeros((rows * count, cols), block.dtype)
    packed = jnp.zeros((count, block.shape[0] - rows, cols), block.dtype)

    def put(totals, piece, at, col):
        found, packed = totals
        found = lax.dynamic_update_slice(found, piece[:rows], (at % count * rows, col))
        packed = lax.dynamic_update_slice(packed, piece[rows:][None], (at % count, 0, col))
        return found, packed

    totals = put((found, packed), block, place, 0)
    up, down = block[:, : cols // 2], block[:, cols // 2 :]
    steps = []
    for distance in range(1, count):
        if distance in waits:
            up, down = after((up, down), *waits[distance])
        up, down = shift_groups(up, 1), shift_groups(down, -1)
        steps.append(up)
        totals = put(totals, up, place - distance, 0)
        totals = put(totals, down, place + distance, cols // 2)
    return totals, steps


def rms_scale(x):
    return lax.rsqrt(jnp.mean(x * x, axis=1, keepdims=True) + NORM_EPSILON)


def channel_places(count, depth, head_count, head_size):
    size, slice_size = depth // count, head_size // count
    shared = 2 * STATE // count
    width = head_count * head_size
    places = np.zeros((depth, width + 2 * STATE), np.float32)
    for group in range(count):
        for head in range(head_count):
            for at in range(slice_size):
                lane = group * size + head * slice_size + at
                places[lane, head * head_size + group * slice_size + at] = 1
        for at in range(shared):
            lane = group * size + head_count * slice_size + at
            places[lane, width + group * shared + at] = 1
    return places


def shards(
    tokens,
    out_grad,
    seq_lengths,
    norm_gain,
    w_zx,
    w_bc,
    w_dt,
    conv_x,
    conv_bc,
    out_gain,
    head_params,
    out_weight,
):
    core = lax.axis_index("pipe")
    place = lax.axis_index("tensor")
    is_first = core == 0
    fsdp_count = lax.axis_size("fsdp")
    fsdp_at = lax.axis_index("fsdp")
    tensor_count = lax.axis_size("tensor")
    local_depth = norm_gain.shape[1]
    depth = local_depth * fsdp_count
    width = w_zx.shape[3]
    half = width // 2
    head_count = w_dt.shape[2]
    head_size = width // head_count
    local_head = conv_x.shape[3]
    local_wide = head_count * local_head
    inner_total = width * tensor_count
    joined = width + 2 * STATE
    local_rows = tokens.shape[1]
    tap_rows = conv_x.shape[1]
    places = jnp.asarray(
        channel_places(fsdp_count, depth, head_count, head_size), BF16
    )

    def by_core(first, second):
        return jnp.where(is_first, first, second)

    def local_order(value):
        size = value.shape[-1] // 2
        return by_core(
            value, jnp.concatenate([value[..., size:], value[..., :size]], axis=-1)
        )

    def micro(array):
        return lax.dynamic_index_in_dim(array, core, 0, keepdims=False)

    def pad_to(value, rows, cols):
        return jnp.pad(value, ((0, rows - value.shape[0]), (0, cols - value.shape[1])))

    lengths = lax.dynamic_index_in_dim(seq_lengths, core, 0, keepdims=False)[0]
    scalars = jnp.stack([core, lengths[0], lengths[0] + lengths[1], place]).astype(jnp.int32)

    heads, left_over = [], head_params[0]
    for _ in range(3):
        part = lax.reduce_precision(left_over, 8, 7)
        heads.append(part.astype(BF16))
        left_over = left_over - part
    heads = jnp.concatenate(heads)
    packed = jnp.concatenate(
        [
            pad_to(w_dt[0].T, 16, local_depth),
            pad_to(
                jnp.concatenate([conv_x[0].reshape(tap_rows, local_wide), conv_bc[0]], axis=1),
                tap_rows,
                local_depth,
            ),
            pad_to(out_gain[0].reshape(1, local_wide), 1, local_depth),
            norm_gain,
            pad_to(heads, 16 - tap_rows - 2, local_depth),
        ]
    )

    def shared_half(which):
        weights = jnp.concatenate(
            [
                lax.dynamic_slice(w_zx, (0, 0, 1, which * half), (1, local_depth, 1, half))[
                    0, :, 0
                ],
                lax.dynamic_slice_in_dim(w_bc[0], which * STATE, STATE, 1),
            ],
            axis=1,
        )
        rows = lax.dynamic_slice_in_dim(packed, which * 16, 16, 0)
        return jnp.concatenate([weights, pad_to(rows, 16, half + STATE)])

    def gate_half(which):
        return lax.dynamic_slice(w_zx, (0, 0, 0, which * half), (1, local_depth, 1, half))[
            0, :, 0
        ]

    def out_half(which):
        return lax.dynamic_slice_in_dim(out_weight[0], which * half, half, 0)

    shared_theirs = swap_cores(shared_half(1 - core))
    begun = gather_begin(micro(tokens))
    shared_mine = shared_half(core)
    first, second = {}, {}
    cotangent = micro(out_grad)
    blocks = gather_end(begun)
    natural_cotangent = lax.all_gather(
        after(cotangent, *blocks[3:]), "tensor", axis=0, tiled=True
    ).reshape(-1, CHUNK, depth)
    (first["own"], packed_own), steps = ring_groups(
        jnp.concatenate(
            [
                by_core(shared_mine, shared_theirs),
                by_core(shared_theirs, shared_mine)[local_depth:],
            ]
        ),
        local_depth,
        {2: begun[1:]},
    )
    first["other"] = swap_cores(first["own"])

    packed_other = swap_cores(packed_own)

    def small_weights(weights, own, other):
        steps_part, wide_part = [
            jnp.moveaxis(part[:, :, :local_depth], 0, 1).reshape(16, depth)
            for part in (by_core(own, other), by_core(other, own))
        ]
        wide = dot(wide_part[:8], places)
        weights["wide"] = jnp.concatenate([local_order(wide[:, :width]), wide[:, width:]], axis=1)
        weights["step"] = by_core(
            steps_part,
            jnp.concatenate(
                [
                    steps_part[head_count // 2 : head_count],
                    steps_part[: head_count // 2],
                    steps_part[head_count:],
                ]
            ),
        )
        weights["norm"] = wide_part[tap_rows + 1 : tap_rows + 9].astype(F32)
        heads = wide_part[tap_rows + 2 :, :head_count].astype(F32).reshape(3, 3, head_count)
        weights["head"] = pad_to(local_order(heads[0] + (heads[1] + heads[2])), 8, LANES)

    small_weights(first, packed_own[:, :16], packed_other[:, :16])
    small_weights(second, packed_own[:, 16:], packed_other[:, 16:])

    gate_mine, gate_theirs = gate_half(core), gate_half(1 - core)
    out_mine, out_theirs = out_half(core), out_half(1 - core)
    if local_depth == half:
        both = swap_cores(
            after(jnp.concatenate([gate_theirs, out_theirs], axis=1), *begun[1:])
        )
        gate_theirs, out_theirs = both[:, :half], both[:, half:]
    else:
        gate_theirs, out_theirs = swap_cores(gate_theirs), swap_cores(out_theirs)
    gate_begun = gather_groups_begin(after(by_core(gate_mine, gate_theirs), steps[-1]))

    slots, conv, inputs, y, raw, states = run_mixer(scalars, blocks, first)
    kept_first = (conv, inputs, raw, states)
    first["gate_own"] = gather_groups_end(after(gate_begun, y), 0)
    first["gate_other"] = swap_cores(first["gate_own"])
    out_block = after(by_core(out_mine, out_theirs), y, *gate_begun[1:])
    out_begun = gather_groups_begin(out_block)
    z, hidden, sums = run_gate(scalars, slots, y, first)
    joined_block = after(
        jnp.concatenate(
            [
                by_core(shared_theirs, shared_mine)[:local_depth],
                by_core(gate_theirs, gate_mine),
            ],
            axis=1,
        ),
        hidden,
        *out_begun[1:],
    )
    joined_second = lax.all_gather(joined_block, "fsdp", axis=0, tiled=True)
    second["out_own"] = lax.all_gather(
        after(by_core(out_theirs, out_mine), joined_block), "fsdp", axis=1, tiled=True
    )
    first_saved = (slots, z, y)
    sums = sum_tensor(sums[:1])[0]
    scale_first = lax.rsqrt(sums / inner_total + NORM_EPSILON)
    own_scale = lax.dynamic_slice_in_dim(scale_first, place * local_rows, local_rows, 0)
    first["out_own"] = gather_groups_end(after(out_begun, hidden), 1)
    first["out_other"] = swap_cores(first["out_own"])
    outputs = run_project(scalars, hidden, first, events=(scale_first, natural_cotangent))
    scatter_state, _ = scatter_middle(scatter_begin(outputs))
    summed = jnp.concatenate(scatter_end(scatter_state), axis=1)
    x_0 = micro(tokens).astype(F32)
    y_first = (x_0 + summed * own_scale[:, None]).astype(BF16)
    begun = gather_begin(y_first)
    joined_second = after(joined_second, *begun[1:])
    second["own"] = second["gate_own"] = joined_second
    second["other"] = second["gate_other"] = swap_cores(joined_second)
    blocks = gather_end(begun)

    slots, conv, inputs, y, raw, states = run_mixer(scalars, blocks, second)
    kept_second = (conv, inputs, raw, states)
    second["out_own"] = after(second["out_own"], y)
    second["out_other"] = swap_cores(second["out_own"])
    z, hidden_second, squares = run_gate(scalars, slots, y, second)
    *outputs, crossed = run_project(
        scalars, hidden_second, second, natural_cotangent
    )
    sums = sum_tensor(jnp.concatenate([squares[:1], crossed[:1]]))
    early_backs = run_early_back(
        scalars, natural_cotangent, second, events=(crossed,)
    )
    scale_second = lax.rsqrt(sums[0] / inner_total + NORM_EPSILON)
    own_scale = lax.dynamic_slice_in_dim(scale_second, place * local_rows, local_rows, 0)

    def both_micros(one, two):
        keep, send = by_core(one, two), by_core(two, one)
        got = swap_cores(send)
        return jnp.stack([by_core(keep, got), by_core(got, keep)])[None]

    def both_halves(one, two):
        keep, send = by_core(one, two), by_core(two, one)
        got = swap_cores(send)
        return by_core(keep, got), by_core(got, keep)

    def add_cores(own, got):
        return (own.astype(F32) + got.astype(F32)).astype(BF16)

    def rows_of(value):
        return value.reshape(-1, value.shape[-1])

    own_gate, other_gate, hidden, grad_y, gain_grad = run_gate_backward(
        scalars,
        early_backs,
        jnp.pad(jnp.stack([scale_second, sums[1]]), ((0, 6), (0, 0))),
        second,
        z,
        y,
        inner_total,
    )
    y_parts = [
        exchange(part, at) for at, part in zip(range(1, 4), after(outputs[1:], sums))
    ]
    *backs, own_grad, other_grad, small_second = run_mixer_backward(
        scalars, grad_y, [own_gate, other_gate], gain_grad, second, slots, kept_second
    )
    scatter_state = scatter_begin(backs)
    in_own, in_other = run_weight_grad(
        scalars, slots, [own_gate, other_gate, own_grad, other_grad], events=y_parts
    )
    scatter_state, sent = scatter_middle(scatter_state, in_other)
    in_other = after(in_other, *sent)
    in_sum = add_cores(in_own, swap_cores(in_other))
    in_second = in_sum[:, :width]
    shared_second = in_sum[:, width:]
    dnormed = scatter_end(scatter_state, in_second)
    in_second = lax.psum_scatter(in_second, "fsdp", scatter_dimension=0, tiled=True)
    grad_second = run_norm_backward(
        scalars, y_first, second["norm"], cotangent, dnormed, summed
    )
    begun = gather_begin(grad_second)
    out_own, out_other = run_weight_grad(
        scalars, None, [], natural_cotangent, hidden, events=(grad_second,)
    )
    out_other, from_1, from_2 = after((out_other, *begun[1:]))
    blocks = gather_end((begun[0], from_1, from_2))
    out_own_second = out_own

    slots, z, y = first_saved
    own_gate, other_gate, hidden, grad_y, gain_grad, grads = run_gate_backward(
        scalars,
        blocks,
        jnp.pad(scale_first[None], ((0, 7), (0, 0))),
        first,
        z,
        y,
        inner_total,
    )
    out_sum = add_cores(out_own_second, swap_cores(after(out_other, grad_y)))
    out_second = lax.psum_scatter(out_sum, "fsdp", scatter_dimension=0, tiled=True)
    gate_own, gate_other = run_weight_grad(
        scalars, slots, [own_gate, other_gate], grads, hidden, events=(in_second,), cost=1
    )
    gate_sum = add_cores(gate_own, swap_cores(gate_other))
    gate_first = lax.psum_scatter(gate_sum, "fsdp", scatter_dimension=0, tiled=True)
    *backs, own_grad, other_grad, small_first = run_mixer_backward(
        scalars,
        grad_y,
        [own_gate, other_gate],
        gain_grad,
        first,
        slots,
        kept_first,
        events=(gate_sum,),
    )
    left, right, left_3, right_3, right_1, left_2 = scatter_begin(backs)
    ours = by_core(small_first, small_second) + swap_cores(by_core(small_second, small_first))
    shared_own, shared_other = run_weight_grad(
        scalars, slots, [own_grad, other_grad], cost=1
    )
    left_3, right_3, ours, shared_other = after((left_3, right_3, ours, shared_other))
    left_1 = exchange((left[1].astype(F32) + left_3.astype(F32)).astype(BF16), 1)
    right_2 = exchange((right[2].astype(F32) + right_3.astype(F32)).astype(BF16), 2)
    shared_got = swap_cores(shared_other)
    ours = sum_groups(ours, 0)
    shared_sum = add_cores(shared_own, shared_got)
    conv_sum = after(shared_sum[:, :half], gate_first, out_second)
    conv_first = lax.psum_scatter(conv_sum, "fsdp", scatter_dimension=0, tiled=True)
    ours, shared_sum = after((ours, shared_sum[:, half:]), conv_sum)
    shared_low, shared_high = both_halves(shared_sum, shared_second)
    total = sum_groups(ours, 1)
    dnormed = scatter_end((left[0], left_1, left_2, right[0], right_1, right_2))
    grad_first = run_norm_backward(
        scalars,
        lax.dynamic_index_in_dim(tokens, core, 0, keepdims=False),
        first["norm"],
        grad_second,
        dnormed,
        summed,
    )
    grad_bc = jnp.concatenate([shared_low, shared_high], axis=1).reshape(
        fsdp_count, tensor_count, -1, 2 * STATE
    )
    grad_bc, total, grad_first = after((jnp.moveaxis(grad_bc, 1, 0), total, grad_first))
    input_out = both_micros(grad_first, grad_second)[:, :, :local_rows]
    rows = lax.dynamic_slice_in_dim(total[:24], fsdp_at * local_depth, local_depth, 1)
    wide = total[24:, :joined]
    everywhere = sum_tensor(
        jnp.concatenate([rows[16:17], wide[:5, width:].reshape(1, -1)], axis=1)
    )[0]
    grad_bc = add_up(spread_parts(grad_bc, "tensor"))
    grad_bc = add_up(spread_parts(grad_bc, "fsdp"))
    second_parts = jnp.concatenate([in_second[:, :half], out_second], axis=1)
    low_half, high_half = both_halves(after(gate_first, total), second_parts)
    y_summed = after(outputs[0], total).astype(F32)
    for part in y_parts:
        y_summed = y_summed + part.astype(F32)
    y_second = (y_first.astype(F32) + y_summed * own_scale[:, None]).astype(BF16)
    section_out = both_micros(y_first, y_second)
    grad_out_weight = jnp.concatenate(
        [low_half[:, half:].T, high_half[:, half:].T], axis=0
    ).astype(F32)
    conv_low, conv_high = both_halves(conv_first, in_second[:, half:])
    grad_zx = jnp.stack(
        [
            jnp.concatenate([low_half[:, :half], high_half[:, :half]], axis=1),
            jnp.concatenate([conv_low, conv_high], axis=1),
        ],
        axis=1,
    ).astype(F32)

    by_head = lax.dynamic_slice_in_dim(
        wide[:7, :width].reshape(7, head_count, head_size), fsdp_at * local_head, local_head, 2
    )
    grad_heads = jnp.concatenate(
        [
            wide[7:8, :head_count],
            wide[7:8, LANES : LANES + head_count],
            jnp.sum(wide[6, :width].reshape(1, head_count, head_size), axis=2),
        ]
    )
    grad_dt = rows[:head_count].T
    gain_size = local_depth // tensor_count
    grad_gain = lax.dynamic_slice_in_dim(everywhere, place * gain_size, gain_size, 0)
    shared_size = 2 * STATE // (fsdp_count * tensor_count)
    grad_shared = lax.dynamic_slice_in_dim(
        everywhere[local_depth:].reshape(tap_rows, -1), (fsdp_at * tensor_count + place) * shared_size, shared_size, 1
    )
    return (
        section_out,
        input_out,
        grad_gain[None],
        grad_zx[None],
        grad_bc.astype(F32)[None],
        grad_dt[None],
        by_head[:tap_rows][None],
        grad_shared[None],
        by_head[5][None],
        grad_heads[None],
        grad_out_weight[None],
    )


def solution(mesh):
    return jax.shard_map(
        shards,
        mesh=mesh,
        in_specs=(
            P(None, ("fsdp", "tensor"), None),
            P(None, ("fsdp", "tensor"), None),
            P(None, "fsdp", None),
            P("pipe", "fsdp"),
            P("pipe", "fsdp", None, "tensor"),
            P("pipe", "fsdp", None),
            P("pipe", "fsdp", "tensor"),
            P("pipe", None, "tensor", "fsdp"),
            P("pipe", None, "fsdp"),
            P("pipe", "tensor", "fsdp"),
            P("pipe", None, "tensor"),
            P("pipe", "tensor", "fsdp"),
        ),
        out_specs=(
            P("pipe", None, ("fsdp", "tensor"), None),
            P("pipe", None, ("fsdp", "tensor"), None),
            P("pipe", ("fsdp", "tensor")),
            P("pipe", "fsdp", None, "tensor"),
            P("pipe", ("fsdp", "tensor"), None),
            P("pipe", "fsdp", "tensor"),
            P("pipe", None, "tensor", "fsdp"),
            P("pipe", None, ("fsdp", "tensor")),
            P("pipe", "tensor", "fsdp"),
            P("pipe", None, "tensor"),
            P("pipe", "tensor", "fsdp"),
        ),
        check_vma=False,
    )
```

time: 744 us -> 617 us (0.83)
  waiting for transfers between devices: 243 us -> 144 us
  Pallas kernels: 133 us -> 230 us
  blocking collectives: 65.7 us -> 0 us
  starting transfers between devices: 43.2 us -> 82.6 us
  other arithmetic: 93.1 us -> 59 us
  matrix products: 37.4 us -> 5.03 us
  local copies, waits for them, and re-layouts: 100 us -> 71.1 us
    pallas_call x4 -> x40, Pallas kernels: 133 us -> 230 us  [the longest x17 230 us: call(): pl.pallas_call(body, grid_spec=pltpu.PrefetchScalarGridSpec(num_scalar_pr...]
    reduce_scatter x3 -> x4, waiting for transfers between devices: 91.6 us -> 4.39 us  [the longest x1 4.37 us: shards(): lax.psum_scatter(in_second, 'fsdp', scatter_dimension=0, tiled=True)]
    ppermute x0 -> x20, waiting for transfers between devices: none -> 54.5 us  [the longest x12 25.1 us: shift_groups(): lax.ppermute(block, 'fsdp', [(i, (i + distance) % count) for i in range(c...]
    psum x1 -> x0, blocking collectives: 43.6 us -> none  [shards(): lax.psum(jnp.concatenate([a.reshape(-1) for a in shared_small]), ('pipe',...]
    ppermute x36 -> x42, waiting for transfers between devices: 114 us -> 74.7 us  [exchange(): return lax.ppermute(block, 'tensor', crossing(bit))]
    another operation x34 -> x3, other arithmetic: 37.5 us -> 0.72 us  [the longest x1 0.62 us: shards(): jnp.stack([scale_second, sums[1]])]
    all_gather x4 -> x3, waiting for transfers between devices: 36.8 us -> 4.44 us  [the longest x1 4.44 us: shards(): lax.all_gather(after(by_core(out_theirs, out_mine), joined_block), 'fsdp'...]
    dot_general x10 -> x2, matrix products: 37.4 us -> 5.03 us  [dot(): lax.dot_general(a, b, (((1,), (0,)), ((), ())), preferred_element_type=F32)]
  transfers between devices with their start and end apart: 62 -> 87, of which waited for: 30 -> 37; matrix products, arithmetic and copies ran while one was open for 29% -> 17% of each run, Pallas kernels for 9% -> 35%
where the time goes in v2:
time: 617 us; the launch traced here: 609 us
  Pallas kernels  230 us (37%)
  waiting for transfers between devices  144 us (23%)
  starting transfers between devices  82.6 us (13%)
  local copies, waits for them, and re-layouts  71.1 us (12%)
  other arithmetic  59 us (10%)
  between operations  17.4 us (3%)
    pallas_call x17, Pallas kernels, call(): pl.pallas_call(body, grid_spec=pltpu.PrefetchScalarGridSpec(num_scalar_pr...  230 us
    ppermute x42, waiting for transfers between devices, exchange(): return lax.ppermute(block, 'tensor', crossing(bit))  74.7 us
    ppermute x42, starting transfers between devices, exchange(): return lax.ppermute(block, 'tensor', crossing(bit))  48.2 us
    unnamed x213, local copies, waits for them, and re-layouts  31.1 us
    ppermute x12, waiting for transfers between devices, shift_groups(): lax.ppermute(block, 'fsdp', [(i, (i + distance) % count) for i in range(c...  25.1 us
    ppermute x12, starting transfers between devices, shift_groups(): lax.ppermute(block, 'fsdp', [(i, (i + distance) % count) for i in range(c...  24.9 us
    ppermute x2, waiting for transfers between devices, sum_groups(): lax.ppermute(value, 'fsdp', [(i, i ^ bit) for i in range(count)])  16 us
    ppermute x6, waiting for transfers between devices, spread_parts(): parts.append(lax.ppermute(block, axis_name, pairs))  13.4 us
  transfers between devices with their start and end apart: 87, of which 37 were waited for; matrix products, arithmetic and copies ran while one was open for 17% of the time, Pallas kernels for 35%

profile of v2, /device:TPU:0, one launch (start us, length us, event | category | flops | bytes accessed | tf_op | source)
XLA Modules:
  0.0 609.1 jit_solution(14111215053409702666)
XLA Ops:
  9.4 2.9 collective-permute-start
  14.2 5.9 constant_dynamic-slice_fusion.6
  33.3 5.9 collective-permute-done.5.refs_0_
  39.2 3.6 collective-permute-done.6.refs_1_
  52.9 2.7 collective-permute-start.8
  56.5 4.6 collective-permute-done.8
  61.2 4.3 collective-permute-start.10
  66.3 3.0 collective-permute-done.10
  82.0 3.9 collective-permute-start.15
  86.4 20.3 %mixer.2 = (bf16[4,256,1536]{2,1,0:T(8,128)(2,1)}, bf16[4,256,1024]{2,1,0:T(8,128)(2,1)}, bf16[4,256,1024]{2,1,0:T(8,128)(2,1)}, bf16[4,256,768]{2,1,0:T(8,128)(...) custom-call(s32[4]{0:T(128)} %pad_add_fusion.scalars, bf16[256,1536]{1,0:T(8,128)(2,1)} %dynamic-slice_bitcast_fusion.1.refs_0_, ...), custom_call_target="tpu_custom_call" | custom-call | flops 99999997952 | bytes 1 | tf_op jit(solution)/shard_map/mixer/pallas_call | solution.py:697
  110.2 5.8 collective-permute-start.18
  119.5 8.5 %gate.2 = (bf16[4,256,768]{2,1,0:T(8,128)(2,1)}, bf16[4,256,768]{2,1,0:T(8,128)(2,1)}, f32[8,1024]{1,0:T(8,128)}) custom-call(s32[4]{0:T(128)} %pad_add_fusion.scalars, bf16[4,256,1536]{2,1,0:T(8,128)(2,1)} %get-tuple-element.114.refs_0_.refs_12_, bf16[1536,384]{1,0:T(8,128)(2,1)} %copy-done.54, bf16[1536,384]{1,0:T(8,128)(2,1)} %copy-done.93, ...), custom_call_target="tpu_custom_call" | custom-call | flops 20000000000 | bytes 1 | tf_op jit(solution)/shard_map/gate/pallas_call | solution.py:697
  128.0 8.0 %collective-permute-done.19.refs_2_.refs_3_ = bf16[384,384]{1,0:T(8,128)(2,1)S(1)} collective-permute-done((bf16[384,384]{1,0:T(8,128)(2,1)S(1)}, bf16[384,384]{1,0:T(8,128)(2,1)S(1)}, u32[]{:S(2)}, u32[]{:S(2)}) %collective-permute-start.19) | collective-permute-done | bytes 294944 | tf_op jit(solution)/shard_map/ppermute | solution.py:1016
  148.2 8.4 %project.2 = (bf16[256,768]{1,0:T(8,128)(2,1)}, bf16[256,768]{1,0:T(8,128)(2,1)}, bf16[256,768]{1,0:T(8,128)(2,1)}, bf16[256,768]{1,0:T(8,128)(2,1)}, bf16[256,7...) custom-call(s32[4]{0:T(128)} %pad_add_fusion.scalars, ...), custom_call_target="tpu_custom_call" | custom-call | flops 1000000000 | bytes 1 | tf_op jit(solution)/shard_map/project/pallas_call | solution.py:697
  160.2 8.7 %collective-permute-done.29 = bf16[256,768]{1,0:T(8,128)(2,1)S(1)} collective-permute-done((bf16[256,768]{1,0:T(8,128)(2,1)}, bf16[256,768]{1,0:T(8,128)(2,1)S(1)}, u32[]{:S(2)}, u32[]{:S(2)}) %collective-permute-start.29) | collective-permute-done | bytes 393248 | tf_op jit(solution)/shard_map/ppermute | solution.py:1007
  174.5 2.8 collective-permute-done.28
  177.3 3.6 collective-permute-done.30
  181.1 4.1 collective-permute-done.27
  190.3 13.1 %collective-permute-done.31.refs_1_ = bf16[256,1536]{1,0:T(8,128)(2,1)S(1)} collective-permute-done((bf16[256,1536]{1,0:T(8,128)(2,1)S(1)}, bf16[256,1536]{1,0:T(8,128)(2,1)S(1)}, u32[]{:S(2)}, u32[]{:S(2)}) %collective-permute-start.31) | collective-permute-done | bytes 786464 | tf_op jit(solution)/shard_map/ppermute | solution.py:1007
  213.3 8.0 %collective-permute-done.33.refs_3_ = bf16[256,768]{1,0:T(8,128)(2,1)S(1)} collective-permute-done((bf16[256,768]{1,0:T(8,128)(2,1)S(1)}, bf16[256,768]{1,0:T(8,128)(2,1)S(1)}, u32[]{:S(2)}, u32[]{:S(2)}) %collective-permute-start.33) | collective-permute-done | bytes 393248 | tf_op jit(solution)/shard_map/ppermute | solution.py:1007
  223.5 20.8 %mixer.3 = (bf16[4,256,1536]{2,1,0:T(8,128)(2,1)}, bf16[4,256,1024]{2,1,0:T(8,128)(2,1)}, bf16[4,256,1024]{2,1,0:T(8,128)(2,1)}, bf16[4,256,768]{2,1,0:T(8,128)(...) custom-call(s32[4]{0:T(128)} %pad_add_fusion.scalars, bf16[256,1536]{1,0:T(8,128)(2,1)} %copy-done.5, ...), custom_call_target="tpu_custom_call" | custom-call | flops 99999997952 | bytes 1 | tf_op jit(solution)/shard_map/mixer/pallas_call | solution.py:697
  244.3 4.4 all-gather.8.cloned.1.call-done.refs_0_
  248.7 9.6 %gate.3 = (bf16[4,256,768]{2,1,0:T(8,128)(2,1)}, bf16[4,256,768]{2,1,0:T(8,128)(2,1)}, f32[8,1024]{1,0:T(8,128)}) custom-call(s32[4]{0:T(128)} %pad_add_fusion.scalars, bf16[4,256,1536]{2,1,0:T(8,128)(2,1)} %get-tuple-element.134.refs_0_.refs_12_, bf16[1536,896]{1,0:T(8,128)(2,1)} %fence.31.refs_5_.refs_1_.refs_3_, ...), custom_call_target="tpu_custom_call" | custom-call | flops 20000000000 | bytes 1 | tf_op jit(solution)/shard_map/gate/pallas_call | solution.py:697
  260.1 9.4 %project.3 = (bf16[256,1536]{1,0:T(8,128)(2,1)}, bf16[256,1536]{1,0:T(8,128)(2,1)}, bf16[256,1536]{1,0:T(8,128)(2,1)}, bf16[256,1536]{1,0:T(8,128)(2,1)}, f32[8,1024]{1,0:T(8,128)}) custom-call(s32[4]{0:T(128)} %pad_add_fusion.scalars, bf16[4,256,768]{2,1,0:T(8,128)(2,1)} %get-tuple-element.136.refs_0_, bf16[384,1536]{1,0:T(8,128)(2,1)} %fence.33.refs_1_, ...), custom_call_target="tpu_custom_call" | custom-call | flops 20000000000 | bytes 1 | tf_op jit(solution)/shard_map/project/pallas_call | solution.py:697
  273.8 7.5 %early_back.1 = (bf16[4,256,384]{2,1,0:T(8,128)(2,1)}, bf16[4,256,384]{2,1,0:T(8,128)(2,1)}) custom-call(s32[4]{0:T(128)} %pad_add_fusion.scalars, bf16[4,256,1536]{2,1,0:T(8,128)(2,1)} %bitcast.182, bf16[384,1536]{1,0:T(8,128)(2,1)} %fence.33.refs_1_, bf16[384,1536]{1,0:T(8,128)(2,1)} %copy-done.94, f32[8,1024]{1,0:T(8,128)} %get-tuple-element.138.refs_3_), custom_call_target="tpu_custom_call" | custom-call | flops 20000000000 | bytes 1 | tf_op jit(solution)/shard_map/early_back/pallas_call | solution.py:697
  286.1 7.6 %gate_backward.2 = (bf16[4,256,384]{2,1,0:T(8,128)(2,1)}, bf16[4,256,384]{2,1,0:T(8,128)(2,1)}, bf16[4,256,768]{2,1,0:T(8,128)(2,1)}, bf16[4,256,768]{2,1,0:T(8,128)(2,1)}, f32[8,768]{1,0:T(8,128)}) custom-call(s32[4]{0:T(128)} %pad_add_fusion.scalars, bf16[4,256,384]{2,1,0:T(8,128)(2,1)} %get-tuple-element.139.refs_0_, ...), custom_call_target="tpu_custom_call" | custom-call | flops 1000000000 | bytes 1 | tf_op jit(solution)/shard_map/gate_backward/pallas_call | solution.py:697
  293.6 39.6 %mixer_backward.2 = (bf16[256,768]{1,0:T(8,128)(2,1)}, bf16[256,768]{1,0:T(8,128)(2,1)}, bf16[256,768]{1,0:T(8,128)(2,1)}, bf16[256,768]{1,0:T(8,128)(2,1)}, bf1...) custom-call(s32[4]{0:T(128)} %pad_add_fusion.scalars, ...), custom_call_target="tpu_custom_call" | custom-call | flops 99999997952 | bytes 1 | tf_op jit(solution)/shard_map/mixer_backward/pallas_call | solution.py:697
  337.7 11.2 %weight_grad.4 = (bf16[1536,896]{1,0:T(8,128)(2,1)}, bf16[1536,896]{1,0:T(8,128)(2,1)}) custom-call(s32[4]{0:T(128)} %pad_add_fusion.scalars, bf16[4,256,1536]{2,1,0:T(8,128)(2,1)} %get-tuple-element.134.refs_0_.refs_12_, bf16[4,256,384]{2,1,0:T(8,128)(2,1)} %get-tuple-element.144.refs_1_, bf16[4,256,384]{2,1,0:T(8,128)(2,1)} %get-tuple-element.145.refs_2_, ...), custom_call_target="tpu_custom_call" | custom-call | flops 99999997952 | bytes 1 | tf_op jit(solution)/shard_map/weight_grad/pallas_call | solution.py:697
  359.5 8.0 %collective-permute-done.48 = bf16[256,768]{1,0:T(8,128)(2,1)S(1)} collective-permute-done((bf16[256,768]{1,0:T(8,128)(2,1)S(1)}, bf16[256,768]{1,0:T(8,128)(2,1)S(1)}, u32[]{:S(2)}, u32[]{:S(2)}) %collective-permute-start.48) | collective-permute-done | bytes 393248 | tf_op jit(solution)/shard_map/ppermute | solution.py:1007
  376.9 5.1 norm_backward.2.refs_2_.refs_0_
  384.4 7.4 %weight_grad.5 = (bf16[1536,384]{1,0:T(8,128)(2,1)}, bf16[1536,384]{1,0:T(8,128)(2,1)}) custom-call(s32[4]{0:T(128)} %pad_add_fusion.scalars, bf16[4,256,1536]{2,1,0:T(8,128)(2,1)} %bitcast.183, bf16[4,256,768]{2,1,0:T(8,128)(2,1)} %get-tuple-element.171.refs_1_, bf16[272,1536]{1,0:T(8,128)(2,1)} %norm_backward.2.refs_2_.refs_0_), custom_call_target="tpu_custom_call" | custom-call | flops 99999997952 | bytes 1 | tf_op jit(solution)/shard_map/weight_grad/pallas_call | solution.py:697
  391.8 9.3 %collective-permute-done.50.refs_1_ = bf16[272,1536]{1,0:T(8,128)(2,1)S(1)} collective-permute-done((bf16[272,1536]{1,0:T(8,128)(2,1)}, bf16[272,1536]{1,0:T(8,128)(2,1)S(1)}, u32[]{:S(2)}, u32[]{:S(2)}) %collective-permute-start.50) | collective-permute-done | bytes 835616 | tf_op jit(solution)/shard_map/ppermute | solution.py:1007
  407.0 6.0 collective-permute-done.52.refs_3_
  415.1 12.8 %gate_backward.3 = (bf16[4,256,384]{2,1,0:T(8,128)(2,1)}, bf16[4,256,384]{2,1,0:T(8,128)(2,1)}, bf16[4,256,768]{2,1,0:T(8,128)(2,1)}, bf16[4,256,768]{2,1,0:T(8,...) custom-call(s32[4]{0:T(128)} %pad_add_fusion.scalars, bf16[272,1536]{1,0:T(8,128)(2,1)} %norm_backward.2.refs_2_.refs_0_, ...), custom_call_target="tpu_custom_call" | custom-call | flops 1000000000 | bytes 1 | tf_op jit(solution)/shard_map/gate_backward/pallas_call | solution.py:697
  428.0 4.4 reduce-scatter.5.cloned.1.call-done.refs_5_
  432.4 11.4 %weight_grad.6 = (bf16[1536,768]{1,0:T(8,128)(2,1)}, bf16[1536,768]{1,0:T(8,128)(2,1)}) custom-call(s32[4]{0:T(128)} %pad_add_fusion.scalars, bf16[4,256,1536]{2,1,0:T(8,128)(2,1)} %get-tuple-element.114.refs_0_.refs_12_, bf16[4,256,384]{2,1,0:T(8,128)(2,1)} %get-tuple-element.177.refs_1_, bf16[4,256,384]{2,1,0:T(8,128)(2,1)} %get-tuple-element.178.refs_2_, ...), custom_call_target="tpu_custom_call" | custom-call | flops 1000000000 | bytes 1 | tf_op jit(solution)/shard_map/weight_grad/pallas_call | solution.py:697
  445.2 3.5 collective-permute-done.54
  448.6 4.4 add_convert_fusion.1.refs_17_
  453.1 37.7 %mixer_backward.3 = (bf16[256,768]{1,0:T(8,128)(2,1)}, bf16[256,768]{1,0:T(8,128)(2,1)}, bf16[256,768]{1,0:T(8,128)(2,1)}, bf16[256,768]{1,0:T(8,128)(2,1)}, bf1...) custom-call(s32[4]{0:T(128)} %pad_add_fusion.scalars, ...), custom_call_target="tpu_custom_call" | custom-call | flops 99999997952 | bytes 1 | tf_op jit(solution)/shard_map/mixer_backward/pallas_call | solution.py:697
  494.9 7.9 %weight_grad.7 = (bf16[1536,512]{1,0:T(8,128)(2,1)}, bf16[1536,512]{1,0:T(8,128)(2,1)}) custom-call(s32[4]{0:T(128)} %pad_add_fusion.scalars, bf16[4,256,1536]{2,1,0:T(8,128)(2,1)} %get-tuple-element.114.refs_0_.refs_12_, bf16[4,256,512]{2,1,0:T(8,128)(2,1)} %get-tuple-element.192.refs_1_, bf16[4,256,512]{2,1,0:T(8,128)(2,1)} %get-tuple-element.193.refs_2_), custom_call_target="tpu_custom_call" | custom-call | flops 1000000000 | bytes 1 | tf_op jit(solution)/shard_map/weight_grad/pallas_call | solution.py:697
  511.1 12.9 %collective-permute-done.58 = f32[32,1536]{1,0:T(8,128)S(1)} collective-permute-done((f32[32,1536]{1,0:T(8,128)}, f32[32,1536]{1,0:T(8,128)S(1)}, u32[]{:S(2)}, u32[]{:S(2)}) %collective-permute-start.58) | collective-permute-done | bytes 196640 | tf_op jit(solution)/shard_map/ppermute | solution.py:1087
  537.4 5.0 norm_backward.3.refs_2_
  542.4 3.0 collective-permute-done.62
  556.9 3.5 broadcast_select_fusion.2
  568.8 5.6 collective-permute-done.76
  574.4 3.7 collective-permute-done.75
  584.1 2.6 collective-permute-done.78
  597.4 3.2 copy.85
  (558 shorter events, 195.9 us)
Async XLA Ops:
  7.2 139.9 %all-gather.4.cloned.1.call-start = ((), (), s32[]{:S(2)}) async-start(), calls=%async_computation.4 | async-start | bytes 3932160 | tf_op jit(solution)/shard_map/all_gather | solution.py:1276
  9.4 33.5 %collective-permute-start = (bf16[256,1536]{1,0:T(8,128)(2,1)}, bf16[256,1536]{1,0:T(8,128)(2,1)S(1)}, u32[]{:S(2)}, u32[]{:S(2)}) collective-permute-start(bf16[256,1536]{1,0:T(8,128)(2,1)} %dynamic-slice_bitcast_fusion.1.refs_0_), channel_id=1, source_target_pairs={{0,1},{1,0},{2,3},{3,2},{4,5},{5,4},{6,7},{7,6},{8,9},{9,8},{10,11... | collective-permute-start | bytes 2359304 | tf_op jit(solution)/shard_map/ppermute | solution.py:1007
  12.4 31.7 %collective-permute-start.1 = (bf16[256,1536]{1,0:T(8,128)(2,1)}, bf16[256,1536]{1,0:T(8,128)(2,1)}, u32[]{:S(2)}, u32[]{:S(2)}) collective-permute-start(bf16[256,1536]{1,0:T(8,128)(2,1)} %dynamic-slice_bitcast_fusion.1.refs_0_), channel_id=1, source_target_pairs={{0,2},{1,3},{2,0},{3,1},{4,6},{5,7},{6,4},{7,5},{8,10},{9,11},{10,... | collective-permute-start | bytes 2359304 | tf_op jit(solution)/shard_map/ppermute | solution.py:1007
  50.0 16.2 %collective-permute-start.2 = (bf16[256,768]{1,0:T(8,128)(2,1)}, bf16[256,768]{1,0:T(8,128)(2,1)}, u32[]{:S(2)}, u32[]{:S(2)}) collective-permute-start(bf16[256,768]{1,0:T(8,128)(2,1)} %slice.429), channel_id=1, source_target_pairs={{0,2},{1,3},{2,0},{3,1},{4,6},{5,7},{6,4},{7,5},{8,10},{9,11},{10,... | collective-permute-start | bytes 1179656 | tf_op jit(solution)/shard_map/ppermute | solution.py:1007
  52.3 13.9 %collective-permute-start.3 = (bf16[256,768]{1,0:T(8,128)(2,1)}, bf16[256,768]{1,0:T(8,128)(2,1)}, u32[]{:S(2)}, u32[]{:S(2)}) collective-permute-start(bf16[256,768]{1,0:T(8,128)(2,1)} %slice.430), channel_id=1, source_target_pairs={{0,1},{1,0},{2,3},{3,2},{4,5},{5,4},{6,7},{7,6},{8,9},{9,8},{10,11... | collective-permute-start | bytes 1179656 | tf_op jit(solution)/shard_map/ppermute | solution.py:1007
  55.6 23.0 %collective-permute-start.13 = (bf16[384,768]{1,0:T(8,128)(2,1)}, bf16[384,768]{1,0:T(8,128)(2,1)S(1)}, u32[]{:S(2)}, u32[]{:S(2)}) collective-permute-start(bf16[384,768]{1,0:T(8,128)(2,1)} %fence.24), channel_id=1, source_target_pairs={{0,16},{16,0},{1,17},{17,1},{2,18},{18,2},{3,19},{19,3},{4,20},{20... | collective-permute-start | bytes 1769480 | tf_op jit(solution)/shard_map/ppermute | solution.py:1011
  66.2 137.9 %all-gather.6.cloned.1.call-start = ((), (), s32[]{:S(2)}) async-start(), calls=%async_computation.5 | async-start | bytes 3440640 | tf_op jit(solution)/shard_map/all_gather | solution.py:1346
  69.4 17.0 %collective-permute-start.11 = (bf16[1536,512]{1,0:T(8,128)(2,1)S(1)}, bf16[1536,512]{1,0:T(8,128)(2,1)}, u32[]{:S(2)}, u32[]{:S(2)}) collective-permute-start(bf16[1536,512]{1,0:T(8,128)(2,1)S(1)} %slice_dynamic-update-slice_fusion.1.refs_5_.refs_3_), channel_id=1, source_target_pairs={{0,16},{16,0},{1,17},{17,1},{2,18},{18,2},{3,19},{19,3},{4,20},{20... | collective-permute-start | bytes 4718600 | tf_op jit(solution)/shard_map/ppermute | solution.py:1011
  81.6 25.1 %collective-permute-start.14 = (bf16[384,384]{1,0:T(8,128)(2,1)}, bf16[384,384]{1,0:T(8,128)(2,1)S(1)}, u32[]{:S(2)}, u32[]{:S(2)}) collective-permute-start(bf16[384,384]{1,0:T(8,128)(2,1)} %fence.25.refs_0_), channel_id=1, source_target_pairs={{0,4},{4,8},{8,12},{12,0},{1,5},{5,9},{9,13},{13,1},{2,6},{6,10},{... | collective-permute-start | bytes 884744 | tf_op jit(solution)/shard_map/ppermute | solution.py:1016
  82.0 24.8 %collective-permute-start.15 = (bf16[384,384]{1,0:T(8,128)(2,1)}, bf16[384,384]{1,0:T(8,128)(2,1)S(1)}, u32[]{:S(2)}, u32[]{:S(2)}) collective-permute-start(bf16[384,384]{1,0:T(8,128)(2,1)} %fence.25.refs_0_), channel_id=1, source_target_pairs={{0,8},{4,12},{8,0},{12,4},{1,9},{5,13},{9,1},{13,5},{2,10},{6,14},... | collective-permute-start | bytes 884744 | tf_op jit(solution)/shard_map/ppermute | solution.py:1016
  85.9 20.8 %collective-permute-start.16 = (bf16[384,384]{1,0:T(8,128)(2,1)}, bf16[384,384]{1,0:T(8,128)(2,1)S(1)}, u32[]{:S(2)}, u32[]{:S(2)}) collective-permute-start(bf16[384,384]{1,0:T(8,128)(2,1)} %fence.25.refs_0_), channel_id=1, source_target_pairs={{0,12},{4,0},{8,4},{12,8},{1,13},{5,1},{9,5},{13,9},{2,14},{6,2},{... | collective-permute-start | bytes 884744 | tf_op jit(solution)/shard_map/ppermute | solution.py:1016
  110.2 17.8 %collective-permute-start.18 = (bf16[384,384]{1,0:T(8,128)(2,1)S(1)}, bf16[384,384]{1,0:T(8,128)(2,1)S(1)}, u32[]{:S(2)}, u32[]{:S(2)}) collective-permute-start(bf16[384,384]{1,0:T(8,128)(2,1)S(1)} %copy-done.16), channel_id=1, source_target_pairs={{0,4},{4,8},{8,12},{12,0},{1,5},{5,9},{9,13},{13,1},{2,6},{6,10},{... | collective-permute-start | bytes 884744 | tf_op jit(solution)/shard_map/ppermute | solution.py:1016
  116.1 19.9 %collective-permute-start.19 = (bf16[384,384]{1,0:T(8,128)(2,1)S(1)}, bf16[384,384]{1,0:T(8,128)(2,1)S(1)}, u32[]{:S(2)}, u32[]{:S(2)}) collective-permute-start(bf16[384,384]{1,0:T(8,128)(2,1)S(1)} %copy-done.16), channel_id=1, source_target_pairs={{0,8},{4,12},{8,0},{12,4},{1,9},{5,13},{9,1},{13,5},{2,10},{6,14},... | collective-permute-start | bytes 884744 | tf_op jit(solution)/shard_map/ppermute | solution.py:1016
  116.3 19.7 %collective-permute-start.20 = (bf16[384,384]{1,0:T(8,128)(2,1)S(1)}, bf16[384,384]{1,0:T(8,128)(2,1)S(1)}, u32[]{:S(2)}, u32[]{:S(2)}) collective-permute-start(bf16[384,384]{1,0:T(8,128)(2,1)S(1)} %copy-done.16), channel_id=1, source_target_pairs={{0,12},{4,0},{8,4},{12,8},{1,13},{5,1},{9,5},{13,9},{2,14},{6,2},{... | collective-permute-start | bytes 884744 | tf_op jit(solution)/shard_map/ppermute | solution.py:1016
  138.4 110.3 %all-gather.8.cloned.1.call-start = ((), (), s32[]{:S(2)}) async-start(), calls=%async_computation.6 | async-start | bytes 1474560 | tf_op jit(solution)/shard_map/all_gather | solution.py:1347
  156.6 12.3 %collective-permute-start.29 = (bf16[256,768]{1,0:T(8,128)(2,1)}, bf16[256,768]{1,0:T(8,128)(2,1)S(1)}, u32[]{:S(2)}, u32[]{:S(2)}) collective-permute-start(bf16[256,768]{1,0:T(8,128)(2,1)} %get-tuple-element.133), channel_id=1, source_target_pairs={{0,1},{1,0},{2,3},{3,2},{4,5},{5,4},{6,7},{7,6},{8,9},{9,8},{10,11... | collective-permute-start | bytes 1179656 | tf_op jit(solution)/shard_map/ppermute | solution.py:1007
  157.1 14.9 %collective-permute-start.25 = (bf16[256,768]{1,0:T(8,128)(2,1)}, bf16[256,768]{1,0:T(8,128)(2,1)S(1)}, u32[]{:S(2)}, u32[]{:S(2)}) collective-permute-start(bf16[256,768]{1,0:T(8,128)(2,1)} %get-tuple-element.128), channel_id=1, source_target_pairs={{0,2},{1,3},{2,0},{3,1},{4,6},{5,7},{6,4},{7,5},{8,10},{9,11},{10,... | collective-permute-start | bytes 1179656 | tf_op jit(solution)/shard_map/ppermute | solution.py:1007
  158.7 18.6 %collective-permute-start.28 = (bf16[256,768]{1,0:T(8,128)(2,1)}, bf16[256,768]{1,0:T(8,128)(2,1)S(1)}, u32[]{:S(2)}, u32[]{:S(2)}) collective-permute-start(bf16[256,768]{1,0:T(8,128)(2,1)} %get-tuple-element.131), channel_id=1, source_target_pairs={{0,1},{1,0},{2,3},{3,2},{4,5},{5,4},{6,7},{7,6},{8,9},{9,8},{10,11... | collective-permute-start | bytes 1179656 | tf_op jit(solution)/shard_map/ppermute | solution.py:1007
  171.6 13.6 %collective-permute-start.27 = (bf16[256,768]{1,0:T(8,128)(2,1)}, bf16[256,768]{1,0:T(8,128)(2,1)S(1)}, u32[]{:S(2)}, u32[]{:S(2)}) collective-permute-start(bf16[256,768]{1,0:T(8,128)(2,1)} %get-tuple-element.129), channel_id=1, source_target_pairs={{0,2},{1,3},{2,0},{3,1},{4,6},{5,7},{6,4},{7,5},{8,10},{9,11},{10,... | collective-permute-start | bytes 1179656 | tf_op jit(solution)/shard_map/ppermute | solution.py:1007
  187.7 15.7 %collective-permute-start.31 = (bf16[256,1536]{1,0:T(8,128)(2,1)S(1)}, bf16[256,1536]{1,0:T(8,128)(2,1)S(1)}, u32[]{:S(2)}, u32[]{:S(2)}) collective-permute-start(bf16[256,1536]{1,0:T(8,128)(2,1)S(1)} %get-tuple-element.246.refs_0_), channel_id=1, source_target_pairs={{0,1},{1,0},{2,3},{3,2},{4,5},{5,4},{6,7},{7,6},{8,9},{9,8},{10,11... | collective-permute-start | bytes 2359304 | tf_op jit(solution)/shard_map/ppermute | solution.py:1007
  188.7 15.4 %collective-permute-start.32 = (bf16[256,1536]{1,0:T(8,128)(2,1)S(1)}, bf16[256,1536]{1,0:T(8,128)(2,1)S(1)}, u32[]{:S(2)}, u32[]{:S(2)}) collective-permute-start(bf16[256,1536]{1,0:T(8,128)(2,1)S(1)} %get-tuple-element.246.refs_0_), channel_id=1, source_target_pairs={{0,2},{1,3},{2,0},{3,1},{4,6},{5,7},{6,4},{7,5},{8,10},{9,11},{10,... | collective-permute-start | bytes 2359304 | tf_op jit(solution)/shard_map/ppermute | solution.py:1007
  205.0 17.7 %collective-permute-start.35 = (bf16[1536,896]{1,0:T(8,128)(2,1)}, bf16[1536,896]{1,0:T(8,128)(2,1)}, u32[]{:S(2)}, u32[]{:S(2)}) collective-permute-start(bf16[1536,896]{1,0:T(8,128)(2,1)} %fence.31.refs_5_.refs_1_.refs_3_), channel_id=1, source_target_pairs={{0,16},{16,0},{1,17},{17,1},{2,18},{18,2},{3,19},{19,3},{4,20},{20... | collective-permute-start | bytes 8257544 | tf_op jit(solution)/shard_map/ppermute | solution.py:1011
  213.1 219.2 %reduce-scatter.5.cloned.1.call-start = ((), (), s32[]{:S(2)}) async-start(), calls=%async_computation.7 | async-start | bytes 2949120 | tf_op jit(solution)/shard_map/reduce_scatter | solution.py:1423
  281.9 54.3 %collective-permute-start.42 = (bf16[256,1536]{1,0:T(8,128)(2,1)}, bf16[256,1536]{1,0:T(8,128)(2,1)S(1)}, u32[]{:S(2)}, u32[]{:S(2)}) collective-permute-start(bf16[256,1536]{1,0:T(8,128)(2,1)} %get-tuple-element.159), channel_id=1, source_target_pairs={{0,3},{1,2},{2,1},{3,0},{4,7},{5,6},{6,5},{7,4},{8,11},{9,10},{10,... | collective-permute-start | bytes 2359304 | tf_op jit(solution)/shard_map/ppermute | solution.py:1007
  284.3 52.0 %collective-permute-start.41 = (bf16[256,1536]{1,0:T(8,128)(2,1)}, bf16[256,1536]{1,0:T(8,128)(2,1)S(1)}, u32[]{:S(2)}, u32[]{:S(2)}) collective-permute-start(bf16[256,1536]{1,0:T(8,128)(2,1)} %get-tuple-element.158), channel_id=1, source_target_pairs={{0,2},{1,3},{2,0},{3,1},{4,6},{5,7},{6,4},{7,5},{8,10},{9,11},{10,... | collective-permute-start | bytes 2359304 | tf_op jit(solution)/shard_map/ppermute | solution.py:1007
  284.9 51.4 %collective-permute-start.40 = (bf16[256,1536]{1,0:T(8,128)(2,1)}, bf16[256,1536]{1,0:T(8,128)(2,1)S(1)}, u32[]{:S(2)}, u32[]{:S(2)}) collective-permute-start(bf16[256,1536]{1,0:T(8,128)(2,1)} %get-tuple-element.157), channel_id=1, source_target_pairs={{0,1},{1,0},{2,3},{3,2},{4,5},{5,4},{6,7},{7,6},{8,9},{9,8},{10,11... | collective-permute-start | bytes 2359304 | tf_op jit(solution)/shard_map/ppermute | solution.py:1007
  333.3 15.6 %collective-permute-start.43 = (bf16[256,768]{1,0:T(8,128)(2,1)}, bf16[256,768]{1,0:T(8,128)(2,1)S(1)}, u32[]{:S(2)}, u32[]{:S(2)}) collective-permute-start(bf16[256,768]{1,0:T(8,128)(2,1)} %get-tuple-element.163), channel_id=1, source_target_pairs={{0,2},{1,3},{2,0},{3,1},{4,6},{5,7},{6,4},{7,5},{8,10},{9,11},{10,... | collective-permute-start | bytes 1179656 | tf_op jit(solution)/shard_map/ppermute | solution.py:1007
  334.9 14.0 %collective-permute-start.44 = (bf16[256,768]{1,0:T(8,128)(2,1)}, bf16[256,768]{1,0:T(8,128)(2,1)S(1)}, u32[]{:S(2)}, u32[]{:S(2)}) collective-permute-start(bf16[256,768]{1,0:T(8,128)(2,1)} %get-tuple-element.164), channel_id=1, source_target_pairs={{0,1},{1,0},{2,3},{3,2},{4,5},{5,4},{6,7},{7,6},{8,9},{9,8},{10,11... | collective-permute-start | bytes 1179656 | tf_op jit(solution)/shard_map/ppermute | solution.py:1007
  354.5 14.7 %collective-permute-start.45 = (bf16[1536,896]{1,0:T(8,128)(2,1)}, bf16[1536,896]{1,0:T(8,128)(2,1)S(1)}, u32[]{:S(2)}, u32[]{:S(2)}) collective-permute-start(bf16[1536,896]{1,0:T(8,128)(2,1)} %fence.36), channel_id=1, source_target_pairs={{0,16},{16,0},{1,17},{17,1},{2,18},{18,2},{3,19},{19,3},{4,20},{20... | collective-permute-start | bytes 8257544 | tf_op jit(solution)/shard_map/ppermute | solution.py:1011
  356.6 18.3 %collective-permute-start.47 = (bf16[256,768]{1,0:T(8,128)(2,1)S(1)}, bf16[256,768]{1,0:T(8,128)(2,1)S(1)}, u32[]{:S(2)}, u32[]{:S(2)}) collective-permute-start(bf16[256,768]{1,0:T(8,128)(2,1)S(1)} %copy-done.95), channel_id=1, source_target_pairs={{0,2},{1,3},{2,0},{3,1},{4,6},{5,7},{6,4},{7,5},{8,10},{9,11},{10,... | collective-permute-start | bytes 1179656 | tf_op jit(solution)/shard_map/ppermute | solution.py:1007
  358.1 16.8 %collective-permute-start.46 = (bf16[256,768]{1,0:T(8,128)(2,1)S(1)}, bf16[256,768]{1,0:T(8,128)(2,1)S(1)}, u32[]{:S(2)}, u32[]{:S(2)}) collective-permute-start(bf16[256,768]{1,0:T(8,128)(2,1)S(1)} %copy-done.44), channel_id=1, source_target_pairs={{0,1},{1,0},{2,3},{3,2},{4,5},{5,4},{6,7},{7,6},{8,9},{9,8},{10,11... | collective-permute-start | bytes 1179656 | tf_op jit(solution)/shard_map/ppermute | solution.py:1007
  382.0 19.1 %collective-permute-start.50 = (bf16[272,1536]{1,0:T(8,128)(2,1)}, bf16[272,1536]{1,0:T(8,128)(2,1)S(1)}, u32[]{:S(2)}, u32[]{:S(2)}) collective-permute-start(bf16[272,1536]{1,0:T(8,128)(2,1)} %norm_backward.2.refs_2_.refs_0_), channel_id=1, source_target_pairs={{0,1},{1,0},{2,3},{3,2},{4,5},{5,4},{6,7},{7,6},{8,9},{9,8},{10,11... | collective-permute-start | bytes 2506760 | tf_op jit(solution)/shard_map/ppermute | solution.py:1007
  383.4 18.8 %collective-permute-start.51 = (bf16[272,1536]{1,0:T(8,128)(2,1)}, bf16[272,1536]{1,0:T(8,128)(2,1)S(1)}, u32[]{:S(2)}, u32[]{:S(2)}) collective-permute-start(bf16[272,1536]{1,0:T(8,128)(2,1)} %norm_backward.2.refs_2_.refs_0_), channel_id=1, source_target_pairs={{0,2},{1,3},{2,0},{3,1},{4,6},{5,7},{6,4},{7,5},{8,10},{9,11},{10,... | collective-permute-start | bytes 2506760 | tf_op jit(solution)/shard_map/ppermute | solution.py:1007
  383.8 146.2 %reduce-scatter.9.cloned.1.call-start = ((), (), s32[]{:S(2)}) async-start(), calls=%async_computation.9 | async-start | bytes 1474560 | tf_op jit(solution)/shard_map/reduce_scatter | solution.py:1446
  427.9 15.9 %collective-permute-start.60 = (bf16[1536,384]{1,0:T(8,128)(2,1)}, bf16[1536,384]{1,0:T(8,128)(2,1)S(1)}, u32[]{:S(2)}, u32[]{:S(2)}) collective-permute-start(bf16[1536,384]{1,0:T(8,128)(2,1)} %fence.40), channel_id=1, source_target_pairs={{0,16},{16,0},{1,17},{17,1},{2,18},{18,2},{3,19},{19,3},{4,20},{20... | collective-permute-start | bytes 3538952 | tf_op jit(solution)/shard_map/ppermute | solution.py:1011
  445.1 84.9 %reduce-scatter.7.cloned.1.call-start = ((), (), s32[]{:S(2)}) async-start(), calls=%async_computation.8 | async-start | bytes 2949120 | tf_op jit(solution)/shard_map/reduce_scatter | solution.py:1451
  453.1 140.4 %reduce-scatter.11.cloned.1.call-start = ((), (), s32[]{:S(2)}) async-start(), calls=%async_computation.10 | async-start | bytes 1474560 | tf_op jit(solution)/shard_map/reduce_scatter | solution.py:1474
  505.2 21.0 %collective-permute-start.59 = (bf16[1536,512]{1,0:T(8,128)(2,1)}, bf16[1536,512]{1,0:T(8,128)(2,1)}, u32[]{:S(2)}, u32[]{:S(2)}) collective-permute-start(bf16[1536,512]{1,0:T(8,128)(2,1)} %get-tuple-element.197), channel_id=1, source_target_pairs={{0,16},{16,0},{1,17},{17,1},{2,18},{18,2},{3,19},{19,3},{4,20},{20... | collective-permute-start | bytes 4718600 | tf_op jit(solution)/shard_map/ppermute | solution.py:1011
  506.2 25.1 %collective-permute-start.64 = (bf16[256,768]{1,0:T(8,128)(2,1)}, bf16[256,768]{1,0:T(8,128)(2,1)}, u32[]{:S(2)}, u32[]{:S(2)}) collective-permute-start(bf16[256,768]{1,0:T(8,128)(2,1)} %get-tuple-element.205), channel_id=1, source_target_pairs={{0,2},{1,3},{2,0},{3,1},{4,6},{5,7},{6,4},{7,5},{8,10},{9,11},{10,... | collective-permute-start | bytes 1179656 | tf_op jit(solution)/shard_map/ppermute | solution.py:1007
  506.7 26.8 %collective-permute-start.65 = (bf16[256,768]{1,0:T(8,128)(2,1)}, bf16[256,768]{1,0:T(8,128)(2,1)}, u32[]{:S(2)}, u32[]{:S(2)}) collective-permute-start(bf16[256,768]{1,0:T(8,128)(2,1)} %get-tuple-element.207), channel_id=1, source_target_pairs={{0,1},{1,0},{2,3},{3,2},{4,5},{5,4},{6,7},{7,6},{8,9},{9,8},{10,11... | collective-permute-start | bytes 1179656 | tf_op jit(solution)/shard_map/ppermute | solution.py:1007
  508.2 15.8 %collective-permute-start.58 = (f32[32,1536]{1,0:T(8,128)}, f32[32,1536]{1,0:T(8,128)S(1)}, u32[]{:S(2)}, u32[]{:S(2)}) collective-permute-start(f32[32,1536]{1,0:T(8,128)} %get-tuple-element.195), channel_id=1, source_target_pairs={{0,4},{4,0},{8,12},{12,8},{1,5},{5,1},{9,13},{13,9},{2,6},{6,2},{1... | collective-permute-start | bytes 589832 | tf_op jit(solution)/shard_map/ppermute | solution.py:1087
  510.4 20.8 %collective-permute-start.63 = (bf16[256,768]{1,0:T(8,128)(2,1)}, bf16[256,768]{1,0:T(8,128)(2,1)}, u32[]{:S(2)}, u32[]{:S(2)}) collective-permute-start(bf16[256,768]{1,0:T(8,128)(2,1)} %add_convert_fusion.7), channel_id=1, source_target_pairs={{0,1},{1,0},{2,3},{3,2},{4,5},{5,4},{6,7},{7,6},{8,9},{9,8},{10,11... | collective-permute-start | bytes 1179656 | tf_op jit(solution)/shard_map/ppermute | solution.py:1007
  531.2 15.0 %collective-permute-start.61 = (bf16[1536,128]{1,0:T(8,128)(2,1)S(1)}, bf16[1536,128]{1,0:T(8,128)(2,1)S(1)}, u32[]{:S(2)}, u32[]{:S(2)}) collective-permute-start(bf16[1536,128]{1,0:T(8,128)(2,1)S(1)} %broadcast_select_fusion.12), channel_id=1, source_target_pairs={{0,16},{16,0},{1,17},{17,1},{2,18},{18,2},{3,19},{19,3},{4,20},{20... | collective-permute-start | bytes 1179656 | tf_op jit(solution)/shard_map/ppermute | solution.py:1011
  550.7 15.6 %collective-permute-start.71 = (f32[1,1664]{1,0:T(1,128)}, f32[1,1664]{1,0:T(1,128)S(1)}, u32[]{:S(2)}, u32[]{:S(2)}) collective-permute-start(f32[1,1664]{1,0:T(1,128)} %pad_maximum_fusion.9), channel_id=1, source_target_pairs={{0,3},{1,2},{2,1},{3,0},{4,7},{5,6},{6,5},{7,4},{8,11},{9,10},{10,... | collective-permute-start | bytes 19976 | tf_op jit(solution)/shard_map/ppermute | solution.py:1007
  551.4 15.6 %collective-permute-start.70 = (f32[1,1664]{1,0:T(1,128)}, f32[1,1664]{1,0:T(1,128)S(1)}, u32[]{:S(2)}, u32[]{:S(2)}) collective-permute-start(f32[1,1664]{1,0:T(1,128)} %pad_maximum_fusion.9), channel_id=1, source_target_pairs={{0,2},{1,3},{2,0},{3,1},{4,6},{5,7},{6,4},{7,5},{8,10},{9,11},{10,... | collective-permute-start | bytes 19976 | tf_op jit(solution)/shard_map/ppermute | solution.py:1007
  553.0 15.6 %collective-permute-start.69 = (f32[1,1664]{1,0:T(1,128)}, f32[1,1664]{1,0:T(1,128)S(1)}, u32[]{:S(2)}, u32[]{:S(2)}) collective-permute-start(f32[1,1664]{1,0:T(1,128)} %pad_maximum_fusion.9), channel_id=1, source_target_pairs={{0,1},{1,0},{2,3},{3,2},{4,5},{5,4},{6,7},{7,6},{8,9},{9,8},{10,11... | collective-permute-start | bytes 19976 | tf_op jit(solution)/shard_map/ppermute | solution.py:1007
  560.5 27.9 %collective-permute-start.67 = (bf16[256,1536]{1,0:T(8,128)(2,1)}, bf16[256,1536]{1,0:T(8,128)(2,1)}, u32[]{:S(2)}, u32[]{:S(2)}) collective-permute-start(bf16[256,1536]{1,0:T(8,128)(2,1)} %get-tuple-element.235), channel_id=1, source_target_pairs={{0,16},{16,0},{1,17},{17,1},{2,18},{18,2},{3,19},{19,3},{4,20},{20... | collective-permute-start | bytes 2359304 | tf_op jit(solution)/shard_map/ppermute | solution.py:1011
  561.5 29.5 %collective-permute-start.68 = (bf16[272,1536]{1,0:T(8,128)(2,1)}, bf16[272,1536]{1,0:T(8,128)(2,1)}, u32[]{:S(2)}, u32[]{:S(2)}) collective-permute-start(bf16[272,1536]{1,0:T(8,128)(2,1)} %broadcast_select_fusion), channel_id=1, source_target_pairs={{0,16},{16,0},{1,17},{17,1},{2,18},{18,2},{3,19},{19,3},{4,20},{20... | collective-permute-start | bytes 2506760 | tf_op jit(solution)/shard_map/ppermute | solution.py:1011
  (139 other events, 866.2 us)
Sparse Core Ops, SparseCore 0:
  66.3 42.1 all-gather.3
  138.5 63.5 all-gather.5
  213.2 35.4 all-gather.7
  384.0 48.3 reduce-scatter.4
  445.2 28.8 reduce-scatter.8
  476.8 50.8 reduce-scatter.6
  542.5 27.6 reduce-scatter.10
